TPU v7x, 512 devices: a whole 4x8x8 slice. The times are simulated.
512 devices in a mesh: gx: 16 (over x, z_lo, core), gy: 32 (over z_hi, y).
Axes of the slice: x: 4, y: 8, z: 8 (z_hi: 4, z_lo: 2; z = z_hi * 2 + z_lo), core: 2. Of those that a mesh axis runs over, the one named last changes fastest.
Arguments:
- activator: float32 [56, 1024, 2048], P(None, 'gy', 'gx'), may hold values from 0 to 1
- inhibitor: float32 [56, 1024, 2048], P(None, 'gy', 'gx'), may hold values from 0 to 0.5
- feed_rate: bfloat16 [56, 1024, 2048], P(None, 'gy', 'gx'), may hold values from 0.0019989014 to 0.029907227
- kill_rate: bfloat16 [56, 1024, 2048], P(None, 'gy', 'gx'), may hold values from 0.019897461 to 0.19921875
Outputs:
- activator_out: float32 [56, 1024, 2048], P(None, 'gy', 'gx')
- inhibitor_out: float32 [56, 1024, 2048], P(None, 'gy', 'gx')
All inputs are finite; a program needn't handle non-finite values.
Results may differ from a plain program's by a relative error of at most 0.0003.
Values sent between devices are 32-bit elements; how exact they have to be, the bound alone decides.
No kernel may reach another device: no remote copies, remote signals or barrier semaphores. Data moves between devices by JAX's collectives and lax.ppermute only.
A program may use at most 64 MiB of HBM per device.

v0:
```python
import jax
import jax.numpy as jnp
from jax import lax
from jax.sharding import PartitionSpec as P

STEPS = 4


def padded_2(block, sides, width):
    for axis, dim in sides:
        count = lax.axis_size(axis)
        forward = [(i, i + 1) for i in range(count - 1)]
        forward.append((count - 1, 0))
        backward = [(target, source) for source, target in forward]
        low = lax.ppermute(
            lax.slice_in_dim(block, block.shape[dim] - width, None, axis=dim), axis, forward
        )
        high = lax.ppermute(lax.slice_in_dim(block, 0, width, axis=dim), axis, backward)
        block = jnp.concatenate([low, block, high], axis=dim)
    return block


def z_laplace(field):
    padded = jnp.pad(field, ((1, 1), (0, 0), (0, 0)), mode="edge")
    return padded[2:] + padded[:-2] - 2.0 * field


def advance(conc_u, conc_v, near_u, near_v, feed, kill):
    react = conc_u * conc_v * conc_v
    new_u = (
        conc_u
        + 0.24 * (near_u - 4.0 * conc_u)
        + 0.01 * z_laplace(conc_u)
        - react
        + feed * (1.0 - conc_u)
    )
    new_v = (
        conc_v
        + 0.12 * (near_v - 4.0 * conc_v)
        + 0.005 * z_laplace(conc_v)
        + react
        - (feed + kill) * conc_v
    )
    return (new_u, new_v)


def shards(activator, inhibitor, feed_rate, kill_rate):
    feed = feed_rate.astype(jnp.float32)
    kill = kill_rate.astype(jnp.float32)
    conc_u = activator
    conc_v = inhibitor
    for step in range(STEPS):
        both = jnp.stack([conc_u, conc_v])
        along_x = padded_2(both, (("gx", 3),), 1)
        along_y = padded_2(both, (("gy", 2),), 1)
        near = along_x[..., 2:] + along_x[..., :-2] + along_y[:, :, 2:, :] + along_y[:, :, :-2, :]
        conc_u, conc_v = advance(conc_u, conc_v, near[0], near[1], feed, kill)
    return (conc_u, conc_v)


def solution(mesh):
    return jax.shard_map(
        shards,
        mesh=mesh,
        in_specs=(
            P(None, "gy", "gx"),
            P(None, "gy", "gx"),
            P(None, "gy", "gx"),
            P(None, "gy", "gx"),
        ),
        out_specs=(P(None, "gy", "gx"), P(None, "gy", "gx")),
        check_vma=False,
    )
```

profile of v0, /device:TPU:71, one launch (start us, length us, event | category | flops | bytes accessed | tf_op | source)
XLA Modules:
  0.0 150.5 jit_solution(3940877725326460772)
XLA Ops:
  0.6 4.5 %fusion.6 = (f32[2,56,32,1]{3,2,1,0:T(8,128)}, f32[2,56,32,1]{3,2,1,0:T(8,128)}) fusion(f32[1,56,32,128]{3,2,1,0:T(8,128)} %bitcast.109, f32[1,56,32,128]{3,2,1,0:T(8,128)} %bitcast.106), kind=kLoop, calls=%fused_computation.30 | loop fusion | flops 7168 | bytes 1863680 | tf_op jit(solution)/shard_map/stack | solution.py:53
  5.1 2.5 %copy.87 = f32[2,56,32,1]{1,2,3,0:T(8,128)S(1)} copy(f32[2,56,32,1]{3,2,1,0:T(8,128)} %get-tuple-element.24) | data formatting | bytes 28672
  7.7 2.6 %collective-permute-start = (f32[2,56,32,1]{1,2,3,0:T(8,128)S(1)}, f32[2,56,32,1]{1,2,3,0:T(8,128)S(1)}, u32[]{:S(2)}, u32[]{:S(2)}) collective-permute-start(f32[2,56,32,1]{1,2,3,0:T(8,128)S(1)} %copy.87), channel_id=1, source_target_pairs={{32,0},{64,32},{96,64},{128,96},{160,128},{192,160},{224,192},{256... | collective-permute-start | bytes 43016 | tf_op jit(solution)/shard_map/ppermute | solution.py:18
  10.3 2.4 %copy.88 = f32[2,56,32,1]{1,2,3,0:T(8,128)S(1)} copy(f32[2,56,32,1]{3,2,1,0:T(8,128)} %get-tuple-element.25) | data formatting | bytes 28672
  12.7 6.5 %collective-permute-start.1 = (f32[2,56,32,1]{1,2,3,0:T(8,128)S(1)}, f32[2,56,32,1]{1,2,3,0:T(8,128)S(1)}, u32[]{:S(2)}, u32[]{:S(2)}) collective-permute-start(f32[2,56,32,1]{1,2,3,0:T(8,128)S(1)} %copy.88), channel_id=1, source_target_pairs={{0,32},{32,64},{64,96},{96,128},{128,160},{160,192},{192,224},{224... | collective-permute-start | bytes 43016 | tf_op jit(solution)/shard_map/ppermute | solution.py:15
  19.2 11.3 %collective-permute-start.2 = (f32[2,56,1,128]{3,2,1,0:T(1,128)S(1)}, f32[2,56,1,128]{3,2,1,0:T(1,128)S(1)}, u32[]{:S(2)}, u32[]{:S(2)}) collective-permute-start(f32[2,56,1,128]{3,2,1,0:T(1,128)S(1)} %get-tuple-element.26), channel_id=1, source_target_pairs={{1,0},{2,1},{3,2},{4,3},{5,4},{6,5},{7,6},{8,7},{9,8},{10,9},{11,1... | collective-permute-start | bytes 172040 | tf_op jit(solution)/shard_map/ppermute | solution.py:18
  30.5 1.9 %collective-permute-start.3 = (f32[2,56,1,128]{3,2,1,0:T(1,128)S(1)}, f32[2,56,1,128]{3,2,1,0:T(1,128)S(1)}, u32[]{:S(2)}, u32[]{:S(2)}) collective-permute-start(f32[2,56,1,128]{3,2,1,0:T(1,128)S(1)} %get-tuple-element.27), channel_id=1, source_target_pairs={{0,1},{1,2},{2,3},{3,4},{4,5},{5,6},{6,7},{7,8},{8,9},{9,10},{10,1... | collective-permute-start | bytes 172040 | tf_op jit(solution)/shard_map/ppermute | solution.py:15
  32.5 2.6 %copy.72 = f32[2,56,32,1]{3,2,1,0:T(8,128)} copy(f32[2,56,32,1]{1,2,3,0:T(8,128)S(1)} %collective-permute-done) | data formatting | bytes 28672 | tf_op jit(solution)/shard_map/ppermute | solution.py:18
  35.1 2.6 %copy.74 = f32[2,56,32,1]{3,2,1,0:T(8,128)} copy(f32[2,56,32,1]{1,2,3,0:T(8,128)S(1)} %collective-permute-done.1) | data formatting | bytes 28672 | tf_op jit(solution)/shard_map/ppermute | solution.py:15
  37.7 1.9 %collective-permute-done.3 = f32[2,56,1,128]{3,2,1,0:T(1,128)S(1)} collective-permute-done((f32[2,56,1,128]{3,2,1,0:T(1,128)S(1)}, f32[2,56,1,128]{3,2,1,0:T(1,128)S(1)}, u32[]{:S(2)}, u32[]{:S(2)}) %collective-permute-start.3) | collective-permute-done | bytes 57376 | tf_op jit(solution)/shard_map/ppermute | solution.py:15
  39.7 3.4 %fusion.17 = f32[2,56,32,128]{3,2,1,0:T(8,128)S(1)} fusion(f32[2,56,1,128]{3,2,1,0:T(1,128)S(1)} %collective-permute-done.3, f32[1,56,32,128]{3,2,1,0:T(8,128)S(1)} %bitcast.108, f32[1,56,32,128]{3,2,1,0:T(8,128)S(1)} %bitcast.111, f32[2,56,1,128]{3,2,1,0:T(1,128)S(1)} %collective-permute-done.2, f32[2,56,32,1]{3,2,1,0:T(8,128)} %copy.74, ...), kind=kLoop, calls=%fused_computation.66 | loop fusion | flops 5046272 | bytes 3813376 | tf_op jit(solution)/shard_map/add | solution.py:56
  43.1 0.9 fusion.80
  44.0 2.5 %fusion.4 = (f32[2,56,32,1]{3,2,1,0:T(8,128)}, f32[2,56,32,1]{3,2,1,0:T(8,128)}) fusion(f32[1,56,32,128]{3,2,1,0:T(8,128)S(1)} %bitcast.103, f32[1,56,32,128]{3,2,1,0:T(8,128)S(1)} %bitcast.100), kind=kLoop, calls=%fused_computation.28 | loop fusion | flops 7168 | bytes 1863680 | tf_op jit(solution)/shard_map/stack | solution.py:53
  46.6 2.4 %copy.89 = f32[2,56,32,1]{1,2,3,0:T(8,128)S(1)} copy(f32[2,56,32,1]{3,2,1,0:T(8,128)} %get-tuple-element.20) | data formatting | bytes 28672
  49.0 1.9 %collective-permute-start.4 = (f32[2,56,32,1]{1,2,3,0:T(8,128)S(1)}, f32[2,56,32,1]{1,2,3,0:T(8,128)S(1)}, u32[]{:S(2)}, u32[]{:S(2)}) collective-permute-start(f32[2,56,32,1]{1,2,3,0:T(8,128)S(1)} %copy.89), channel_id=1, source_target_pairs={{32,0},{64,32},{96,64},{128,96},{160,128},{192,160},{224,192},{256... | collective-permute-start | bytes 43016 | tf_op jit(solution)/shard_map/ppermute | solution.py:18
  51.0 2.4 %copy.90 = f32[2,56,32,1]{1,2,3,0:T(8,128)S(1)} copy(f32[2,56,32,1]{3,2,1,0:T(8,128)} %get-tuple-element.21) | data formatting | bytes 28672
  53.4 5.7 %collective-permute-start.5 = (f32[2,56,32,1]{1,2,3,0:T(8,128)S(1)}, f32[2,56,32,1]{1,2,3,0:T(8,128)S(1)}, u32[]{:S(2)}, u32[]{:S(2)}) collective-permute-start(f32[2,56,32,1]{1,2,3,0:T(8,128)S(1)} %copy.90), channel_id=1, source_target_pairs={{0,32},{32,64},{64,96},{96,128},{128,160},{160,192},{192,224},{224... | collective-permute-start | bytes 43016 | tf_op jit(solution)/shard_map/ppermute | solution.py:15
  59.1 5.8 %collective-permute-start.6 = (f32[2,56,1,128]{3,2,1,0:T(1,128)S(1)}, f32[2,56,1,128]{3,2,1,0:T(1,128)S(1)}, u32[]{:S(2)}, u32[]{:S(2)}) collective-permute-start(f32[2,56,1,128]{3,2,1,0:T(1,128)S(1)} %get-tuple-element.22), channel_id=1, source_target_pairs={{1,0},{2,1},{3,2},{4,3},{5,4},{6,5},{7,6},{8,7},{9,8},{10,9},{11,1... | collective-permute-start | bytes 172040 | tf_op jit(solution)/shard_map/ppermute | solution.py:18
  64.9 2.1 %collective-permute-start.7 = (f32[2,56,1,128]{3,2,1,0:T(1,128)S(1)}, f32[2,56,1,128]{3,2,1,0:T(1,128)S(1)}, u32[]{:S(2)}, u32[]{:S(2)}) collective-permute-start(f32[2,56,1,128]{3,2,1,0:T(1,128)S(1)} %get-tuple-element.23), channel_id=1, source_target_pairs={{0,1},{1,2},{2,3},{3,4},{4,5},{5,6},{6,7},{7,8},{8,9},{9,10},{10,1... | collective-permute-start | bytes 172040 | tf_op jit(solution)/shard_map/ppermute | solution.py:15
  67.1 2.6 %copy.76 = f32[2,56,32,1]{3,2,1,0:T(8,128)} copy(f32[2,56,32,1]{1,2,3,0:T(8,128)S(1)} %collective-permute-done.4) | data formatting | bytes 28672 | tf_op jit(solution)/shard_map/ppermute | solution.py:18
  69.7 2.6 %copy.78 = f32[2,56,32,1]{3,2,1,0:T(8,128)} copy(f32[2,56,32,1]{1,2,3,0:T(8,128)S(1)} %collective-permute-done.5) | data formatting | bytes 28672 | tf_op jit(solution)/shard_map/ppermute | solution.py:15
  72.3 1.8 %collective-permute-done.7 = f32[2,56,1,128]{3,2,1,0:T(1,128)S(1)} collective-permute-done((f32[2,56,1,128]{3,2,1,0:T(1,128)S(1)}, f32[2,56,1,128]{3,2,1,0:T(1,128)S(1)}, u32[]{:S(2)}, u32[]{:S(2)}) %collective-permute-start.7) | collective-permute-done | bytes 57376 | tf_op jit(solution)/shard_map/ppermute | solution.py:15
  74.1 3.4 %fusion.14 = f32[2,56,32,128]{3,2,1,0:T(8,128)S(1)} fusion(f32[2,56,1,128]{3,2,1,0:T(1,128)S(1)} %collective-permute-done.7, f32[1,56,32,128]{3,2,1,0:T(8,128)S(1)} %bitcast.102, f32[1,56,32,128]{3,2,1,0:T(8,128)S(1)} %bitcast.105, f32[2,56,1,128]{3,2,1,0:T(1,128)S(1)} %collective-permute-done.6, f32[2,56,32,1]{3,2,1,0:T(8,128)} %copy.78, ...), kind=kLoop, calls=%fused_computation.55 | loop fusion | flops 5046272 | bytes 3813376 | tf_op jit(solution)/shard_map/add | solution.py:56
  77.5 2.8 %fusion.63 = (f32[56,32,128]{2,1,0:T(8,128)S(1)}, f32[56,32,128]{2,1,0:T(8,128)S(1)}) fusion(f32[56,32,128]{2,1,0:T(8,128)S(1)} %get-tuple-element.10, f32[1,32,128]{2,1,0:T(8,128)S(1)} %get-tuple-element.35, f32[1,32,128]{2,1,0:T(8,128)S(1)} %get-tuple-element.34, f32[2,56,32,128]{3,2,1,0:T(8,128)S(1)} %fusion.14, bf16[56,32,128]{2,1,0:T(8,128)(2,1)S(1)} %copy-done.6, ...), kind=kLoop, calls=%fused_computation.141 | loop fusion | flops 7798784 | bytes 6488064 | tf_op jit(solution)/shard_map/sub | solution.py:38
  80.3 2.5 %fusion.2 = (f32[2,56,32,1]{3,2,1,0:T(8,128)}, f32[2,56,32,1]{3,2,1,0:T(8,128)}) fusion(f32[1,56,32,128]{3,2,1,0:T(8,128)S(1)} %bitcast.91, f32[1,56,32,128]{3,2,1,0:T(8,128)S(1)} %bitcast.88), kind=kLoop, calls=%fused_computation.26 | loop fusion | flops 7168 | bytes 1863680 | tf_op jit(solution)/shard_map/stack | solution.py:53
  82.9 2.4 %copy.91 = f32[2,56,32,1]{1,2,3,0:T(8,128)S(1)} copy(f32[2,56,32,1]{3,2,1,0:T(8,128)} %get-tuple-element.16) | data formatting | bytes 28672
  85.2 1.9 %collective-permute-start.8 = (f32[2,56,32,1]{1,2,3,0:T(8,128)S(1)}, f32[2,56,32,1]{1,2,3,0:T(8,128)S(1)}, u32[]{:S(2)}, u32[]{:S(2)}) collective-permute-start(f32[2,56,32,1]{1,2,3,0:T(8,128)S(1)} %copy.91), channel_id=1, source_target_pairs={{32,0},{64,32},{96,64},{128,96},{160,128},{192,160},{224,192},{256... | collective-permute-start | bytes 43016 | tf_op jit(solution)/shard_map/ppermute | solution.py:18
  87.2 2.4 %copy.92 = f32[2,56,32,1]{1,2,3,0:T(8,128)S(1)} copy(f32[2,56,32,1]{3,2,1,0:T(8,128)} %get-tuple-element.17) | data formatting | bytes 28672
  89.6 5.7 %collective-permute-start.9 = (f32[2,56,32,1]{1,2,3,0:T(8,128)S(1)}, f32[2,56,32,1]{1,2,3,0:T(8,128)S(1)}, u32[]{:S(2)}, u32[]{:S(2)}) collective-permute-start(f32[2,56,32,1]{1,2,3,0:T(8,128)S(1)} %copy.92), channel_id=1, source_target_pairs={{0,32},{32,64},{64,96},{96,128},{128,160},{160,192},{192,224},{224... | collective-permute-start | bytes 43016 | tf_op jit(solution)/shard_map/ppermute | solution.py:15
  95.3 5.9 %collective-permute-start.10 = (f32[2,56,1,128]{3,2,1,0:T(1,128)S(1)}, f32[2,56,1,128]{3,2,1,0:T(1,128)S(1)}, u32[]{:S(2)}, u32[]{:S(2)}) collective-permute-start(f32[2,56,1,128]{3,2,1,0:T(1,128)S(1)} %get-tuple-element.18), channel_id=1, source_target_pairs={{1,0},{2,1},{3,2},{4,3},{5,4},{6,5},{7,6},{8,7},{9,8},{10,9},{11,1... | collective-permute-start | bytes 172040 | tf_op jit(solution)/shard_map/ppermute | solution.py:18
  101.2 2.1 %collective-permute-start.11 = (f32[2,56,1,128]{3,2,1,0:T(1,128)S(1)}, f32[2,56,1,128]{3,2,1,0:T(1,128)S(1)}, u32[]{:S(2)}, u32[]{:S(2)}) collective-permute-start(f32[2,56,1,128]{3,2,1,0:T(1,128)S(1)} %get-tuple-element.19), channel_id=1, source_target_pairs={{0,1},{1,2},{2,3},{3,4},{4,5},{5,6},{6,7},{7,8},{8,9},{9,10},{10,1... | collective-permute-start | bytes 172040 | tf_op jit(solution)/shard_map/ppermute | solution.py:15
  103.4 2.6 %copy.80 = f32[2,56,32,1]{3,2,1,0:T(8,128)} copy(f32[2,56,32,1]{1,2,3,0:T(8,128)S(1)} %collective-permute-done.8) | data formatting | bytes 28672 | tf_op jit(solution)/shard_map/ppermute | solution.py:18
  106.0 2.6 %copy.82 = f32[2,56,32,1]{3,2,1,0:T(8,128)} copy(f32[2,56,32,1]{1,2,3,0:T(8,128)S(1)} %collective-permute-done.9) | data formatting | bytes 28672 | tf_op jit(solution)/shard_map/ppermute | solution.py:15
  108.6 1.7 %collective-permute-done.11 = f32[2,56,1,128]{3,2,1,0:T(1,128)S(1)} collective-permute-done((f32[2,56,1,128]{3,2,1,0:T(1,128)S(1)}, f32[2,56,1,128]{3,2,1,0:T(1,128)S(1)}, u32[]{:S(2)}, u32[]{:S(2)}) %collective-permute-start.11) | collective-permute-done | bytes 57376 | tf_op jit(solution)/shard_map/ppermute | solution.py:15
  110.4 3.4 %fusion.11 = f32[2,56,32,128]{3,2,1,0:T(8,128)S(1)} fusion(f32[2,56,1,128]{3,2,1,0:T(1,128)S(1)} %collective-permute-done.11, f32[1,56,32,128]{3,2,1,0:T(8,128)S(1)} %bitcast.90, f32[1,56,32,128]{3,2,1,0:T(8,128)S(1)} %bitcast.93, f32[2,56,1,128]{3,2,1,0:T(1,128)S(1)} %collective-permute-done.10, f32[2,56,32,1]{3,2,1,0:T(8,128)} %copy.82, ...), kind=kLoop, calls=%fused_computation.44 | loop fusion | flops 5046272 | bytes 3813376 | tf_op jit(solution)/shard_map/add | solution.py:56
  113.8 0.9 fusion.46
  114.7 2.5 %fusion = (f32[2,56,32,1]{3,2,1,0:T(8,128)}, f32[2,56,32,1]{3,2,1,0:T(8,128)}) fusion(f32[1,56,32,128]{3,2,1,0:T(8,128)S(1)} %bitcast.97, f32[1,56,32,128]{3,2,1,0:T(8,128)S(1)} %bitcast.94), kind=kLoop, calls=%fused_computation.24 | loop fusion | flops 7168 | bytes 1863680 | tf_op jit(solution)/shard_map/stack | solution.py:53
  117.3 2.5 %copy.93 = f32[2,56,32,1]{1,2,3,0:T(8,128)S(1)} copy(f32[2,56,32,1]{3,2,1,0:T(8,128)} %get-tuple-element.12) | data formatting | bytes 28672
  119.8 1.9 %collective-permute-start.12 = (f32[2,56,32,1]{1,2,3,0:T(8,128)S(1)}, f32[2,56,32,1]{1,2,3,0:T(8,128)S(1)}, u32[]{:S(2)}, u32[]{:S(2)}) collective-permute-start(f32[2,56,32,1]{1,2,3,0:T(8,128)S(1)} %copy.93), channel_id=1, source_target_pairs={{32,0},{64,32},{96,64},{128,96},{160,128},{192,160},{224,192},{256... | collective-permute-start | bytes 43016 | tf_op jit(solution)/shard_map/ppermute | solution.py:18
  121.7 2.4 %copy.94 = f32[2,56,32,1]{1,2,3,0:T(8,128)S(1)} copy(f32[2,56,32,1]{3,2,1,0:T(8,128)} %get-tuple-element.13) | data formatting | bytes 28672
  124.1 5.7 %collective-permute-start.13 = (f32[2,56,32,1]{1,2,3,0:T(8,128)S(1)}, f32[2,56,32,1]{1,2,3,0:T(8,128)S(1)}, u32[]{:S(2)}, u32[]{:S(2)}) collective-permute-start(f32[2,56,32,1]{1,2,3,0:T(8,128)S(1)} %copy.94), channel_id=1, source_target_pairs={{0,32},{32,64},{64,96},{96,128},{128,160},{160,192},{192,224},{224... | collective-permute-start | bytes 43016 | tf_op jit(solution)/shard_map/ppermute | solution.py:15
  129.9 5.9 %collective-permute-start.14 = (f32[2,56,1,128]{3,2,1,0:T(1,128)S(1)}, f32[2,56,1,128]{3,2,1,0:T(1,128)S(1)}, u32[]{:S(2)}, u32[]{:S(2)}) collective-permute-start(f32[2,56,1,128]{3,2,1,0:T(1,128)S(1)} %get-tuple-element.14), channel_id=1, source_target_pairs={{1,0},{2,1},{3,2},{4,3},{5,4},{6,5},{7,6},{8,7},{9,8},{10,9},{11,1... | collective-permute-start | bytes 172040 | tf_op jit(solution)/shard_map/ppermute | solution.py:18
  135.8 1.9 %collective-permute-start.15 = (f32[2,56,1,128]{3,2,1,0:T(1,128)S(1)}, f32[2,56,1,128]{3,2,1,0:T(1,128)S(1)}, u32[]{:S(2)}, u32[]{:S(2)}) collective-permute-start(f32[2,56,1,128]{3,2,1,0:T(1,128)S(1)} %get-tuple-element.15), channel_id=1, source_target_pairs={{0,1},{1,2},{2,3},{3,4},{4,5},{5,6},{6,7},{7,8},{8,9},{9,10},{10,1... | collective-permute-start | bytes 172040 | tf_op jit(solution)/shard_map/ppermute | solution.py:15
  137.8 2.6 %copy.84 = f32[2,56,32,1]{3,2,1,0:T(8,128)} copy(f32[2,56,32,1]{1,2,3,0:T(8,128)S(1)} %collective-permute-done.12) | data formatting | bytes 28672 | tf_op jit(solution)/shard_map/ppermute | solution.py:18
  140.4 2.6 %copy.86 = f32[2,56,32,1]{3,2,1,0:T(8,128)} copy(f32[2,56,32,1]{1,2,3,0:T(8,128)S(1)} %collective-permute-done.13) | data formatting | bytes 28672 | tf_op jit(solution)/shard_map/ppermute | solution.py:15
  143.0 1.9 %collective-permute-done.15 = f32[2,56,1,128]{3,2,1,0:T(1,128)S(1)} collective-permute-done((f32[2,56,1,128]{3,2,1,0:T(1,128)S(1)}, f32[2,56,1,128]{3,2,1,0:T(1,128)S(1)}, u32[]{:S(2)}, u32[]{:S(2)}) %collective-permute-start.15) | collective-permute-done | bytes 57376 | tf_op jit(solution)/shard_map/ppermute | solution.py:15
  145.0 3.4 %fusion.8 = f32[2,56,32,128]{3,2,1,0:T(8,128)S(1)} fusion(f32[2,56,1,128]{3,2,1,0:T(1,128)S(1)} %collective-permute-done.15, f32[1,56,32,128]{3,2,1,0:T(8,128)S(1)} %bitcast.96, f32[1,56,32,128]{3,2,1,0:T(8,128)S(1)} %bitcast.99, f32[2,56,1,128]{3,2,1,0:T(1,128)S(1)} %collective-permute-done.14, f32[2,56,32,1]{3,2,1,0:T(8,128)} %copy.86, ...), kind=kLoop, calls=%fused_computation.33 | loop fusion | flops 5046272 | bytes 3813376 | tf_op jit(solution)/shard_map/add | solution.py:56
  148.4 2.1 %fusion.29 = (f32[56,32,128]{2,1,0:T(8,128)}, f32[56,32,128]{2,1,0:T(8,128)}) fusion(f32[56,32,128]{2,1,0:T(8,128)S(1)} %get-tuple-element.6, f32[1,32,128]{2,1,0:T(8,128)S(1)} %get-tuple-element.29, f32[1,32,128]{2,1,0:T(8,128)S(1)} %get-tuple-element.28, f32[2,56,32,128]{3,2,1,0:T(8,128)S(1)} %fusion.8, bf16[56,32,128]{2,1,0:T(8,128)(2,1)S(1)} %copy-done.6, ...), kind=kLoop, calls=%fused_computation.95 | loop fusion | flops 7798784 | bytes 6488064 | tf_op jit(solution)/shard_map/sub | solution.py:38
  (45 shorter events, 0.4 us)
Async XLA Ops:
  5.1 14.0 %copy-start.3 = (f32[56,32,128]{2,1,0:T(8,128)S(1)}, f32[56,32,128]{2,1,0:T(8,128)}, u32[]{:S(2)}) copy-start(f32[56,32,128]{2,1,0:T(8,128)} %param.5) | copy-start | bytes 2752516
  5.1 14.0 %copy-start.4 = (f32[56,32,128]{2,1,0:T(8,128)S(1)}, f32[56,32,128]{2,1,0:T(8,128)}, u32[]{:S(2)}) copy-start(f32[56,32,128]{2,1,0:T(8,128)} %param.4) | copy-start | bytes 2752516
  7.7 24.8 %collective-permute-start = (f32[2,56,32,1]{1,2,3,0:T(8,128)S(1)}, f32[2,56,32,1]{1,2,3,0:T(8,128)S(1)}, u32[]{:S(2)}, u32[]{:S(2)}) collective-permute-start(f32[2,56,32,1]{1,2,3,0:T(8,128)S(1)} %copy.87), channel_id=1, source_target_pairs={{32,0},{64,32},{96,64},{128,96},{160,128},{192,160},{224,192},{256... | collective-permute-start | bytes 43016 | tf_op jit(solution)/shard_map/ppermute | solution.py:18
  12.7 22.4 %collective-permute-start.1 = (f32[2,56,32,1]{1,2,3,0:T(8,128)S(1)}, f32[2,56,32,1]{1,2,3,0:T(8,128)S(1)}, u32[]{:S(2)}, u32[]{:S(2)}) collective-permute-start(f32[2,56,32,1]{1,2,3,0:T(8,128)S(1)} %copy.88), channel_id=1, source_target_pairs={{0,32},{32,64},{64,96},{96,128},{128,160},{160,192},{192,224},{224... | collective-permute-start | bytes 43016 | tf_op jit(solution)/shard_map/ppermute | solution.py:15
  19.2 18.5 %collective-permute-start.2 = (f32[2,56,1,128]{3,2,1,0:T(1,128)S(1)}, f32[2,56,1,128]{3,2,1,0:T(1,128)S(1)}, u32[]{:S(2)}, u32[]{:S(2)}) collective-permute-start(f32[2,56,1,128]{3,2,1,0:T(1,128)S(1)} %get-tuple-element.26), channel_id=1, source_target_pairs={{1,0},{2,1},{3,2},{4,3},{5,4},{6,5},{7,6},{8,7},{9,8},{10,9},{11,1... | collective-permute-start | bytes 172040 | tf_op jit(solution)/shard_map/ppermute | solution.py:18
  30.5 9.1 %collective-permute-start.3 = (f32[2,56,1,128]{3,2,1,0:T(1,128)S(1)}, f32[2,56,1,128]{3,2,1,0:T(1,128)S(1)}, u32[]{:S(2)}, u32[]{:S(2)}) collective-permute-start(f32[2,56,1,128]{3,2,1,0:T(1,128)S(1)} %get-tuple-element.27), channel_id=1, source_target_pairs={{0,1},{1,2},{2,3},{3,4},{4,5},{5,6},{6,7},{7,8},{8,9},{9,10},{10,1... | collective-permute-start | bytes 172040 | tf_op jit(solution)/shard_map/ppermute | solution.py:15
  37.7 5.4 %copy-start.5 = (f32[56,32,128]{2,1,0:T(8,128)S(1)}, f32[56,32,128]{2,1,0:T(8,128)}, u32[]{:S(2)}) copy-start(f32[56,32,128]{2,1,0:T(8,128)} %param.4) | copy-start | bytes 2752516
  37.7 5.4 %copy-start.6 = (bf16[56,32,128]{2,1,0:T(8,128)(2,1)S(1)}, bf16[56,32,128]{2,1,0:T(8,128)(2,1)}, u32[]{:S(2)}) copy-start(bf16[56,32,128]{2,1,0:T(8,128)(2,1)} %param.7) | copy-start | bytes 1376260
  37.7 5.4 %copy-start.7 = (bf16[56,32,128]{2,1,0:T(8,128)(2,1)S(1)}, bf16[56,32,128]{2,1,0:T(8,128)(2,1)}, u32[]{:S(2)}) copy-start(bf16[56,32,128]{2,1,0:T(8,128)(2,1)} %param.6) | copy-start | bytes 1376260
  44.0 30.1 %copy-start.2 = (f32[56,32,128]{2,1,0:T(8,128)}, f32[56,32,128]{2,1,0:T(8,128)S(1)}, u32[]{:S(2)}) copy-start(f32[56,32,128]{2,1,0:T(8,128)S(1)} %get-tuple-element.11) | copy-start | bytes 2752516
  49.0 18.0 %collective-permute-start.4 = (f32[2,56,32,1]{1,2,3,0:T(8,128)S(1)}, f32[2,56,32,1]{1,2,3,0:T(8,128)S(1)}, u32[]{:S(2)}, u32[]{:S(2)}) collective-permute-start(f32[2,56,32,1]{1,2,3,0:T(8,128)S(1)} %copy.89), channel_id=1, source_target_pairs={{32,0},{64,32},{96,64},{128,96},{160,128},{192,160},{224,192},{256... | collective-permute-start | bytes 43016 | tf_op jit(solution)/shard_map/ppermute | solution.py:18
  53.4 16.3 %collective-permute-start.5 = (f32[2,56,32,1]{1,2,3,0:T(8,128)S(1)}, f32[2,56,32,1]{1,2,3,0:T(8,128)S(1)}, u32[]{:S(2)}, u32[]{:S(2)}) collective-permute-start(f32[2,56,32,1]{1,2,3,0:T(8,128)S(1)} %copy.90), channel_id=1, source_target_pairs={{0,32},{32,64},{64,96},{96,128},{128,160},{160,192},{192,224},{224... | collective-permute-start | bytes 43016 | tf_op jit(solution)/shard_map/ppermute | solution.py:15
  59.1 13.2 %collective-permute-start.6 = (f32[2,56,1,128]{3,2,1,0:T(1,128)S(1)}, f32[2,56,1,128]{3,2,1,0:T(1,128)S(1)}, u32[]{:S(2)}, u32[]{:S(2)}) collective-permute-start(f32[2,56,1,128]{3,2,1,0:T(1,128)S(1)} %get-tuple-element.22), channel_id=1, source_target_pairs={{1,0},{2,1},{3,2},{4,3},{5,4},{6,5},{7,6},{8,7},{9,8},{10,9},{11,1... | collective-permute-start | bytes 172040 | tf_op jit(solution)/shard_map/ppermute | solution.py:18
  64.9 9.1 %collective-permute-start.7 = (f32[2,56,1,128]{3,2,1,0:T(1,128)S(1)}, f32[2,56,1,128]{3,2,1,0:T(1,128)S(1)}, u32[]{:S(2)}, u32[]{:S(2)}) collective-permute-start(f32[2,56,1,128]{3,2,1,0:T(1,128)S(1)} %get-tuple-element.23), channel_id=1, source_target_pairs={{0,1},{1,2},{2,3},{3,4},{4,5},{5,6},{6,7},{7,8},{8,9},{9,10},{10,1... | collective-permute-start | bytes 172040 | tf_op jit(solution)/shard_map/ppermute | solution.py:15
  72.3 5.2 %copy-start.8 = (bf16[56,32,128]{2,1,0:T(8,128)(2,1)S(1)}, bf16[56,32,128]{2,1,0:T(8,128)(2,1)}, u32[]{:S(2)}) copy-start(bf16[56,32,128]{2,1,0:T(8,128)(2,1)} %param.6) | copy-start | bytes 1376260
  85.2 18.1 %collective-permute-start.8 = (f32[2,56,32,1]{1,2,3,0:T(8,128)S(1)}, f32[2,56,32,1]{1,2,3,0:T(8,128)S(1)}, u32[]{:S(2)}, u32[]{:S(2)}) collective-permute-start(f32[2,56,32,1]{1,2,3,0:T(8,128)S(1)} %copy.91), channel_id=1, source_target_pairs={{32,0},{64,32},{96,64},{128,96},{160,128},{192,160},{224,192},{256... | collective-permute-start | bytes 43016 | tf_op jit(solution)/shard_map/ppermute | solution.py:18
  89.6 16.4 %collective-permute-start.9 = (f32[2,56,32,1]{1,2,3,0:T(8,128)S(1)}, f32[2,56,32,1]{1,2,3,0:T(8,128)S(1)}, u32[]{:S(2)}, u32[]{:S(2)}) collective-permute-start(f32[2,56,32,1]{1,2,3,0:T(8,128)S(1)} %copy.92), channel_id=1, source_target_pairs={{0,32},{32,64},{64,96},{96,128},{128,160},{160,192},{192,224},{224... | collective-permute-start | bytes 43016 | tf_op jit(solution)/shard_map/ppermute | solution.py:15
  95.3 13.3 %collective-permute-start.10 = (f32[2,56,1,128]{3,2,1,0:T(1,128)S(1)}, f32[2,56,1,128]{3,2,1,0:T(1,128)S(1)}, u32[]{:S(2)}, u32[]{:S(2)}) collective-permute-start(f32[2,56,1,128]{3,2,1,0:T(1,128)S(1)} %get-tuple-element.18), channel_id=1, source_target_pairs={{1,0},{2,1},{3,2},{4,3},{5,4},{6,5},{7,6},{8,7},{9,8},{10,9},{11,1... | collective-permute-start | bytes 172040 | tf_op jit(solution)/shard_map/ppermute | solution.py:18
  101.2 9.1 %collective-permute-start.11 = (f32[2,56,1,128]{3,2,1,0:T(1,128)S(1)}, f32[2,56,1,128]{3,2,1,0:T(1,128)S(1)}, u32[]{:S(2)}, u32[]{:S(2)}) collective-permute-start(f32[2,56,1,128]{3,2,1,0:T(1,128)S(1)} %get-tuple-element.19), channel_id=1, source_target_pairs={{0,1},{1,2},{2,3},{3,4},{4,5},{5,6},{6,7},{7,8},{8,9},{9,10},{10,1... | collective-permute-start | bytes 172040 | tf_op jit(solution)/shard_map/ppermute | solution.py:15
  108.6 5.1 %copy-start.9 = (bf16[56,32,128]{2,1,0:T(8,128)(2,1)S(1)}, bf16[56,32,128]{2,1,0:T(8,128)(2,1)}, u32[]{:S(2)}) copy-start(bf16[56,32,128]{2,1,0:T(8,128)(2,1)} %param.6) | copy-start | bytes 1376260
  114.7 2.5 %copy-start = (f32[56,32,128]{2,1,0:T(8,128)}, f32[56,32,128]{2,1,0:T(8,128)S(1)}, u32[]{:S(2)}) copy-start(f32[56,32,128]{2,1,0:T(8,128)S(1)} %get-tuple-element.7) | copy-start | bytes 2752516
  117.3 20.4 %copy-start.1 = (f32[56,32,128]{2,1,0:T(8,128)S(1)}, f32[56,32,128]{2,1,0:T(8,128)}, u32[]{:S(2)}) copy-start(f32[56,32,128]{2,1,0:T(8,128)} %copy-done) | copy-start | bytes 2752516
  119.8 18.0 %collective-permute-start.12 = (f32[2,56,32,1]{1,2,3,0:T(8,128)S(1)}, f32[2,56,32,1]{1,2,3,0:T(8,128)S(1)}, u32[]{:S(2)}, u32[]{:S(2)}) collective-permute-start(f32[2,56,32,1]{1,2,3,0:T(8,128)S(1)} %copy.93), channel_id=1, source_target_pairs={{32,0},{64,32},{96,64},{128,96},{160,128},{192,160},{224,192},{256... | collective-permute-start | bytes 43016 | tf_op jit(solution)/shard_map/ppermute | solution.py:18
  124.1 16.3 %collective-permute-start.13 = (f32[2,56,32,1]{1,2,3,0:T(8,128)S(1)}, f32[2,56,32,1]{1,2,3,0:T(8,128)S(1)}, u32[]{:S(2)}, u32[]{:S(2)}) collective-permute-start(f32[2,56,32,1]{1,2,3,0:T(8,128)S(1)} %copy.94), channel_id=1, source_target_pairs={{0,32},{32,64},{64,96},{96,128},{128,160},{160,192},{192,224},{224... | collective-permute-start | bytes 43016 | tf_op jit(solution)/shard_map/ppermute | solution.py:15
  129.9 13.2 %collective-permute-start.14 = (f32[2,56,1,128]{3,2,1,0:T(1,128)S(1)}, f32[2,56,1,128]{3,2,1,0:T(1,128)S(1)}, u32[]{:S(2)}, u32[]{:S(2)}) collective-permute-start(f32[2,56,1,128]{3,2,1,0:T(1,128)S(1)} %get-tuple-element.14), channel_id=1, source_target_pairs={{1,0},{2,1},{3,2},{4,3},{5,4},{6,5},{7,6},{8,7},{9,8},{10,9},{11,1... | collective-permute-start | bytes 172040 | tf_op jit(solution)/shard_map/ppermute | solution.py:18
  135.8 9.1 %collective-permute-start.15 = (f32[2,56,1,128]{3,2,1,0:T(1,128)S(1)}, f32[2,56,1,128]{3,2,1,0:T(1,128)S(1)}, u32[]{:S(2)}, u32[]{:S(2)}) collective-permute-start(f32[2,56,1,128]{3,2,1,0:T(1,128)S(1)} %get-tuple-element.15), channel_id=1, source_target_pairs={{0,1},{1,2},{2,3},{3,4},{4,5},{5,6},{6,7},{7,8},{8,9},{9,10},{10,1... | collective-permute-start | bytes 172040 | tf_op jit(solution)/shard_map/ppermute | solution.py:15
  143.0 5.4 %copy-start.10 = (bf16[56,32,128]{2,1,0:T(8,128)(2,1)S(1)}, bf16[56,32,128]{2,1,0:T(8,128)(2,1)}, u32[]{:S(2)}) copy-start(bf16[56,32,128]{2,1,0:T(8,128)(2,1)} %param.6) | copy-start | bytes 1376260
where the time goes:
time: 151 us
  starting transfers between devices  69 us (46%)
  local copies, waits for them, and re-layouts  40.4 us (27%)
  other arithmetic  32.7 us (22%)
  waiting for transfers between devices  7.34 us (5%)
    ppermute x8, starting transfers between devices, padded_2(): lax.ppermute(lax.slice_in_dim(block, 0, width, axis=dim), axis, backward)  37.2 us
    ppermute x8, starting transfers between devices, padded_2(): lax.ppermute(lax.slice_in_dim(block, block.shape[dim] - width, None, axis...  31.8 us
    unnamed x30, local copies, waits for them, and re-layouts  19.4 us
    add x4, other arithmetic, shards(): along_x[..., 2:] + along_x[..., :-2] + along_y[:, :, 2:, :]  13.7 us
    another operation x8, other arithmetic, shards(): both = jnp.stack([conc_u, conc_v])  12.4 us
    ppermute x4, local copies, waits for them, and re-layouts, padded_2(): lax.ppermute(lax.slice_in_dim(block, block.shape[dim] - width, None, axis...  10.6 us
    ppermute x4, local copies, waits for them, and re-layouts, padded_2(): lax.ppermute(lax.slice_in_dim(block, 0, width, axis=dim), axis, backward)  10.4 us
    ppermute x8, waiting for transfers between devices, padded_2(): lax.ppermute(lax.slice_in_dim(block, block.shape[dim] - width, None, axis...  7.32 us
  transfers between devices with their start and end apart: 16, of which 4 were waited for; matrix products, arithmetic and copies ran while one was open for 20% of the time, Pallas kernels for 0%

commit v1 on v0

v1 whole, which is shorter than its diff:
```python
import jax
import jax.numpy as jnp
from jax import lax
from jax.experimental import pallas as pl
from jax.experimental.pallas import tpu as pltpu
from jax.sharding import PartitionSpec as P

STEPS = 4
NZ, NY, NX = 56, 32, 128
W = 4
ROWS = NY + 2 * W
TILES = NZ // 8
ZP = NZ + 16
G = 24
VMEM_LIMIT = 48 * 1024 * 1024


def swap_pairs(count, parity):
    pairs = []
    for low in range(parity, count, 2):
        high = (low + 1) % count
        pairs += [(low, high), (high, low)]
    return pairs


def swap(block, axis, parity):
    return lax.ppermute(block, axis, swap_pairs(lax.axis_size(axis), parity))


def lanes():
    return lax.broadcasted_iota(jnp.int32, (8, NX), 1)


def take_lanes(value, index):
    return jnp.take_along_axis(value, index, axis=1, mode="promise_in_bounds")


def row_of(ref, y, tile):
    return ref[pl.ds(y + 8 * NY * tile, 8, stride=NY), :]


def widen(ref, wide):
    def body(i, carry):
        at = pl.ds(pl.multiple_of(i * 128, 128), 128)
        wide[at, :] = ref[at, :].astype(jnp.float32)
        return carry

    lax.fori_loop(0, NZ * NY // 128, body, 0)


def pack_y_kernel(u, v, f, k, out_b, out_a, fw, kw):
    even = lax.rem(lax.axis_index("gy"), 2) == 0
    widen(f, fw)
    widen(k, kw)
    for out, is_low in ((out_b, even), (out_a, jnp.logical_not(even))):
        start = jnp.where(is_low, 0, NY - W)
        start_rate = jnp.where(is_low, 0, NY - W + 1)
        for n, (ref, base, count) in enumerate(
            ((u, start, W), (v, start, W), (fw, start_rate, W - 1), (kw, start_rate, W - 1))
        ):
            first = (0, W, 2 * W, 3 * W - 1)[n]
            for r in range(count):
                for i in range(TILES):
                    out[first + r, 8 * i : 8 * i + 8, :] = row_of(ref, base + r, i)


def pack_y(u, v, f, k):
    shape = jax.ShapeDtypeStruct((4 * W - 2, NZ, NX), jnp.float32)
    return pl.pallas_call(
        pack_y_kernel,
        out_shape=(shape, shape),
        scratch_shapes=[pltpu.VMEM((NZ * NY, NX), jnp.float32)] * 2,
        compiler_params=pltpu.CompilerParams(vmem_limit_bytes=VMEM_LIMIT),
        name="pack_y",
    )(u, v, f, k)


def pack_x_kernel(u, v, f, k, out_b, out_a, fw, kw):
    even = lax.rem(lax.axis_index("gx"), 2) == 0
    widen(f, fw)
    widen(k, kw)
    lane = lanes()
    for n, ref in enumerate((u, v, fw, kw)):

        def body(y, carry):
            place = lax.rem(4 * (y + W), NX)
            mask_r = (lane >= place) & (lane < place + 4)
            place_l = lax.rem(place + 4, NX)
            mask_l = (lane >= place_l) & (lane < place_l + 4)
            new = []
            for i in range(TILES):
                value = pltpu.roll(row_of(ref, y, i), place + 4, 1)
                left, right = carry[i]
                new.append((jnp.where(mask_l, value, left), jnp.where(mask_r, value, right)))
            return tuple(new)

        zero = jnp.zeros((8, NX), jnp.float32)
        packed = lax.fori_loop(0, NY, body, ((zero, zero),) * TILES)
        for i, (left, right) in enumerate(packed):
            left = pltpu.roll(left, NX - 4, 1)
            out_b[n, 8 * i : 8 * i + 8, :] = jnp.where(even, left, right)
            out_a[n, 8 * i : 8 * i + 8, :] = jnp.where(even, right, left)


def pack_x(u, v, f, k):
    shape = jax.ShapeDtypeStruct((4, NZ, NX), jnp.float32)
    return pl.pallas_call(
        pack_x_kernel,
        out_shape=(shape, shape),
        scratch_shapes=[pltpu.VMEM((NZ * NY, NX), jnp.float32)] * 2,
        compiler_params=pltpu.CompilerParams(vmem_limit_bytes=VMEM_LIMIT),
        name="pack_x",
    )(u, v, f, k)


def pack_corner_kernel(x_b, x_a, out_b, out_a):
    even_x = lax.rem(lax.axis_index("gx"), 2) == 0
    even_y = lax.rem(lax.axis_index("gy"), 2) == 0
    lane = lanes()
    for i in range(TILES):
        at = slice(8 * i, 8 * i + 8)
        low = jnp.zeros((8, NX), jnp.float32)
        high = low
        for n in range(4):
            b, a = x_b[n, at, :], x_a[n, at, :]
            for side, value in enumerate((jnp.where(even_x, b, a), jnp.where(even_x, a, b))):
                place = (2 * n + side) * 16
                mask = (lane >= place) & (lane < place + 16)
                low = jnp.where(mask, pltpu.roll(value, (place - 16) % NX, 1), low)
                high = jnp.where(mask, pltpu.roll(value, place, 1), high)
        out_b[at, :] = jnp.where(even_y, low, high)
        out_a[at, :] = jnp.where(even_y, high, low)


def pack_corner(x_b, x_a):
    shape = jax.ShapeDtypeStruct((NZ, NX), jnp.float32)
    return pl.pallas_call(pack_corner_kernel, out_shape=(shape, shape), name="pack_corner")(x_b, x_a)


def step_plane(src_u, src_v, feed, decay, dst_u, dst_v, y):
    for i in range(TILES):
        z = 8 + 8 * i
        u = src_u[y, pl.ds(z, 8), :]
        v = src_v[y, pl.ds(z, 8), :]
        f = feed[y, pl.ds(z, 8), :]
        d = decay[y, pl.ds(z, 8), :]
        near_u = (
            pltpu.roll(u, 1, 1)
            + pltpu.roll(u, NX - 1, 1)
            + (src_u[y - 1, pl.ds(z, 8), :] + src_u[y + 1, pl.ds(z, 8), :])
        )
        near_v = (
            pltpu.roll(v, 1, 1)
            + pltpu.roll(v, NX - 1, 1)
            + (src_v[y - 1, pl.ds(z, 8), :] + src_v[y + 1, pl.ds(z, 8), :])
        )
        along_u = src_u[y, pl.ds(z - 1, 8), :] + src_u[y, pl.ds(z + 1, 8), :]
        along_v = src_v[y, pl.ds(z - 1, 8), :] + src_v[y, pl.ds(z + 1, 8), :]
        react = u * v * v
        new_u = (0.24 * near_u + 0.01 * along_u) + (0.02 * u + f * (1.0 - u)) - react
        new_v = (0.12 * near_v + 0.005 * along_v) + d * v + react
        dst_u[y, pl.ds(z, 8), :] = new_u
        dst_v[y, pl.ds(z, 8), :] = new_v
        if i == 0:
            dst_u[y, pl.ds(7, 1), :] = new_u[:1]
            dst_v[y, pl.ds(7, 1), :] = new_v[:1]
        if i == TILES - 1:
            dst_u[y, pl.ds(8 + NZ, 1), :] = new_u[7:]
            dst_v[y, pl.ds(8 + NZ, 1), :] = new_v[7:]


def put_plane(dst, y, i, value, ends):
    dst[y, pl.ds(8 + 8 * i, 8), :] = value
    if ends and i == 0:
        dst[y, pl.ds(7, 1), :] = value[:1]
    if ends and i == TILES - 1:
        dst[y, pl.ds(8 + NZ, 1), :] = value[7:]


def steps_kernel(
    u, v, f, k, y_b, y_a, x_b, x_a, c_b, c_a, out_u, out_v,
    fw, kw, u0, v0, u1, v1, feed, decay, su0, sv0, su1, sv1, s_feed, s_decay,
):
    even_x = lax.rem(lax.axis_index("gx"), 2) == 0
    even_y = lax.rem(lax.axis_index("gy"), 2) == 0
    widen(f, fw)
    widen(k, kw)
    lane = lanes()

    def own(y, carry):
        for i in range(TILES):
            put_plane(u0, y + W, i, row_of(u, y, i), True)
            put_plane(v0, y + W, i, row_of(v, y, i), True)
            rate = row_of(fw, y, i)
            put_plane(feed, y + W, i, rate, False)
            put_plane(decay, y + W, i, 0.51 - (rate + row_of(kw, y, i)), False)
        return carry

    lax.fori_loop(0, NY, own, 0)

    for src, is_low in ((y_b, even_y), (y_a, jnp.logical_not(even_y))):
        start = jnp.where(is_low, 0, NY + W)
        start_rate = jnp.where(is_low, 1, NY + W)
        for r in range(W):
            for i in range(TILES):
                at = slice(8 * i, 8 * i + 8)
                put_plane(u0, start + r, i, src[r, at, :], True)
                put_plane(v0, start + r, i, src[W + r, at, :], True)
                if r < W - 1:
                    rate = src[2 * W + r, at, :]
                    put_plane(feed, start_rate + r, i, rate, False)
                    put_plane(decay, start_rate + r, i, 0.51 - (rate + src[3 * W - 1 + r, at, :]), False)
    for ref in (feed, decay):
        for r in (0, ROWS - 1):
            for i in range(TILES):
                put_plane(ref, r, i, jnp.zeros((8, NX), jnp.float32), False)

    group = lax.div(lane, G)
    inner = lane - group * G
    own_index = jnp.where(inner < 8, inner + 120, jnp.where(inner >= 16, inner - 16, 0))
    own_lane = (inner < 8) | (inner >= 16)
    halo_d = lax.rem(inner, 4)
    is_right = (inner >= 8) & (inner < 12)
    is_left = (inner >= 12) & (inner < 16)

    def strip(j, carry):
        dense_index = lax.rem(lax.rem(group, 4) * 32 + j * 4 + halo_d, NX)
        is_low = j < W
        corner_group = jnp.where(is_low, 0, 4)
        is_corner = (group == corner_group) & (is_right | is_left)
        side = jnp.where(is_right, 1, 0)
        c_low = jnp.logical_not(jnp.logical_xor(is_low, even_y))
        for i in range(TILES):
            at = slice(8 * i, 8 * i + 8)
            corner = jnp.where(c_low, c_b[at, :], c_a[at, :])
            made = []
            for n, ref in enumerate((u0, v0, feed, decay)):
                value = jnp.zeros((8, NX), jnp.float32)
                for g in range(5):
                    row = ref[8 * g + j, pl.ds(8 + 8 * i, 8), :]
                    value = jnp.where((group == g) & own_lane, take_lanes(row, own_index), value)
                b, a = x_b[n, at, :], x_a[n, at, :]
                halo = jnp.where(
                    is_left,
                    take_lanes(jnp.where(even_x, b, a), dense_index),
                    take_lanes(jnp.where(even_x, a, b), dense_index),
                )
                corner_index = lax.rem((2 * n + side) * 16 + lax.rem(j, 4) * 4 + halo_d, NX)
                halo = jnp.where(is_corner, take_lanes(corner, corner_index), halo)
                made.append((value, halo))
            halo_lane = is_right | is_left
            rate = jnp.where(halo_lane, made[2][1], made[2][0])
            put_plane(su0, j + 1, i, jnp.where(halo_lane, made[0][1], made[0][0]), True)
            put_plane(sv0, j + 1, i, jnp.where(halo_lane, made[1][1], made[1][0]), True)
            put_plane(s_feed, j + 1, i, rate, False)
            put_plane(s_decay, j + 1, i, jnp.where(halo_lane, 0.51 - (rate + made[3][1]), made[3][0]), False)
        return carry

    lax.fori_loop(0, 8, strip, 0)

    main, strips = [(u0, v0), (u1, v1)], [(su0, sv0), (su1, sv1)]
    for step in range(STEPS):
        (mu, mv), (nu, nv) = main[step % 2], main[(step + 1) % 2]

        def main_row(y, carry):
            step_plane(mu, mv, feed, decay, nu, nv, y)
            return carry

        lax.fori_loop(step + 1, ROWS - 1 - step, main_row, 0)

        (tu, tv), (wu, wv) = strips[step % 2], strips[(step + 1) % 2]
        for ref in (tu, tv):
            for i in range(TILES):
                at = pl.ds(8 + 8 * i, 8)
                ref[0, at, :] = pltpu.roll(ref[8, at, :], G, 1)
                ref[9, at, :] = pltpu.roll(ref[1, at, :], NX - G, 1)

        def strip_row(y, carry):
            step_plane(tu, tv, s_feed, s_decay, wu, wv, y)
            return carry

        lax.fori_loop(1, 9, strip_row, 0)

    edge = (lane < 4) | (lane >= 124)

    def finish(y, carry):
        g, j = lax.div(y + W, 8), lax.rem(y + W, 8)
        index = lax.rem(jnp.where(lane < 4, lane + 16, lane + 8) + g * G, NX)
        index = jnp.where(lane < 4, lane + 16 + g * G, jnp.where(lane >= 124, lane - 120 + g * G, 0))
        for i in range(TILES):
            at = pl.ds(8 + 8 * i, 8)
            to = pl.ds(y + 8 * NY * i, 8, stride=NY)
            out_u[to, :] = jnp.where(edge, take_lanes(su0[j + 1, at, :], index), u0[y + W, at, :])
            out_v[to, :] = jnp.where(edge, take_lanes(sv0[j + 1, at, :], index), v0[y + W, at, :])
        return carry

    lax.fori_loop(0, NY, finish, 0)


def steps(*args):
    shape = jax.ShapeDtypeStruct((NZ * NY, NX), jnp.float32)
    wide = pltpu.VMEM((NZ * NY, NX), jnp.float32)
    field = pltpu.VMEM((ROWS, ZP, NX), jnp.float32)
    strip = pltpu.VMEM((10, ZP, NX), jnp.float32)
    return pl.pallas_call(
        steps_kernel,
        out_shape=(shape, shape),
        scratch_shapes=[wide] * 2 + [field] * 6 + [strip] * 6,
        compiler_params=pltpu.CompilerParams(vmem_limit_bytes=VMEM_LIMIT),
        name="steps",
    )(*args)


def shards(activator, inhibitor, feed_rate, kill_rate):
    u, v, f, k = (a.reshape(NZ * NY, NX) for a in (activator, inhibitor, feed_rate, kill_rate))
    send_b, send_a = pack_y(u, v, f, k)
    y_b = swap(send_b, "gy", 1)
    x_send_b, x_send_a = pack_x(u, v, f, k)
    x_b = swap(x_send_b, "gx", 1)
    x_a = swap(x_send_a, "gx", 0)
    y_a = swap(send_a, "gy", 0)
    c_send_b, c_send_a = pack_corner(x_b, x_a)
    c_b = swap(c_send_b, "gy", 1)
    c_a = swap(c_send_a, "gy", 0)
    out_u, out_v = steps(u, v, f, k, y_b, y_a, x_b, x_a, c_b, c_a)
    return out_u.reshape(NZ, NY, NX), out_v.reshape(NZ, NY, NX)


def solution(mesh):
    spec = P(None, "gy", "gx")
    return jax.shard_map(
        shards, mesh=mesh, in_specs=(spec,) * 4, out_specs=(spec,) * 2, check_vma=False
    )
```

time: 151 us -> 93.2 us (0.62)
  the two profiles are of different devices: /device:TPU:71 before, /device:TPU:6 now
where the time goes in v1:
time: 93.2 us; the launch traced here: 92.5 us
  Pallas kernels  50.2 us (54%)
  starting transfers between devices  27.8 us (30%)
  local copies, waits for them, and re-layouts  7.48 us (8%)
  waiting for transfers between devices  6.27 us (7%)
    pallas_call x1, Pallas kernels, steps(): pl.pallas_call(steps_kernel, out_shape=(shape, shape), scratch_shapes=[wi...  33.6 us
    ppermute x6, starting transfers between devices, swap(): return lax.ppermute(block, axis, swap_pairs(lax.axis_size(axis), parity))  27.8 us
    pallas_call x1, Pallas kernels, pack_x(): pl.pallas_call(pack_x_kernel, out_shape=(shape, shape), scratch_shapes=[p...  13.3 us
    unnamed x24, local copies, waits for them, and re-layouts  7.48 us
    ppermute x6, waiting for transfers between devices, swap(): return lax.ppermute(block, axis, swap_pairs(lax.axis_size(axis), parity))  6.27 us
  transfers between devices with their start and end apart: 6, of which 3 were waited for; matrix products, arithmetic and copies ran while one was open for 0% of the time, Pallas kernels for 16%

profile of v1, /device:TPU:6, one launch (start us, length us, event | category | flops | bytes accessed | tf_op | source)
XLA Modules:
  0.0 92.5 jit_solution(8490211810631187912)
XLA Ops:
  0.6 0.0 copy-start
  0.6 1.2 %copy-done = f32[56,32,128]{2,1,0:T(8,128)S(1)} copy-done((f32[56,32,128]{2,1,0:T(8,128)S(1)}, f32[56,32,128]{2,1,0:T(8,128)}, u32[]{:S(2)}) %copy-start) | copy-done | bytes 917528
  1.8 0.0 copy-start.2
  1.8 1.2 %copy-done.2 = f32[56,32,128]{2,1,0:T(8,128)S(1)} copy-done((f32[56,32,128]{2,1,0:T(8,128)S(1)}, f32[56,32,128]{2,1,0:T(8,128)}, u32[]{:S(2)}) %copy-start.2) | copy-done | bytes 917528
  3.0 0.0 copy-start.4
  3.0 1.0 %copy-done.4 = bf16[56,32,128]{2,1,0:T(8,128)(2,1)S(1)} copy-done((bf16[56,32,128]{2,1,0:T(8,128)(2,1)S(1)}, bf16[56,32,128]{2,1,0:T(8,128)(2,1)}, u32[]{:S(2)}) %copy-start.4) | copy-done | bytes 458776
  4.0 0.0 copy-start.6
  4.0 1.0 %copy-done.6 = bf16[56,32,128]{2,1,0:T(8,128)(2,1)S(1)} copy-done((bf16[56,32,128]{2,1,0:T(8,128)(2,1)S(1)}, bf16[56,32,128]{2,1,0:T(8,128)(2,1)}, u32[]{:S(2)}) %copy-start.6) | copy-done | bytes 458776
  5.0 1.6 %pack_y.1 = (f32[14,56,128]{2,1,0:T(8,128)}, f32[14,56,128]{2,1,0:T(8,128)}) custom-call(f32[1792,128]{1,0:T(8,128)S(1)} %bitcast.6, f32[1792,128]{1,0:T(8,128)S(1)} %bitcast.9, bf16[1792,128]{1,0:T(8,128)(2,1)S(1)} %bitcast.12, bf16[1792,128]{1,0:T(8,128)(2,1)S(1)} %bitcast.15), custom_call_target="tpu_custom_call" | custom-call | tf_op jit(solution)/shard_map/pack_y/pallas_call | solution.py:69
  6.6 13.8 %collective-permute-start = (f32[14,56,128]{2,1,0:T(8,128)}, f32[14,56,128]{2,1,0:T(8,128)S(1)}, u32[]{:S(2)}, u32[]{:S(2)}) collective-permute-start(f32[14,56,128]{2,1,0:T(8,128)} %get-tuple-element.10), channel_id=1, source_target_pairs={{1,2},{2,1},{3,4},{4,3},{5,6},{6,5},{7,8},{8,7},{9,10},{10,9},{11,... | collective-permute-start | bytes 1204232 | tf_op jit(solution)/shard_map/ppermute | solution.py:27
  20.4 0.0 copy-start.1
  20.4 0.0 copy-start.3
  20.5 2.1 %collective-permute-start.1 = (f32[14,56,128]{2,1,0:T(8,128)}, f32[14,56,128]{2,1,0:T(8,128)}, u32[]{:S(2)}, u32[]{:S(2)}) collective-permute-start(f32[14,56,128]{2,1,0:T(8,128)} %get-tuple-element.11), channel_id=1, source_target_pairs={{0,1},{1,0},{2,3},{3,2},{4,5},{5,4},{6,7},{7,6},{8,9},{9,8},{10,11... | collective-permute-start | bytes 1204232 | tf_op jit(solution)/shard_map/ppermute | solution.py:27
  22.5 0.0 copy-start.5
  22.5 0.0 copy-start.7
  22.5 13.3 %pack_x.1 = (f32[4,56,128]{2,1,0:T(8,128)S(1)}, f32[4,56,128]{2,1,0:T(8,128)S(1)}) custom-call(f32[1792,128]{1,0:T(8,128)S(1)} %bitcast.7, f32[1792,128]{1,0:T(8,128)S(1)} %bitcast.10, bf16[1792,128]{1,0:T(8,128)(2,1)S(1)} %bitcast.13, bf16[1792,128]{1,0:T(8,128)(2,1)S(1)} %bitcast.16), custom_call_target="tpu_custom_call" | custom-call | tf_op jit(solution)/shard_map/pack_x/pallas_call | solution.py:107
  35.9 2.8 %collective-permute-start.2 = (f32[4,56,128]{2,1,0:T(8,128)S(1)}, f32[4,56,128]{2,1,0:T(8,128)S(1)}, u32[]{:S(2)}, u32[]{:S(2)}) collective-permute-start(f32[4,56,128]{2,1,0:T(8,128)S(1)} %get-tuple-element.12), channel_id=1, source_target_pairs={{32,64},{64,32},{96,128},{128,96},{160,192},{192,160},{224,256},{2... | collective-permute-start | bytes 344072 | tf_op jit(solution)/shard_map/ppermute | solution.py:27
  38.7 2.6 %collective-permute-start.3 = (f32[4,56,128]{2,1,0:T(8,128)S(1)}, f32[4,56,128]{2,1,0:T(8,128)S(1)}, u32[]{:S(2)}, u32[]{:S(2)}) collective-permute-start(f32[4,56,128]{2,1,0:T(8,128)S(1)} %get-tuple-element.13), channel_id=1, source_target_pairs={{0,32},{32,0},{64,96},{96,64},{128,160},{160,128},{192,224},{224,1... | collective-permute-start | bytes 344072 | tf_op jit(solution)/shard_map/ppermute | solution.py:27
  41.3 2.2 %collective-permute-done.2.x_b = f32[4,56,128]{2,1,0:T(8,128)S(1)} collective-permute-done((f32[4,56,128]{2,1,0:T(8,128)S(1)}, f32[4,56,128]{2,1,0:T(8,128)S(1)}, u32[]{:S(2)}, u32[]{:S(2)}) %collective-permute-start.2) | collective-permute-done | bytes 114720 | tf_op jit(solution)/shard_map/ppermute | solution.py:27
  43.5 0.0 copy-start.8
  43.5 0.0 collective-permute-done.3.x_a
  43.5 0.6 copy-done.8
  44.2 0.0 copy-start.10
  44.2 0.6 copy-done.10
  44.8 1.8 %pack_corner.1 = (f32[56,128]{1,0:T(8,128)}, f32[56,128]{1,0:T(8,128)}) custom-call(f32[4,56,128]{2,1,0:T(8,128)} %copy-done.8, f32[4,56,128]{2,1,0:T(8,128)} %copy-done.10), custom_call_target="tpu_custom_call" | custom-call | tf_op jit(solution)/shard_map/pack_corner/pallas_call | solution.py:137
  46.6 4.6 %collective-permute-start.4 = (f32[56,128]{1,0:T(8,128)}, f32[56,128]{1,0:T(8,128)S(1)}, u32[]{:S(2)}, u32[]{:S(2)}) collective-permute-start(f32[56,128]{1,0:T(8,128)} %get-tuple-element.14), channel_id=1, source_target_pairs={{1,2},{2,1},{3,4},{4,3},{5,6},{6,5},{7,8},{8,7},{9,10},{10,9},{11,... | collective-permute-start | bytes 86024 | tf_op jit(solution)/shard_map/ppermute | solution.py:27
  51.1 1.9 %collective-permute-start.5 = (f32[56,128]{1,0:T(8,128)}, f32[56,128]{1,0:T(8,128)S(1)}, u32[]{:S(2)}, u32[]{:S(2)}) collective-permute-start(f32[56,128]{1,0:T(8,128)} %get-tuple-element.15), channel_id=1, source_target_pairs={{0,1},{1,0},{2,3},{3,2},{4,5},{5,4},{6,7},{7,6},{8,9},{9,8},{10,11... | collective-permute-start | bytes 86024 | tf_op jit(solution)/shard_map/ppermute | solution.py:27
  53.1 3.7 %collective-permute-done.4.c_b = f32[56,128]{1,0:T(8,128)S(1)} collective-permute-done((f32[56,128]{1,0:T(8,128)}, f32[56,128]{1,0:T(8,128)S(1)}, u32[]{:S(2)}, u32[]{:S(2)}) %collective-permute-start.4) | collective-permute-done | bytes 28704 | tf_op jit(solution)/shard_map/ppermute | solution.py:27
  56.8 0.4 collective-permute-done.5.c_a
  57.1 0.0 collective-permute-done.y_b
  57.1 0.0 collective-permute-done.1.y_a
  57.1 0.0 copy-done.1
  57.1 0.0 copy-done.3
  57.1 0.0 copy-done.5
  57.2 0.0 copy-done.7
  57.2 0.0 copy-start.9
  57.2 0.9 copy-done.9
  58.1 0.0 copy-start.11
  58.1 0.9 copy-done.11
  59.0 33.6 %steps.1 = (f32[1792,128]{1,0:T(8,128)}, f32[1792,128]{1,0:T(8,128)}) custom-call(f32[1792,128]{1,0:T(8,128)S(1)} %bitcast.8, f32[1792,128]{1,0:T(8,128)S(1)} %bitcast.11, bf16[1792,128]{1,0:T(8,128)(2,1)S(1)} %bitcast.14, bf16[1792,128]{1,0:T(8,128)(2,1)S(1)} %bitcast.17, f32[14,56,128]{2,1,0:T(8,128)S(1)} %collective-permute-done.y_b, ...), custom_call_target="tpu_custom_call" | custom-call | tf_op jit(solution)/shard_map/steps/pallas_call | solution.py:305
Async XLA Ops:
  0.6 1.2 %copy-start = (f32[56,32,128]{2,1,0:T(8,128)S(1)}, f32[56,32,128]{2,1,0:T(8,128)}, u32[]{:S(2)}) copy-start(f32[56,32,128]{2,1,0:T(8,128)} %param.4) | copy-start | bytes 2752516
  1.8 1.2 %copy-start.2 = (f32[56,32,128]{2,1,0:T(8,128)S(1)}, f32[56,32,128]{2,1,0:T(8,128)}, u32[]{:S(2)}) copy-start(f32[56,32,128]{2,1,0:T(8,128)} %param.5) | copy-start | bytes 2752516
  3.0 1.0 %copy-start.4 = (bf16[56,32,128]{2,1,0:T(8,128)(2,1)S(1)}, bf16[56,32,128]{2,1,0:T(8,128)(2,1)}, u32[]{:S(2)}) copy-start(bf16[56,32,128]{2,1,0:T(8,128)(2,1)} %param.6) | copy-start | bytes 1376260
  4.0 1.0 %copy-start.6 = (bf16[56,32,128]{2,1,0:T(8,128)(2,1)S(1)}, bf16[56,32,128]{2,1,0:T(8,128)(2,1)}, u32[]{:S(2)}) copy-start(bf16[56,32,128]{2,1,0:T(8,128)(2,1)} %param.7) | copy-start | bytes 1376260
  6.6 50.5 %collective-permute-start = (f32[14,56,128]{2,1,0:T(8,128)}, f32[14,56,128]{2,1,0:T(8,128)S(1)}, u32[]{:S(2)}, u32[]{:S(2)}) collective-permute-start(f32[14,56,128]{2,1,0:T(8,128)} %get-tuple-element.10), channel_id=1, source_target_pairs={{1,2},{2,1},{3,4},{4,3},{5,6},{6,5},{7,8},{8,7},{9,10},{10,9},{11,... | collective-permute-start | bytes 1204232 | tf_op jit(solution)/shard_map/ppermute | solution.py:27
  20.4 36.7 %copy-start.1 = (f32[56,32,128]{2,1,0:T(8,128)S(1)}, f32[56,32,128]{2,1,0:T(8,128)}, u32[]{:S(2)}) copy-start(f32[56,32,128]{2,1,0:T(8,128)} %param.4) | copy-start | bytes 2752516
  20.4 36.7 %copy-start.3 = (f32[56,32,128]{2,1,0:T(8,128)S(1)}, f32[56,32,128]{2,1,0:T(8,128)}, u32[]{:S(2)}) copy-start(f32[56,32,128]{2,1,0:T(8,128)} %param.5) | copy-start | bytes 2752516
  20.5 36.7 %collective-permute-start.1 = (f32[14,56,128]{2,1,0:T(8,128)}, f32[14,56,128]{2,1,0:T(8,128)}, u32[]{:S(2)}, u32[]{:S(2)}) collective-permute-start(f32[14,56,128]{2,1,0:T(8,128)} %get-tuple-element.11), channel_id=1, source_target_pairs={{0,1},{1,0},{2,3},{3,2},{4,5},{5,4},{6,7},{7,6},{8,9},{9,8},{10,11... | collective-permute-start | bytes 1204232 | tf_op jit(solution)/shard_map/ppermute | solution.py:27
  22.5 34.6 %copy-start.5 = (bf16[56,32,128]{2,1,0:T(8,128)(2,1)S(1)}, bf16[56,32,128]{2,1,0:T(8,128)(2,1)}, u32[]{:S(2)}) copy-start(bf16[56,32,128]{2,1,0:T(8,128)(2,1)} %param.6) | copy-start | bytes 1376260
  22.5 34.6 %copy-start.7 = (bf16[56,32,128]{2,1,0:T(8,128)(2,1)S(1)}, bf16[56,32,128]{2,1,0:T(8,128)(2,1)}, u32[]{:S(2)}) copy-start(bf16[56,32,128]{2,1,0:T(8,128)(2,1)} %param.7) | copy-start | bytes 1376260
  35.9 7.6 %collective-permute-start.2 = (f32[4,56,128]{2,1,0:T(8,128)S(1)}, f32[4,56,128]{2,1,0:T(8,128)S(1)}, u32[]{:S(2)}, u32[]{:S(2)}) collective-permute-start(f32[4,56,128]{2,1,0:T(8,128)S(1)} %get-tuple-element.12), channel_id=1, source_target_pairs={{32,64},{64,32},{96,128},{128,96},{160,192},{192,160},{224,256},{2... | collective-permute-start | bytes 344072 | tf_op jit(solution)/shard_map/ppermute | solution.py:27
  38.7 4.8 %collective-permute-start.3 = (f32[4,56,128]{2,1,0:T(8,128)S(1)}, f32[4,56,128]{2,1,0:T(8,128)S(1)}, u32[]{:S(2)}, u32[]{:S(2)}) collective-permute-start(f32[4,56,128]{2,1,0:T(8,128)S(1)} %get-tuple-element.13), channel_id=1, source_target_pairs={{0,32},{32,0},{64,96},{96,64},{128,160},{160,128},{192,224},{224,1... | collective-permute-start | bytes 344072 | tf_op jit(solution)/shard_map/ppermute | solution.py:27
  43.5 0.6 copy-start.8
  44.2 0.6 copy-start.10
  46.6 10.2 %collective-permute-start.4 = (f32[56,128]{1,0:T(8,128)}, f32[56,128]{1,0:T(8,128)S(1)}, u32[]{:S(2)}, u32[]{:S(2)}) collective-permute-start(f32[56,128]{1,0:T(8,128)} %get-tuple-element.14), channel_id=1, source_target_pairs={{1,2},{2,1},{3,4},{4,3},{5,6},{6,5},{7,8},{8,7},{9,10},{10,9},{11,... | collective-permute-start | bytes 86024 | tf_op jit(solution)/shard_map/ppermute | solution.py:27
  51.1 6.0 %collective-permute-start.5 = (f32[56,128]{1,0:T(8,128)}, f32[56,128]{1,0:T(8,128)S(1)}, u32[]{:S(2)}, u32[]{:S(2)}) collective-permute-start(f32[56,128]{1,0:T(8,128)} %get-tuple-element.15), channel_id=1, source_target_pairs={{0,1},{1,0},{2,3},{3,2},{4,5},{5,4},{6,7},{7,6},{8,9},{9,8},{10,11... | collective-permute-start | bytes 86024 | tf_op jit(solution)/shard_map/ppermute | solution.py:27
  57.2 0.9 copy-start.9
  58.1 0.9 copy-start.11

commit v2 on v0

v2 whole, which is shorter than its diff:
```python
import jax
import jax.numpy as jnp
from jax import lax
from jax.experimental import pallas as pl
from jax.experimental.pallas import tpu as pltpu
from jax.sharding import PartitionSpec as P

STEPS = 4
NZ, NY, NX = 56, 32, 128
W = 4
PY = 48
OWN, LOW, HIGH = 8, 4, 40
ROWS = range(LOW, HIGH + 4, 8)
MSG = 4 * W - 2
GROUPS, GZ = 8, NZ // 8
VMEM_LIMIT = 32 * 1024 * 1024
LOAD_VMEM_LIMIT = 57 * 1024 * 1024


def swap_pairs(count, parity):
    pairs = []
    for low in range(parity, count, 2):
        high = (low + 1) % count
        pairs += [(low, high), (high, low)]
    return pairs


def swap(block, axis, parity):
    return lax.ppermute(block, axis, swap_pairs(lax.axis_size(axis), parity))


def is_even(axis):
    return lax.rem(lax.axis_index(axis), 2) == 0


def lanes():
    return lax.broadcasted_iota(jnp.int32, (8, NX), 1)


def turn(value, shift, axis=1):
    shift = shift % value.shape[axis]
    return value if shift == 0 else pltpu.roll(value, shift, axis)


def pallas(kernel, name, limit=VMEM_LIMIT, **kwargs):
    params = pltpu.CompilerParams(vmem_limit_bytes=limit)
    return pl.pallas_call(kernel, name=name, compiler_params=params, **kwargs)


def f32(*shape):
    return jax.ShapeDtypeStruct(shape, jnp.float32)


def load_kernel(u, v, f, k, pu, pv, fs, ks, out_b, out_a, fw, kw, sems):
    own = pl.ds(OWN, NY)
    copies = [
        pltpu.make_async_copy(f, fs, sems.at[0]),
        pltpu.make_async_copy(k, ks, sems.at[1]),
        pltpu.make_async_copy(u, pu.at[:, own, :], sems.at[2]),
        pltpu.make_async_copy(v, pv.at[:, own, :], sems.at[3]),
    ]
    for copy in copies:
        copy.start()
    even = is_even("gy")
    starts = (jnp.where(even, OWN, OWN + 28), jnp.where(even, OWN + 28, OWN))
    rate_starts = (jnp.where(even, 0, 13), jnp.where(even, 13, 0))

    def rates(z, carry):
        for src, wide, at in ((fs, fw, 8), (ks, kw, 11)):
            row = pl.multiple_of(z * NY, NY)
            wide[z, 0:8, :] = src[pl.ds(row, 16), :].astype(jnp.float32)[:8]
            wide[z, 8:16, :] = src[pl.ds(row + 16, 16), :].astype(jnp.float32)[8:]
            for out, start in zip((out_b, out_a), rate_starts):
                out[pl.ds(z * MSG + at, 3), :] = wide[z, pl.ds(start, 3), :]
        return carry

    def fields(z, carry):
        for src, at in ((pu, 0), (pv, 4)):
            for out, start in zip((out_b, out_a), starts):
                out[pl.ds(z * MSG + at, 4), :] = src[z, pl.ds(start, 4), :]
        return carry

    copies[0].wait()
    copies[1].wait()
    lax.fori_loop(0, NZ, rates, 0, unroll=2)
    copies[2].wait()
    copies[3].wait()
    lax.fori_loop(0, NZ, fields, 0, unroll=4)


def load(u, v, f, k):
    edge = pltpu.VMEM((NZ, 16, NX), jnp.float32)
    rates = jax.ShapeDtypeStruct((NZ * NY, NX), jnp.bfloat16)
    padded, message = f32(NZ, PY, NX), f32(NZ * MSG, NX)
    return pallas(
        load_kernel,
        "load",
        LOAD_VMEM_LIMIT,
        out_shape=(padded, padded, rates, rates, message, message),
        in_specs=[pl.BlockSpec(memory_space=pltpu.HBM)] * 4,
        scratch_shapes=[edge, edge, pltpu.SemaphoreType.DMA((4,))],
    )(u, v, f, k)


def pack_x_kernel(u, v, f, k, strips, out_b, out_a):
    even = is_even("gx")
    lane = lanes()
    inner = lax.rem(lane, 16)
    group = lax.div(lane, 16)

    def body(j, carry):
        for n, ref in enumerate((u, v, f, k)):
            right, left = [None] * 4, [None] * 4
            for g in range(GROUPS):
                z = GZ * g + j
                tiles = []
                if n < 2:
                    tiles = [ref[z, pl.ds(OWN + 8 * t, 8), :] for t in range(4)]
                else:
                    for t in range(0, 4, 2):
                        at = pl.multiple_of(z * NY, NY) + 8 * t
                        two = ref[pl.ds(at, 16), :].astype(jnp.float32)
                        tiles += [two[:8], two[8:]]
                for t in range(4):
                    value = turn(tiles[t], 16 * g + 8)
                    right[t] = value if g == 0 else jnp.where(group == g, value, right[t])
            for t in range(4):
                pass
            left_edge = right_edge = None
            for t in range(4):
                strips[n, j, 8 * t : 8 * t + 8, :] = right[t]
                low, high = turn(right[t], 4 * t - 8), turn(right[t], 4 * t - 4)
                here = (inner >= 4 * t) & (inner < 4 * t + 4)
                left_edge = low if t == 0 else jnp.where(here, low, left_edge)
                right_edge = high if t == 0 else jnp.where(here, high, right_edge)
            out_b[n, j] = jnp.where(even, left_edge, right_edge)
            out_a[n, j] = jnp.where(even, right_edge, left_edge)
        return carry

    lax.fori_loop(0, GZ, body, 0)


def pack_x(u, v, f, k):
    edge = f32(4, GZ, 8, NX)
    return pallas(pack_x_kernel, "pack_x", out_shape=(f32(4, GZ, NY, NX), edge, edge))(u, v, f, k)


def pack_corner_kernel(x_b, x_a, out_b, out_a):
    even_x, even_y = is_even("gx"), is_even("gy")
    inner = lax.rem(lanes(), 16)
    top = lax.broadcasted_iota(jnp.int32, (8, NX), 0) < 4

    def body(j, carry):
        rows = []
        for first, base in ((0, 0), (4, 12)):
            sides = []
            for is_right in (True, False):
                value = None
                for n in range(4):
                    b, a = x_b[n, j], x_a[n, j]
                    halo = jnp.where(even_x, a, b) if is_right else jnp.where(even_x, b, a)
                    here = (inner >= 4 * n) & (inner < 4 * n + 4)
                    halo = turn(halo, 4 * n - base)
                    value = halo if n == 0 else jnp.where(here, halo, value)
                sides.append(turn(value, (0 if is_right else 4) - first, 0))
            rows.append(jnp.where(top, sides[0], sides[1]))
        out_b[j] = jnp.where(even_y, rows[0], rows[1])
        out_a[j] = jnp.where(even_y, rows[1], rows[0])
        return carry

    lax.fori_loop(0, GZ, body, 0, unroll=True)


def pack_corner(x_b, x_a):
    return pallas(pack_corner_kernel, "pack_corner", out_shape=(f32(GZ, 8, NX),) * 2)(x_b, x_a)


def x_sums(src_u, src_v, z, rows):
    sums = []
    for ref in (src_u, src_v):
        for row in rows:
            value = ref[z, pl.ds(row, 8), :]
            sums.append(turn(value, 1) + turn(value, -1))
    return tuple(sums)


def step_rows(src_u, src_v, feed, decay, z, below, above, row, x_u, x_v):
    at, down, up = pl.ds(row, 8), pl.ds(row - 1, 8), pl.ds(row + 1, 8)
    u, v, f = src_u[z, at, :], src_v[z, at, :], feed[z, at, :]
    near_u = x_u + (src_u[z, down, :] + src_u[z, up, :])
    near_v = x_v + (src_v[z, down, :] + src_v[z, up, :])
    along_u = src_u[below, at, :] + src_u[above, at, :]
    along_v = src_v[below, at, :] + src_v[above, at, :]
    react = u * (v * v)
    new_u = (0.24 * near_u + 0.01 * along_u) + (f - u * (f - 0.02)) - react
    new_v = (0.12 * near_v + 0.005 * along_v) + decay[z, at, :] * v + react
    return new_u, new_v


def sweep(src, rates, rows, count, place, emit, unroll):
    def body(i, sums):
        z, below, above = place(i)
        ahead = x_sums(*src, place(jnp.minimum(i + 1, count - 1))[0], rows)
        values = [
            step_rows(*src, *rates, z, below, above, row, sums[n], sums[len(rows) + n])
            for n, row in enumerate(rows)
        ]
        emit(z, values)
        return ahead

    lax.fori_loop(0, count, body, x_sums(*src, place(0)[0], rows), unroll=unroll)


def steps_kernel(
    u, v, f, k, y_b, y_a, strips, x_b, x_a, c_b, c_a, out_u, out_v, u0, v0,
    u1, v1, feed, decay, su0, sv0, su1, sv1, s_feed, s_kill, sems,
):
    even_x, even_y = is_even("gx"), is_even("gy")
    lane = lanes()
    inner = lax.rem(lane, 16)
    group = lax.div(lane, 16)
    start = (jnp.where(even_y, LOW, HIGH), jnp.where(even_y, HIGH, LOW))
    rate_start = (jnp.where(even_y, LOW + 1, HIGH), jnp.where(even_y, HIGH, LOW + 1))

    def own(z, carry):
        at = pl.multiple_of(z * NY, NY)
        for t in range(0, 4, 2):
            here, to = pl.ds(at + 8 * t, 16), pl.ds(OWN + 8 * t, 16)
            rate = f[here, :].astype(jnp.float32)
            feed[z, to, :] = rate
            decay[z, to, :] = 0.51 - (rate + k[here, :].astype(jnp.float32))
        for src, to, rate_to in zip((y_b, y_a), start, rate_start):
            at = z * MSG
            u0[z, pl.ds(to, 4), :] = src[pl.ds(at, 4), :]
            v0[z, pl.ds(to, 4), :] = src[pl.ds(at + 4, 4), :]
            rate = src[pl.ds(at + 8, 3), :]
            feed[z, pl.ds(rate_to, 3), :] = rate
            decay[z, pl.ds(rate_to, 3), :] = 0.51 - (rate + src[pl.ds(at + 11, 3), :])
        return carry

    lax.fori_loop(0, NZ, own, 0, unroll=2)

    right_halo = (inner >= 8) & (inner < 12)
    left_halo = (inner >= 4) & (inner < 8)
    right_plane, left_plane = 1, GZ + 3
    s_refs = (su0, sv0, s_feed, s_kill)

    def strip(j, carry):
        for n, ref in enumerate(s_refs):
            b, a = x_b[n, j], x_a[n, j]
            on_right, on_left = jnp.where(even_x, a, b), jnp.where(even_x, b, a)
            for t in range(4):
                to = pl.ds(OWN + 8 * t, 8)
                value = strips[n, j, 8 * t : 8 * t + 8, :]
                ref[j + right_plane, to, :] = jnp.where(right_halo, turn(on_right, 8 - 4 * t), value)
                ref[j + left_plane, to, :] = jnp.where(left_halo, turn(on_left, 4 - 4 * t), value)
        for y, c, to, rate_to in zip((y_b, y_a), (c_b, c_a), start, rate_start):
            fields = rates = None
            for g in range(GROUPS):
                at = (GZ * g + j) * MSG
                one = turn(y[pl.ds(at, 8), :], 16 * g + 8)
                two = turn(y[pl.ds(at + 6, 8), :], 16 * g + 8)
                fields = one if g == 0 else jnp.where(group == g, one, fields)
                rates = two if g == 0 else jnp.where(group == g, two, rates)
            corner = c[j]
            other = turn(corner, 4, 0)
            for plane, mask, lane_at, top in (
                (j + right_plane, right_halo, 8, corner),
                (j + left_plane, left_halo, 4, other),
            ):
                su0[plane, pl.ds(to, 4), :] = jnp.where(mask, turn(top, lane_at), fields)[:4]
                bottom = other if top is corner else corner
                sv0[plane, pl.ds(to, 4), :] = jnp.where(mask, turn(bottom, lane_at - 4), fields)[4:]
                s_feed[plane, pl.ds(rate_to, 3), :] = rates[2:5]
                s_kill[plane, pl.ds(rate_to, 3), :] = rates[5:]
                for n, ref in ((2, s_feed), (3, s_kill)):
                    halo = turn(top, lane_at - 4 * n)[:4]
                    ref[plane, pl.ds(to, 4), :] = jnp.where(mask[:4], halo, ref[plane, pl.ds(to, 4), :])
        for plane in (j + right_plane, j + left_plane):
            for row in ROWS:
                at = pl.ds(row, 8)
                s_kill[plane, at, :] = 0.51 - (s_feed[plane, at, :] + s_kill[plane, at, :])
        return carry

    lax.fori_loop(0, GZ, strip, 0)

    def strip_place(i):
        z = jnp.where(i < GZ, i + right_plane, i - GZ + left_plane)
        return z, z - 1, z + 1

    levels = [(su0, sv0), (su1, sv1)]
    for step in range(STEPS):
        src, dst = levels[step % 2], levels[(step + 1) % 2]
        for ref in src:
            for plane in (right_plane, left_plane):
                for row in ROWS:
                    at = pl.ds(row, 8)
                    first, last = ref[plane, at, :], ref[plane + GZ - 1, at, :]
                    ref[plane - 1, at, :] = jnp.where(group == 0, first, turn(last, 16))
                    ref[plane + GZ, at, :] = jnp.where(group == GROUPS - 1, last, turn(first, -16))

        def strip_emit(z, values, dst=dst):
            for row, (new_u, new_v) in zip(ROWS, values):
                dst[0][z, pl.ds(row, 8), :] = new_u
                dst[1][z, pl.ds(row, 8), :] = new_v

        sweep(src, (s_feed, s_kill), ROWS, 2 * GZ, strip_place, strip_emit, 7)

    for j in range(GZ):
        for old, new in ((su0, su1), (sv0, sv1)):
            for t in range(4):
                at = pl.ds(OWN + 8 * t, 8)
                new[j, at, :] = jnp.where(inner < 8, old[j + right_plane, at, :], old[j + left_plane, at, :])

    def place(i):
        return i, jnp.maximum(i - 1, 0), jnp.minimum(i + 1, NZ - 1)

    edge = (lane < 4) | (lane >= 124)
    levels = [(u0, v0), (u1, v1)]
    for step in range(STEPS):
        src, dst = levels[step % 2], levels[(step + 1) % 2]

        def emit(z, values, dst=dst):
            for row, (new_u, new_v) in zip(ROWS, values):
                dst[0][z, pl.ds(row, 8), :] = new_u
                dst[1][z, pl.ds(row, 8), :] = new_v

        def finish(z, values):
            g = lax.div(z, GZ)
            back = NX - 8 - 16 * g
            for t, (new_u, new_v) in enumerate(values):
                at, to = pl.ds(OWN + 8 * t, 8), pl.ds(pl.multiple_of(z * NY, NY) + 8 * t, 8)
                j = z - g * GZ
                out_u[to, :] = jnp.where(edge, pltpu.roll(su1[j, at, :], back, 1), new_u)
                out_v[to, :] = jnp.where(edge, pltpu.roll(sv1[j, at, :], back, 1), new_v)

        if step < STEPS - 1:
            sweep(src, (feed, decay), ROWS, NZ, place, emit, 8)
        else:
            sweep(src, (feed, decay), range(OWN, OWN + NY, 8), NZ, place, finish, 8)


def steps(*args):
    field = pltpu.VMEM((NZ, PY, NX), jnp.float32)
    strip = pltpu.VMEM((2 * GZ + 4, PY, NX), jnp.float32)
    out, padded = f32(NZ * NY, NX), f32(NZ, PY, NX)
    return pallas(
        steps_kernel,
        "steps",
        out_shape=(out, out, padded, padded),
        input_output_aliases={0: 2, 1: 3},
        scratch_shapes=[field] * 4 + [strip] * 6 + [pltpu.SemaphoreType.DMA((2,))],
    )(*args)[:2]


def shards(activator, inhibitor, feed_rate, kill_rate):
    f, k = feed_rate.reshape(NZ * NY, NX), kill_rate.reshape(NZ * NY, NX)
    u, v, f, k, send_b, send_a = load(activator, inhibitor, f, k)
    y_b = swap(send_b, "gy", 1)
    y_a = swap(send_a, "gy", 0)
    strips, x_send_b, x_send_a = pack_x(u, v, f, k)
    x_b = swap(x_send_b, "gx", 1)
    x_a = swap(x_send_a, "gx", 0)
    c_send_b, c_send_a = pack_corner(x_b, x_a)
    c_b = swap(c_send_b, "gy", 1)
    c_a = swap(c_send_a, "gy", 0)
    out_u, out_v = steps(u, v, f, k, y_b, y_a, strips, x_b, x_a, c_b, c_a)
    return out_u.reshape(NZ, NY, NX), out_v.reshape(NZ, NY, NX)


def solution(mesh):
    spec = P(None, "gy", "gx")
    return jax.shard_map(
        shards, mesh=mesh, in_specs=(spec,) * 4, out_specs=(spec,) * 2, check_vma=False
    )
```

time: 151 us -> 65.3 us (0.43)
  the two profiles are of different devices: /device:TPU:71 before, /device:TPU:6 now
where the time goes in v2:
time: 65.3 us; the launch traced here: 64.5 us
  starting transfers between devices  33.1 us (51%)
  Pallas kernels  19.3 us (30%)
  waiting for transfers between devices  6.62 us (10%)
  local copies, waits for them, and re-layouts  4.71 us (7%)
  between operations  0.72 us (1%)
    ppermute x6, starting transfers between devices, swap(): return lax.ppermute(block, axis, swap_pairs(lax.axis_size(axis), parity))  33.1 us
    pallas_call x1, Pallas kernels, steps(): pallas(steps_kernel, 'steps', out_shape=(out, out, padded, padded), input...  12.9 us
    ppermute x6, waiting for transfers between devices, swap(): return lax.ppermute(block, axis, swap_pairs(lax.axis_size(axis), parity))  6.62 us
    unnamed x10, local copies, waits for them, and re-layouts  4.71 us
    pallas_call x1, Pallas kernels, load(): pallas(load_kernel, 'load', LOAD_VMEM_LIMIT, out_shape=(padded, padded, r...  4.02 us
    pallas_call x1, Pallas kernels, pack_x(): pallas(pack_x_kernel, 'pack_x', out_shape=(f32(4, GZ, NY, NX), edge, edge))  2.19 us
  transfers between devices with their start and end apart: 6, of which 2 were waited for; matrix products, arithmetic and copies ran while one was open for 0% of the time, Pallas kernels for 4%

profile of v2, /device:TPU:6, one launch (start us, length us, event | category | flops | bytes accessed | tf_op | source)
XLA Modules:
  0.0 64.5 jit_solution(2879858778462093640)
XLA Ops:
  0.6 4.0 %load.1 = (f32[56,48,128]{2,1,0:T(8,128)}, f32[56,48,128]{2,1,0:T(8,128)}, bf16[1792,128]{1,0:T(8,128)(2,1)}, bf16[1792,128]{1,0:T(8,128)(2,1)}, f32[784,128]{1,0:T(8,128)}, /*index=5*/f32[784,128]{1,0:T(8,128)}) custom-call(f32[56,32,128]{2,1,0:T(8,128)} %u.1, f32[56,32,128]{2,1,0:T(8,128)} %v.1, bf16[1792,128]{1,0:T(8,128)(2,1)} %bitcast.4, ...), custom_call_target="tpu_custom_call" | custom-call | tf_op jit(solution)/shard_map/load/pallas_call | solution.py:95
  4.7 13.8 %collective-permute-start = (f32[784,128]{1,0:T(8,128)}, f32[784,128]{1,0:T(8,128)S(1)}, u32[]{:S(2)}, u32[]{:S(2)}) collective-permute-start(f32[784,128]{1,0:T(8,128)} %get-tuple-element.19), channel_id=1, source_target_pairs={{1,2},{2,1},{3,4},{4,3},{5,6},{6,5},{7,8},{8,7},{9,10},{10,9},{11,... | collective-permute-start | bytes 1204232 | tf_op jit(solution)/shard_map/ppermute | solution.py:29
  18.5 1.9 %collective-permute-start.1 = (f32[784,128]{1,0:T(8,128)}, f32[784,128]{1,0:T(8,128)S(1)}, u32[]{:S(2)}, u32[]{:S(2)}) collective-permute-start(f32[784,128]{1,0:T(8,128)} %get-tuple-element.20), channel_id=1, source_target_pairs={{0,1},{1,0},{2,3},{3,2},{4,5},{5,4},{6,7},{7,6},{8,9},{9,8},{10,11... | collective-permute-start | bytes 1204232 | tf_op jit(solution)/shard_map/ppermute | solution.py:29
  20.4 0.0 copy-start
  20.4 1.3 %copy-done = f32[56,48,128]{2,1,0:T(8,128)S(1)} copy-done((f32[56,48,128]{2,1,0:T(8,128)S(1)}, f32[56,48,128]{2,1,0:T(8,128)}, u32[]{:S(2)}) %copy-start) | copy-done | bytes 1376280
  21.8 0.0 copy-start.2
  21.8 1.3 %copy-done.2 = f32[56,48,128]{2,1,0:T(8,128)S(1)} copy-done((f32[56,48,128]{2,1,0:T(8,128)S(1)}, f32[56,48,128]{2,1,0:T(8,128)}, u32[]{:S(2)}) %copy-start.2) | copy-done | bytes 1376280
  23.1 0.0 copy-start.3
  23.1 1.0 %copy-done.3 = bf16[1792,128]{1,0:T(8,128)(2,1)S(1)} copy-done((bf16[1792,128]{1,0:T(8,128)(2,1)S(1)}, bf16[1792,128]{1,0:T(8,128)(2,1)}, u32[]{:S(2)}) %copy-start.3) | copy-done | bytes 458776
  24.1 0.0 copy-start.4
  24.1 1.0 %copy-done.4 = bf16[1792,128]{1,0:T(8,128)(2,1)S(1)} copy-done((bf16[1792,128]{1,0:T(8,128)(2,1)S(1)}, bf16[1792,128]{1,0:T(8,128)(2,1)}, u32[]{:S(2)}) %copy-start.4) | copy-done | bytes 458776
  25.2 0.0 copy-start.1
  25.2 2.2 %pack_x.1 = (f32[4,7,32,128]{3,2,1,0:T(8,128)S(1)}, f32[4,7,8,128]{3,2,1,0:T(8,128)S(1)}, f32[4,7,8,128]{3,2,1,0:T(8,128)S(1)}) custom-call(f32[56,48,128]{2,1,0:T(8,128)S(1)} %copy-done, f32[56,48,128]{2,1,0:T(8,128)S(1)} %copy-done.2, bf16[1792,128]{1,0:T(8,128)(2,1)S(1)} %copy-done.3, bf16[1792,128]{1,0:T(8,128)(2,1)S(1)} %copy-done.4), custom_call_target="tpu_custom_call" | custom-call | tf_op jit(solution)/shard_map/pack_x/pallas_call | solution.py:145
  27.4 2.8 %collective-permute-start.2 = (f32[4,7,8,128]{3,2,1,0:T(8,128)S(1)}, f32[4,7,8,128]{3,2,1,0:T(8,128)S(1)}, u32[]{:S(2)}, u32[]{:S(2)}) collective-permute-start(f32[4,7,8,128]{3,2,1,0:T(8,128)S(1)} %get-tuple-element.22), channel_id=1, source_target_pairs={{32,64},{64,32},{96,128},{128,96},{160,192},{192,160},{224,256},{2... | collective-permute-start | bytes 344072 | tf_op jit(solution)/shard_map/ppermute | solution.py:29
  30.2 2.6 %collective-permute-start.3 = (f32[4,7,8,128]{3,2,1,0:T(8,128)S(1)}, f32[4,7,8,128]{3,2,1,0:T(8,128)S(1)}, u32[]{:S(2)}, u32[]{:S(2)}) collective-permute-start(f32[4,7,8,128]{3,2,1,0:T(8,128)S(1)} %get-tuple-element.23), channel_id=1, source_target_pairs={{0,32},{32,0},{64,96},{96,64},{128,160},{160,128},{192,224},{224,1... | collective-permute-start | bytes 344072 | tf_op jit(solution)/shard_map/ppermute | solution.py:29
  32.8 2.8 %collective-permute-done.2.x_b = f32[4,7,8,128]{3,2,1,0:T(8,128)S(1)} collective-permute-done((f32[4,7,8,128]{3,2,1,0:T(8,128)S(1)}, f32[4,7,8,128]{3,2,1,0:T(8,128)S(1)}, u32[]{:S(2)}, u32[]{:S(2)}) %collective-permute-start.2) | collective-permute-done | bytes 114720 | tf_op jit(solution)/shard_map/ppermute | solution.py:29
  35.5 0.0 collective-permute-done.3.x_a
  35.6 0.2 pack_corner.1
  35.7 10.1 %collective-permute-start.4 = (f32[7,8,128]{2,1,0:T(8,128)S(1)}, f32[7,8,128]{2,1,0:T(8,128)S(1)}, u32[]{:S(2)}, u32[]{:S(2)}) collective-permute-start(f32[7,8,128]{2,1,0:T(8,128)S(1)} %get-tuple-element.24), channel_id=1, source_target_pairs={{1,2},{2,1},{3,4},{4,3},{5,6},{6,5},{7,8},{8,7},{9,10},{10,9},{11,... | collective-permute-start | bytes 86024 | tf_op jit(solution)/shard_map/ppermute | solution.py:29
  45.8 1.9 %collective-permute-start.5 = (f32[7,8,128]{2,1,0:T(8,128)S(1)}, f32[7,8,128]{2,1,0:T(8,128)S(1)}, u32[]{:S(2)}, u32[]{:S(2)}) collective-permute-start(f32[7,8,128]{2,1,0:T(8,128)S(1)} %get-tuple-element.25), channel_id=1, source_target_pairs={{0,1},{1,0},{2,3},{3,2},{4,5},{5,4},{6,7},{7,6},{8,9},{9,8},{10,11... | collective-permute-start | bytes 86024 | tf_op jit(solution)/shard_map/ppermute | solution.py:29
  47.7 0.0 collective-permute-done.4.c_b
  47.7 3.8 %collective-permute-done.5.c_a = f32[7,8,128]{2,1,0:T(8,128)S(1)} collective-permute-done((f32[7,8,128]{2,1,0:T(8,128)S(1)}, f32[7,8,128]{2,1,0:T(8,128)S(1)}, u32[]{:S(2)}, u32[]{:S(2)}) %collective-permute-start.5) | collective-permute-done | bytes 28704 | tf_op jit(solution)/shard_map/ppermute | solution.py:29
  51.6 0.0 collective-permute-done.y_b
  51.6 0.0 collective-permute-done.1.y_a
  51.6 0.0 copy-done.1
  51.6 12.9 %steps.1 = (f32[1792,128]{1,0:T(8,128)}, f32[1792,128]{1,0:T(8,128)}, f32[56,48,128]{2,1,0:T(8,128)S(1)}, f32[56,48,128]{2,1,0:T(8,128)S(1)}) custom-call(f32[56,48,128]{2,1,0:T(8,128)S(1)} %copy-done.1, f32[56,48,128]{2,1,0:T(8,128)S(1)} %copy-done.2, bf16[1792,128]{1,0:T(8,128)(2,1)S(1)} %copy-done.3, ...), custom_call_target="tpu_custom_call", output_to_operand_aliasing={{2}: (0, {}), {3}: (1, {})} | custom-call | tf_op jit(solution)/shard_map/steps/pallas_call | solution.py:347
Async XLA Ops:
  4.7 46.9 %collective-permute-start = (f32[784,128]{1,0:T(8,128)}, f32[784,128]{1,0:T(8,128)S(1)}, u32[]{:S(2)}, u32[]{:S(2)}) collective-permute-start(f32[784,128]{1,0:T(8,128)} %get-tuple-element.19), channel_id=1, source_target_pairs={{1,2},{2,1},{3,4},{4,3},{5,6},{6,5},{7,8},{8,7},{9,10},{10,9},{11,... | collective-permute-start | bytes 1204232 | tf_op jit(solution)/shard_map/ppermute | solution.py:29
  18.5 33.1 %collective-permute-start.1 = (f32[784,128]{1,0:T(8,128)}, f32[784,128]{1,0:T(8,128)S(1)}, u32[]{:S(2)}, u32[]{:S(2)}) collective-permute-start(f32[784,128]{1,0:T(8,128)} %get-tuple-element.20), channel_id=1, source_target_pairs={{0,1},{1,0},{2,3},{3,2},{4,5},{5,4},{6,7},{7,6},{8,9},{9,8},{10,11... | collective-permute-start | bytes 1204232 | tf_op jit(solution)/shard_map/ppermute | solution.py:29
  20.4 1.3 %copy-start = (f32[56,48,128]{2,1,0:T(8,128)S(1)}, f32[56,48,128]{2,1,0:T(8,128)}, u32[]{:S(2)}) copy-start(f32[56,48,128]{2,1,0:T(8,128)} %get-tuple-element.15.u) | copy-start | bytes 4128772
  21.8 1.3 %copy-start.2 = (f32[56,48,128]{2,1,0:T(8,128)S(1)}, f32[56,48,128]{2,1,0:T(8,128)}, u32[]{:S(2)}) copy-start(f32[56,48,128]{2,1,0:T(8,128)} %get-tuple-element.16.v) | copy-start | bytes 4128772
  23.1 1.0 %copy-start.3 = (bf16[1792,128]{1,0:T(8,128)(2,1)S(1)}, bf16[1792,128]{1,0:T(8,128)(2,1)}, u32[]{:S(2)}) copy-start(bf16[1792,128]{1,0:T(8,128)(2,1)} %get-tuple-element.17.f) | copy-start | bytes 1376260
  24.1 1.0 %copy-start.4 = (bf16[1792,128]{1,0:T(8,128)(2,1)S(1)}, bf16[1792,128]{1,0:T(8,128)(2,1)}, u32[]{:S(2)}) copy-start(bf16[1792,128]{1,0:T(8,128)(2,1)} %get-tuple-element.18.k) | copy-start | bytes 1376260
  25.2 26.4 %copy-start.1 = (f32[56,48,128]{2,1,0:T(8,128)S(1)}, f32[56,48,128]{2,1,0:T(8,128)}, u32[]{:S(2)}) copy-start(f32[56,48,128]{2,1,0:T(8,128)} %get-tuple-element.15.u) | copy-start | bytes 4128772
  27.4 8.2 %collective-permute-start.2 = (f32[4,7,8,128]{3,2,1,0:T(8,128)S(1)}, f32[4,7,8,128]{3,2,1,0:T(8,128)S(1)}, u32[]{:S(2)}, u32[]{:S(2)}) collective-permute-start(f32[4,7,8,128]{3,2,1,0:T(8,128)S(1)} %get-tuple-element.22), channel_id=1, source_target_pairs={{32,64},{64,32},{96,128},{128,96},{160,192},{192,160},{224,256},{2... | collective-permute-start | bytes 344072 | tf_op jit(solution)/shard_map/ppermute | solution.py:29
  30.2 5.4 %collective-permute-start.3 = (f32[4,7,8,128]{3,2,1,0:T(8,128)S(1)}, f32[4,7,8,128]{3,2,1,0:T(8,128)S(1)}, u32[]{:S(2)}, u32[]{:S(2)}) collective-permute-start(f32[4,7,8,128]{3,2,1,0:T(8,128)S(1)} %get-tuple-element.23), channel_id=1, source_target_pairs={{0,32},{32,0},{64,96},{96,64},{128,160},{160,128},{192,224},{224,1... | collective-permute-start | bytes 344072 | tf_op jit(solution)/shard_map/ppermute | solution.py:29
  35.7 12.0 %collective-permute-start.4 = (f32[7,8,128]{2,1,0:T(8,128)S(1)}, f32[7,8,128]{2,1,0:T(8,128)S(1)}, u32[]{:S(2)}, u32[]{:S(2)}) collective-permute-start(f32[7,8,128]{2,1,0:T(8,128)S(1)} %get-tuple-element.24), channel_id=1, source_target_pairs={{1,2},{2,1},{3,4},{4,3},{5,6},{6,5},{7,8},{8,7},{9,10},{10,9},{11,... | collective-permute-start | bytes 86024 | tf_op jit(solution)/shard_map/ppermute | solution.py:29
  45.8 5.8 %collective-permute-start.5 = (f32[7,8,128]{2,1,0:T(8,128)S(1)}, f32[7,8,128]{2,1,0:T(8,128)S(1)}, u32[]{:S(2)}, u32[]{:S(2)}) collective-permute-start(f32[7,8,128]{2,1,0:T(8,128)S(1)} %get-tuple-element.25), channel_id=1, source_target_pairs={{0,1},{1,0},{2,3},{3,2},{4,5},{5,4},{6,7},{7,6},{8,9},{9,8},{10,11... | collective-permute-start | bytes 86024 | tf_op jit(solution)/shard_map/ppermute | solution.py:29

commit v3 on v0

v3 whole, which is shorter than its diff:
```python
import jax
import jax.numpy as jnp
from jax import lax
from jax.experimental import pallas as pl
from jax.experimental.pallas import tpu as pltpu
from jax.sharding import PartitionSpec as P

STEPS = 4
NZ, NY, NX = 56, 32, 128
W = 4
PY = 48
OWN, LOW, HIGH = 8, 4, 40
MSG = 4 * W - 2
GROUPS, GZ = 8, NZ // 8
CORNER = NZ * MSG
RIGHT, LEFT = 1, GZ + 3
SPLANES = 2 * GZ + 4


def swap_pairs(count, parity):
    pairs = []
    for low in range(parity, count, 2):
        high = (low + 1) % count
        pairs += [(low, high), (high, low)]
    return pairs


def swap(block, axis, parity):
    return lax.ppermute(block, axis, swap_pairs(lax.axis_size(axis), parity))


def is_even(axis):
    return lax.rem(lax.axis_index(axis), 2) == 0


def lanes():
    lane = lax.broadcasted_iota(jnp.int32, (8, NX), 1)
    return lane, lax.rem(lane, 16), lax.div(lane, 16)


def turn(value, shift, axis=1):
    shift = shift % value.shape[axis]
    return value if shift == 0 else pltpu.roll(value, shift, axis)


def vmem(*shape):
    return pltpu.VMEM(shape, jnp.float32)


FIELD = (NZ, PY, NX)
STRIP = (SPLANES, PY, NX)
EDGE = (4, GZ, 8, NX)
MESSAGE = (NZ * MSG + 8 * GZ, NX)


def pallas(kernel, name, megabytes, flops=0, **kwargs):
    return pl.pallas_call(
        kernel,
        name=name,
        compiler_params=pltpu.CompilerParams(vmem_limit_bytes=megabytes * 1024 * 1024),
        cost_estimate=pl.CostEstimate(flops=flops, bytes_accessed=flops // 4, transcendentals=0),
        **kwargs,
    )


def load_kernel(u, v, f, k, pu, pv, feed, decay, su, sv, s_feed, s_decay, out_b, out_a, fs, ks, sems):
    own = pl.ds(OWN, NY)
    copies = [
        pltpu.make_async_copy(f, fs, sems.at[0]),
        pltpu.make_async_copy(k, ks, sems.at[1]),
        pltpu.make_async_copy(u, pu.at[:, own, :], sems.at[2]),
        pltpu.make_async_copy(v, pv.at[:, own, :], sems.at[3]),
    ]
    for copy in copies:
        copy.start()
    even = is_even("gx")
    _, inner, group = lanes()

    def rates(z, carry):
        for t in range(0, 4, 2):
            at, to = pl.ds(pl.multiple_of(z * NY, NY) + 8 * t, 16), pl.ds(OWN + 8 * t, 16)
            rate = fs[at, :].astype(jnp.float32)
            feed[z, to, :] = rate
            decay[z, to, :] = 0.51 - (rate + ks[at, :].astype(jnp.float32))
        return carry

    copies[0].wait()
    copies[1].wait()
    lax.fori_loop(0, NZ, rates, 0, unroll=4)

    for n, src, dst in ((2, feed, s_feed), (3, decay, s_decay), (0, pu, su), (1, pv, sv)):
        if n == 0:
            copies[2].wait()
        if n == 1:
            copies[3].wait()

        def body(j, carry, n=n, src=src, dst=dst):
            left_edge = right_edge = None
            for t in range(4):
                at = pl.ds(OWN + 8 * t, 8)
                both = None
                for g in range(GROUPS):
                    value = turn(src[GZ * g + j, at, :], 16 * g + 8)
                    both = value if g == 0 else jnp.where(group == g, value, both)
                dst[j + RIGHT, at, :] = both
                dst[j + LEFT, at, :] = both
                low, high = turn(both, 4 * t - 8), turn(both, 4 * t - 4)
                here = (inner >= 4 * t) & (inner < 4 * t + 4)
                left_edge = low if t == 0 else jnp.where(here, low, left_edge)
                right_edge = high if t == 0 else jnp.where(here, high, right_edge)
            out_b[n, j] = jnp.where(even, left_edge, right_edge)
            out_a[n, j] = jnp.where(even, right_edge, left_edge)
            return carry

        lax.fori_loop(0, GZ, body, 0, unroll=True)


def load(u, v, f, k):
    f, k = f.reshape(NZ * NY, NX), k.reshape(NZ * NY, NX)
    u, v, f, k = (pltpu.with_memory_space_constraint(a, pltpu.HBM) for a in (u, v, f, k))
    rates = pltpu.VMEM((NZ * NY, NX), jnp.bfloat16)
    return pallas(
        load_kernel,
        "load",
        8,
        out_shape=(vmem(*FIELD),) * 4 + (vmem(*STRIP),) * 4 + (vmem(*EDGE),) * 2,
        in_specs=[pl.BlockSpec(memory_space=pltpu.HBM)] * 4,
        scratch_shapes=[rates, rates, pltpu.SemaphoreType.DMA((4,))],
    )(u, v, f, k)


def pack_y_kernel(u, v, feed, decay, x_b, x_a, out_b, out_a):
    even_x, even_y = is_even("gx"), is_even("gy")
    _, inner, _ = lanes()
    top = lax.broadcasted_iota(jnp.int32, (8, NX), 0) < 4
    starts = (jnp.where(even_y, OWN, OWN + 28), jnp.where(even_y, OWN + 28, OWN))
    rate_starts = (jnp.where(even_y, OWN, OWN + 29), jnp.where(even_y, OWN + 29, OWN))

    def rows(z, carry):
        for out, start, rate_start in zip((out_b, out_a), starts, rate_starts):
            at = z * MSG
            out[pl.ds(at, 4), :] = u[z, pl.ds(start, 4), :]
            out[pl.ds(at + 4, 4), :] = v[z, pl.ds(start, 4), :]
            out[pl.ds(at + 8, 3), :] = feed[z, pl.ds(rate_start, 3), :]
            out[pl.ds(at + 11, 3), :] = decay[z, pl.ds(rate_start, 3), :]
        return carry

    lax.fori_loop(0, NZ, rows, 0, unroll=4)
    for j in range(GZ):
        made = []
        for first, base in ((0, 0), (4, 12)):
            sides = []
            for is_right in (True, False):
                value = None
                for n in range(4):
                    b, a = x_b[n, j], x_a[n, j]
                    halo = jnp.where(even_x, a, b) if is_right else jnp.where(even_x, b, a)
                    here = (inner >= 4 * n) & (inner < 4 * n + 4)
                    halo = turn(halo, 4 * n - base)
                    value = halo if n == 0 else jnp.where(here, halo, value)
                sides.append(turn(value, (0 if is_right else 4) - first, 0))
            made.append(jnp.where(top, sides[0], sides[1]))
        at = pl.ds(CORNER + 8 * j, 8)
        out_b[at, :] = jnp.where(even_y, made[0], made[1])
        out_a[at, :] = jnp.where(even_y, made[1], made[0])


def pack_y(u, v, feed, decay, x_b, x_a):
    return pallas(pack_y_kernel, "pack_y", 8, out_shape=(vmem(*MESSAGE),) * 2)(u, v, feed, decay, x_b, x_a)


def x_sums(src_u, src_v, z, rows):
    sums = []
    for ref in (src_u, src_v):
        for row in rows:
            value = ref[z, pl.ds(row, 8), :]
            sums.append(turn(value, 1) + turn(value, -1))
    return tuple(sums)


def step_rows(src_u, src_v, feed, decay, z, below, above, row, x_u, x_v):
    at, down, up = pl.ds(row, 8), pl.ds(row - 1, 8), pl.ds(row + 1, 8)
    u, v, f = src_u[z, at, :], src_v[z, at, :], feed[z, at, :]
    near_u = x_u + (src_u[z, down, :] + src_u[z, up, :])
    near_v = x_v + (src_v[z, down, :] + src_v[z, up, :])
    along_u = src_u[below, at, :] + src_u[above, at, :]
    along_v = src_v[below, at, :] + src_v[above, at, :]
    react = u * (v * v)
    new_u = (0.24 * near_u + 0.01 * along_u) + (f - u * (f - 0.02)) - react
    new_v = (0.12 * near_v + 0.005 * along_v) + decay[z, at, :] * v + react
    return new_u, new_v


def sweep(src, rates, rows, count, place, emit, unroll):
    def body(i, sums):
        z, below, above = place(i)
        ahead = x_sums(*src, place(jnp.minimum(i + 1, count - 1))[0], rows)
        values = [
            step_rows(*src, *rates, z, below, above, row, sums[n], sums[len(rows) + n])
            for n, row in enumerate(rows)
        ]
        emit(z, values)
        return ahead

    lax.fori_loop(0, count, body, x_sums(*src, place(0)[0], rows), unroll=unroll)


def to_planes(dst, rows):
    def emit(z, values):
        for row, new in zip(rows, values):
            for ref, value in zip(dst, new):
                ref[z, pl.ds(row, 8), :] = value

    return emit


def main_place(i):
    return i, jnp.maximum(i - 1, 0), jnp.minimum(i + 1, NZ - 1)


def strip_place(i):
    z = jnp.where(i < GZ, i + RIGHT, i - GZ + LEFT)
    return z, z - 1, z + 1


def strip_ends(refs, rows, group):
    for ref in refs:
        for plane in (RIGHT, LEFT):
            for row in rows:
                at = pl.ds(row, 8)
                first, last = ref[plane, at, :], ref[plane + GZ - 1, at, :]
                ref[plane - 1, at, :] = jnp.where(group == 0, first, turn(last, 16))
                ref[plane + GZ, at, :] = jnp.where(group == GROUPS - 1, last, turn(first, -16))


def merge_strips(src, dst, rows, inner):
    for old, new in zip(src, dst):
        for j in range(GZ):
            for row in rows:
                at = pl.ds(row, 8)
                new[j, at, :] = jnp.where(inner < 8, old[j + RIGHT, at, :], old[j + LEFT, at, :])


def with_edges(merged, z, row, value, edge):
    g = lax.div(z, GZ)
    piece = merged[z - g * GZ, pl.ds(row, 8), :]
    return jnp.where(edge, pltpu.roll(piece, NX - 8 - 16 * g, 1), value)


INNER_ROWS = (8, 16, 24, 32)
LAST_INNER_ROWS = (12, 20, 28)
BORDER_ROWS = (4, 36)
LAST_BORDER_ROWS = (8, 36)


def interior_kernel(
    u0, v0, feed, decay, x_b, x_a, su0_in, sv0_in, s_feed_in, s_decay_in,
    su0, sv0, s_feed, s_decay, u1, v1, u2, v2, u3, v3, su1, sv1, su2, sv2, su3, sv3, o_u, o_v,
    su4, sv4, mu, mv,
):
    even_x = is_even("gx")
    lane, inner, group = lanes()
    right_halo = (inner >= 8) & (inner < 12)
    left_halo = (inner >= 4) & (inner < 8)

    def halos(j, carry):
        for n, ref in enumerate((su0, sv0, s_feed, s_decay)):
            b, a = x_b[n, j], x_a[n, j]
            on_right, on_left = jnp.where(even_x, a, b), jnp.where(even_x, b, a)
            for t in range(4):
                at = pl.ds(OWN + 8 * t, 8)
                both = ref[j + RIGHT, at, :]
                ref[j + RIGHT, at, :] = jnp.where(right_halo, turn(on_right, 8 - 4 * t), both)
                ref[j + LEFT, at, :] = jnp.where(left_halo, turn(on_left, 4 - 4 * t), both)
        return carry

    lax.fori_loop(0, GZ, halos, 0, unroll=True)

    levels = [(su0, sv0), (su1, sv1), (su2, sv2), (su3, sv3), (su4, sv4)]
    for step in range(STEPS):
        rows = INNER_ROWS if step < STEPS - 1 else LAST_INNER_ROWS
        strip_ends(levels[step], INNER_ROWS, group)
        emit = to_planes(levels[step + 1], rows)
        sweep(levels[step], (s_feed, s_decay), rows, 2 * GZ, strip_place, emit, 7)
    merge_strips((su4, sv4), (mu, mv), LAST_INNER_ROWS, inner)

    levels = [(u0, v0), (u1, v1), (u2, v2), (u3, v3)]
    for step in range(STEPS - 1):
        emit = to_planes(levels[step + 1], INNER_ROWS)
        sweep(levels[step], (feed, decay), INNER_ROWS, NZ, main_place, emit, 8)
    edge = (lane < 4) | (lane >= 124)

    def finish(z, values):
        for row, new in zip(LAST_INNER_ROWS, values):
            for out, merged, value in zip((o_u, o_v), (mu, mv), new):
                out[z, pl.ds(row - OWN, 8), :] = with_edges(merged, z, row, value, edge)

    sweep(levels[-1], (feed, decay), LAST_INNER_ROWS, NZ, main_place, finish, 8)


def interior(u0, v0, feed, decay, x_b, x_a, su0, sv0, s_feed, s_decay):
    out = (vmem(*STRIP),) * 4 + (vmem(*FIELD),) * 6 + (vmem(*STRIP),) * 6 + (vmem(NZ, NY, NX),) * 2
    return pallas(
        interior_kernel,
        "interior",
        4,
        40_000_000,
        out_shape=out,
        input_output_aliases={6: 0, 7: 1, 8: 2, 9: 3},
        scratch_shapes=[vmem(*STRIP)] * 2 + [vmem(GZ, PY, NX)] * 2,
    )(u0, v0, feed, decay, x_b, x_a, su0, sv0, s_feed, s_decay)


N_STATE = 22


def border_kernel(*refs):
    y_b, y_a = refs[:2]
    state = refs[2 + N_STATE : 2 + 2 * N_STATE]
    out_u, out_v, su4, sv4, mu, mv, sems = refs[2 + 2 * N_STATE :]
    (u0, v0, feed, decay, su0, sv0, s_feed, s_decay) = state[:8]
    (u1, v1, u2, v2, u3, v3, su1, sv1, su2, sv2, su3, sv3, o_u, o_v) = state[8:]
    even_y = is_even("gy")
    lane, inner, group = lanes()
    start = (jnp.where(even_y, LOW, HIGH), jnp.where(even_y, HIGH, LOW))
    rate_start = (jnp.where(even_y, LOW + 1, HIGH), jnp.where(even_y, HIGH, LOW + 1))

    def rows(z, carry):
        for src, to, rate_to in zip((y_b, y_a), start, rate_start):
            at = z * MSG
            u0[z, pl.ds(to, 4), :] = src[pl.ds(at, 4), :]
            v0[z, pl.ds(to, 4), :] = src[pl.ds(at + 4, 4), :]
            feed[z, pl.ds(rate_to, 3), :] = src[pl.ds(at + 8, 3), :]
            decay[z, pl.ds(rate_to, 3), :] = src[pl.ds(at + 11, 3), :]
        return carry

    lax.fori_loop(0, NZ, rows, 0, unroll=4)

    right_halo = (inner >= 8) & (inner < 12)
    left_halo = (inner >= 4) & (inner < 8)

    def strip(j, carry):
        for y, to, rate_to in zip((y_b, y_a), start, rate_start):
            fields = rates = None
            for g in range(GROUPS):
                at = (GZ * g + j) * MSG
                one = turn(y[pl.ds(at, 8), :], 16 * g + 8)
                two = turn(y[pl.ds(at + 6, 8), :], 16 * g + 8)
                fields = one if g == 0 else jnp.where(group == g, one, fields)
                rates = two if g == 0 else jnp.where(group == g, two, rates)
            corner = y[pl.ds(CORNER + 8 * j, 8), :]
            other = turn(corner, 4, 0)
            for plane, mask, lane_at, top, bottom in (
                (j + RIGHT, right_halo, 8, corner, other),
                (j + LEFT, left_halo, 4, other, corner),
            ):
                su0[plane, pl.ds(to, 4), :] = jnp.where(mask, turn(top, lane_at), fields)[:4]
                sv0[plane, pl.ds(to, 4), :] = jnp.where(mask, turn(bottom, lane_at - 4), fields)[4:]
                s_feed[plane, pl.ds(rate_to, 3), :] = rates[2:5]
                s_decay[plane, pl.ds(rate_to, 3), :] = rates[5:]
                for n, ref in ((2, s_feed), (3, s_decay)):
                    halo = turn(top, lane_at - 4 * n)[:4]
                    at = pl.ds(to, 4)
                    ref[plane, at, :] = jnp.where(mask[:4], halo, ref[plane, at, :])
        return carry

    lax.fori_loop(0, GZ, strip, 0, unroll=True)

    levels = [(su0, sv0), (su1, sv1), (su2, sv2), (su3, sv3), (su4, sv4)]
    for step in range(STEPS):
        rows_now = BORDER_ROWS if step < STEPS - 1 else LAST_BORDER_ROWS
        strip_ends(levels[step], BORDER_ROWS, group)
        emit = to_planes(levels[step + 1], rows_now)
        sweep(levels[step], (s_feed, s_decay), rows_now, 2 * GZ, strip_place, emit, 14)
    merge_strips((su4, sv4), (mu, mv), LAST_BORDER_ROWS, inner)

    levels = [(u0, v0), (u1, v1), (u2, v2), (u3, v3)]
    for step in range(STEPS - 1):
        emit = to_planes(levels[step + 1], BORDER_ROWS)
        sweep(levels[step], (feed, decay), BORDER_ROWS, NZ, main_place, emit, 14)
    edge = (lane < 4) | (lane >= 124)

    def finish(z, values):
        for row, to, new in zip(LAST_BORDER_ROWS, (0, NY - 4), values):
            for out, merged, value in zip((o_u, o_v), (mu, mv), new):
                out[z, pl.ds(to, 4), :] = with_edges(merged, z, row, value, edge)[:4]

    copies = []
    part = NZ // 4
    for c in range(4):

        def place(i, c=c):
            return main_place(i + c * part)

        sweep(levels[-1], (feed, decay), LAST_BORDER_ROWS, part, place, finish, part)
        for n, (src, dst) in enumerate(((o_u, out_u), (o_v, out_v))):
            at = pl.ds(c * part, part)
            copies.append(pltpu.make_async_copy(src.at[at], dst.at[at], sems.at[2 * c + n]))
            copies[-1].start()
    for copy in copies:
        copy.wait()


def border(y_b, y_a, *state):
    out = tuple(vmem(*a.shape) for a in state) + (jax.ShapeDtypeStruct((NZ, NY, NX), jnp.float32),) * 2
    specs = [pl.BlockSpec(memory_space=pltpu.VMEM)] * N_STATE + [pl.BlockSpec(memory_space=pltpu.HBM)] * 2
    return pallas(
        border_kernel,
        "border",
        4,
        20_000_000,
        out_shape=out,
        out_specs=tuple(specs),
        input_output_aliases={2 + n: n for n in range(N_STATE)},
        scratch_shapes=[vmem(*STRIP)] * 2 + [vmem(GZ, PY, NX)] * 2 + [pltpu.SemaphoreType.DMA((8,))],
    )(y_b, y_a, *state)[N_STATE:]


def shards(activator, inhibitor, feed_rate, kill_rate):
    u0, v0, feed, decay, su0, sv0, s_feed, s_decay, x_send_b, x_send_a = load(
        activator, inhibitor, feed_rate, kill_rate
    )
    x_b = swap(x_send_b, "gx", 1)
    x_a = swap(x_send_a, "gx", 0)
    send_b, send_a = pack_y(u0, v0, feed, decay, x_b, x_a)
    y_b = swap(send_b, "gy", 1)
    y_a = swap(send_a, "gy", 0)
    made = interior(u0, v0, feed, decay, x_b, x_a, su0, sv0, s_feed, s_decay)
    return border(y_b, y_a, u0, v0, feed, decay, *made)


def solution(mesh):
    spec = P(None, "gy", "gx")
    return jax.shard_map(
        shards, mesh=mesh, in_specs=(spec,) * 4, out_specs=(spec,) * 2, check_vma=False
    )
```

time: 151 us -> 55 us (0.36)
  the two profiles are of different devices: /device:TPU:71 before, /device:TPU:6 now
where the time goes in v3:
time: 55 us; the launch traced here: 54.8 us
  Pallas kernels  22.4 us (41%)
  starting transfers between devices  21.8 us (40%)
  waiting for transfers between devices  9.93 us (18%)
  between operations  0.68 us (1%)
    ppermute x4, starting transfers between devices, swap(): return lax.ppermute(block, axis, swap_pairs(lax.axis_size(axis), parity))  21.8 us
    ppermute x4, waiting for transfers between devices, swap(): return lax.ppermute(block, axis, swap_pairs(lax.axis_size(axis), parity))  9.93 us
    pallas_call x1, Pallas kernels, interior(): pallas(interior_kernel, 'interior', 4, 40000000, out_shape=out, input_out...  8.76 us
    pallas_call x1, Pallas kernels, load(): pallas(load_kernel, 'load', 8, out_shape=(vmem(*FIELD),) * 4 + (vmem(*STR...  7.55 us
    pallas_call x1, Pallas kernels, border(): pallas(border_kernel, 'border', 4, 20000000, out_shape=out, out_specs=tup...  5.7 us
  transfers between devices with their start and end apart: 4, of which 2 were waited for; matrix products, arithmetic and copies ran while one was open for 0% of the time, Pallas kernels for 16%

profile of v3, /device:TPU:6, one launch (start us, length us, event | category | flops | bytes accessed | tf_op | source)
XLA Modules:
  0.0 54.8 jit_solution(13946225952669897916)
XLA Ops:
  0.6 7.6 %load.1 = (f32[56,48,128]{2,1,0:T(8,128)S(1)}, f32[56,48,128]{2,1,0:T(8,128)S(1)}, f32[56,48,128]{2,1,0:T(8,128)S(1)}, f32[56,48,128]{2,1,0:T(8,128)S(1)}, f32[1...) custom-call(f32[56,32,128]{2,1,0:T(8,128)} %u.1, ...), custom_call_target="tpu_custom_call" | custom-call | tf_op jit(solution)/shard_map/load/pallas_call | solution.py:122
  8.2 4.0 %collective-permute-start = (f32[4,7,8,128]{3,2,1,0:T(8,128)S(1)}, f32[4,7,8,128]{3,2,1,0:T(8,128)S(1)}, u32[]{:S(2)}, u32[]{:S(2)}) collective-permute-start(f32[4,7,8,128]{3,2,1,0:T(8,128)S(1)} %get-tuple-element.38), channel_id=1, source_target_pairs={{32,64},{64,32},{96,128},{128,96},{160,192},{192,160},{224,256},{2... | collective-permute-start | bytes 344072 | tf_op jit(solution)/shard_map/ppermute | solution.py:29
  12.2 2.3 %collective-permute-start.1 = (f32[4,7,8,128]{3,2,1,0:T(8,128)S(1)}, f32[4,7,8,128]{3,2,1,0:T(8,128)S(1)}, u32[]{:S(2)}, u32[]{:S(2)}) collective-permute-start(f32[4,7,8,128]{3,2,1,0:T(8,128)S(1)} %get-tuple-element.39), channel_id=1, source_target_pairs={{0,32},{32,0},{64,96},{96,64},{128,160},{160,128},{192,224},{224,1... | collective-permute-start | bytes 344072 | tf_op jit(solution)/shard_map/ppermute | solution.py:29
  14.5 1.6 %collective-permute-done.x_b = f32[4,7,8,128]{3,2,1,0:T(8,128)S(1)} collective-permute-done((f32[4,7,8,128]{3,2,1,0:T(8,128)S(1)}, f32[4,7,8,128]{3,2,1,0:T(8,128)S(1)}, u32[]{:S(2)}, u32[]{:S(2)}) %collective-permute-start) | collective-permute-done | bytes 114720 | tf_op jit(solution)/shard_map/ppermute | solution.py:29
  16.1 0.0 collective-permute-done.1.x_a
  16.1 0.4 pack_y.1
  16.5 13.5 %collective-permute-start.2 = (f32[840,128]{1,0:T(8,128)S(1)}, f32[840,128]{1,0:T(8,128)S(1)}, u32[]{:S(2)}, u32[]{:S(2)}) collective-permute-start(f32[840,128]{1,0:T(8,128)S(1)} %get-tuple-element.40), channel_id=1, source_target_pairs={{1,2},{2,1},{3,4},{4,3},{5,6},{6,5},{7,8},{8,7},{9,10},{10,9},{11,... | collective-permute-start | bytes 1290248 | tf_op jit(solution)/shard_map/ppermute | solution.py:29
  30.1 1.9 %collective-permute-start.3 = (f32[840,128]{1,0:T(8,128)S(1)}, f32[840,128]{1,0:T(8,128)S(1)}, u32[]{:S(2)}, u32[]{:S(2)}) collective-permute-start(f32[840,128]{1,0:T(8,128)S(1)} %get-tuple-element.41), channel_id=1, source_target_pairs={{0,1},{1,0},{2,3},{3,2},{4,5},{5,4},{6,7},{7,6},{8,9},{9,8},{10,11... | collective-permute-start | bytes 1290248 | tf_op jit(solution)/shard_map/ppermute | solution.py:29
  32.0 8.8 %interior.1 = (f32[18,48,128]{2,1,0:T(8,128)S(1)}, f32[18,48,128]{2,1,0:T(8,128)S(1)}, f32[18,48,128]{2,1,0:T(8,128)S(1)}, f32[18,48,128]{2,1,0:T(8,128)S(1)}, f...) custom-call(f32[56,48,128]{2,1,0:T(8,128)S(1)} %get-tuple-element.34, ...), custom_call_target="tpu_custom_call", output_to_operand_aliasing={{0}: (6, {}), {1}: (7, {}), {2}: (8, {}), {3}: (9, {})} | custom-call | flops 40000000 | bytes 10000000 | tf_op jit(solution)/shard_map/interior/pallas_call | solution.py:303
  40.8 8.3 %collective-permute-done.2.refs_0_ = f32[840,128]{1,0:T(8,128)S(1)} collective-permute-done((f32[840,128]{1,0:T(8,128)S(1)}, f32[840,128]{1,0:T(8,128)S(1)}, u32[]{:S(2)}, u32[]{:S(2)}) %collective-permute-start.2) | collective-permute-done | bytes 430112 | tf_op jit(solution)/shard_map/ppermute | solution.py:29
  49.1 0.0 collective-permute-done.3.refs_1_
  49.1 5.7 %border.1 = (f32[56,48,128]{2,1,0:T(8,128)S(1)}, f32[56,48,128]{2,1,0:T(8,128)S(1)}, f32[56,48,128]{2,1,0:T(8,128)S(1)}, f32[56,48,128]{2,1,0:T(8,128)S(1)}, f32...) custom-call(f32[840,128]{1,0:T(8,128)S(1)} %collective-permute-done., ...), custom_call_target="tpu_custom_call", output_to_operand_aliasing={{0}: (2, {}), {1}: (3, {}), {2}: (4, {}), {3}: (5, {}), {4}... | custom-call | flops 20000000 | bytes 5000000 | tf_op jit(solution)/shard_map/border/pallas_call | solution.py:407
Async XLA Ops:
  8.2 7.9 %collective-permute-start = (f32[4,7,8,128]{3,2,1,0:T(8,128)S(1)}, f32[4,7,8,128]{3,2,1,0:T(8,128)S(1)}, u32[]{:S(2)}, u32[]{:S(2)}) collective-permute-start(f32[4,7,8,128]{3,2,1,0:T(8,128)S(1)} %get-tuple-element.38), channel_id=1, source_target_pairs={{32,64},{64,32},{96,128},{128,96},{160,192},{192,160},{224,256},{2... | collective-permute-start | bytes 344072 | tf_op jit(solution)/shard_map/ppermute | solution.py:29
  12.2 3.9 %collective-permute-start.1 = (f32[4,7,8,128]{3,2,1,0:T(8,128)S(1)}, f32[4,7,8,128]{3,2,1,0:T(8,128)S(1)}, u32[]{:S(2)}, u32[]{:S(2)}) collective-permute-start(f32[4,7,8,128]{3,2,1,0:T(8,128)S(1)} %get-tuple-element.39), channel_id=1, source_target_pairs={{0,32},{32,0},{64,96},{96,64},{128,160},{160,128},{192,224},{224,1... | collective-permute-start | bytes 344072 | tf_op jit(solution)/shard_map/ppermute | solution.py:29
  16.5 32.6 %collective-permute-start.2 = (f32[840,128]{1,0:T(8,128)S(1)}, f32[840,128]{1,0:T(8,128)S(1)}, u32[]{:S(2)}, u32[]{:S(2)}) collective-permute-start(f32[840,128]{1,0:T(8,128)S(1)} %get-tuple-element.40), channel_id=1, source_target_pairs={{1,2},{2,1},{3,4},{4,3},{5,6},{6,5},{7,8},{8,7},{9,10},{10,9},{11,... | collective-permute-start | bytes 1290248 | tf_op jit(solution)/shard_map/ppermute | solution.py:29
  30.1 19.0 %collective-permute-start.3 = (f32[840,128]{1,0:T(8,128)S(1)}, f32[840,128]{1,0:T(8,128)S(1)}, u32[]{:S(2)}, u32[]{:S(2)}) collective-permute-start(f32[840,128]{1,0:T(8,128)S(1)} %get-tuple-element.41), channel_id=1, source_target_pairs={{0,1},{1,0},{2,3},{3,2},{4,5},{5,4},{6,7},{7,6},{8,9},{9,8},{10,11... | collective-permute-start | bytes 1290248 | tf_op jit(solution)/shard_map/ppermute | solution.py:29

commit v4 on v3

--- a/solution.py
+++ b/solution.py
@@ -10,9 +10,11 @@
 W = 4
 PY = 48
 OWN, LOW, HIGH = 8, 4, 40
-MSG = 4 * W - 2
 GROUPS, GZ = 8, NZ // 8
-CORNER = NZ * MSG
+FIELDS, RATES = 2 * W, 2 * (W - 1)
+CORNER = NZ * FIELDS
+TAIL = CORNER + 8 * GZ
+RATE_ROWS = NZ * RATES + 8
 RIGHT, LEFT = 1, GZ + 3
 SPLANES = 2 * GZ + 4
 
@@ -29,6 +31,38 @@
     return lax.ppermute(block, axis, swap_pairs(lax.axis_size(axis), parity))
 
 
+SPAN = 8
+
+
+def relay_pairs(count):
+    pairs = []
+    for i in range(count):
+        run, place = divmod(i, SPAN)
+        runs = count // SPAN
+        step = {0: -1, SPAN - 1: 1}.get(place, 0)
+        pairs.append((i, (run + step) % runs * SPAN + place))
+    return pairs
+
+
+def second_pairs(count):
+    pairs = []
+    for i in range(count):
+        run, place = divmod(i, SPAN)
+        other = (place + 1 if place % 2 else place - 1) % SPAN
+        pairs.append((i, run * SPAN + other))
+    return pairs
+
+
+def relay(block, axis):
+    count = lax.axis_size(axis)
+    return lax.ppermute(block, axis, relay_pairs(count)) if count % SPAN == 0 else block
+
+
+def after_relay(block, axis):
+    count = lax.axis_size(axis)
+    return lax.ppermute(block, axis, second_pairs(count) if count % SPAN == 0 else swap_pairs(count, 1))
+
+
 def is_even(axis):
     return lax.rem(lax.axis_index(axis), 2) == 0
 
@@ -50,7 +84,6 @@
 FIELD = (NZ, PY, NX)
 STRIP = (SPLANES, PY, NX)
 EDGE = (4, GZ, 8, NX)
-MESSAGE = (NZ * MSG + 8 * GZ, NX)
 
 
 def pallas(kernel, name, megabytes, flops=0, **kwargs):
@@ -88,31 +121,32 @@
     copies[1].wait()
     lax.fori_loop(0, NZ, rates, 0, unroll=4)
 
-    for n, src, dst in ((2, feed, s_feed), (3, decay, s_decay), (0, pu, su), (1, pv, sv)):
-        if n == 0:
-            copies[2].wait()
-        if n == 1:
-            copies[3].wait()
-
-        def body(j, carry, n=n, src=src, dst=dst):
-            left_edge = right_edge = None
-            for t in range(4):
-                at = pl.ds(OWN + 8 * t, 8)
-                both = None
-                for g in range(GROUPS):
-                    value = turn(src[GZ * g + j, at, :], 16 * g + 8)
-                    both = value if g == 0 else jnp.where(group == g, value, both)
-                dst[j + RIGHT, at, :] = both
-                dst[j + LEFT, at, :] = both
-                low, high = turn(both, 4 * t - 8), turn(both, 4 * t - 4)
-                here = (inner >= 4 * t) & (inner < 4 * t + 4)
-                left_edge = low if t == 0 else jnp.where(here, low, left_edge)
-                right_edge = high if t == 0 else jnp.where(here, high, right_edge)
-            out_b[n, j] = jnp.where(even, left_edge, right_edge)
-            out_a[n, j] = jnp.where(even, right_edge, left_edge)
+    def pack(arrays):
+        def body(j, carry):
+            for n, src, dst in arrays:
+                left_edge = right_edge = None
+                for t in range(4):
+                    at = pl.ds(OWN + 8 * t, 8)
+                    both = None
+                    for g in range(GROUPS):
+                        value = turn(src[GZ * g + j, at, :], 16 * g + 8)
+                        both = value if g == 0 else jnp.where(group == g, value, both)
+                    dst[j + RIGHT, at, :] = both
+                    dst[j + LEFT, at, :] = both
+                    low, high = turn(both, 4 * t - 8), turn(both, 4 * t - 4)
+                    here = (inner >= 4 * t) & (inner < 4 * t + 4)
+                    left_edge = low if t == 0 else jnp.where(here, low, left_edge)
+                    right_edge = high if t == 0 else jnp.where(here, high, right_edge)
+                out_b[n, j] = jnp.where(even, left_edge, right_edge)
+                out_a[n, j] = jnp.where(even, right_edge, left_edge)
             return carry
 
-        lax.fori_loop(0, GZ, body, 0, unroll=True)
+        lax.fori_loop(0, GZ, body, 0, unroll=2)
+
+    pack(((2, feed, s_feed), (3, decay, s_decay)))
+    copies[2].wait()
+    copies[3].wait()
+    pack(((0, pu, su), (1, pv, sv)))
 
 
 def load(u, v, f, k):
@@ -129,23 +163,39 @@
     )(u, v, f, k)
 
 
+def pack_rates_kernel(feed, decay, out):
+    start = jnp.where(is_even("gy"), OWN, OWN + 29)
+
+    def rows(z, carry):
+        out[pl.ds(RATES * z, 3), :] = feed[z, pl.ds(start, 3), :]
+        out[pl.ds(RATES * z + 3, 3), :] = decay[z, pl.ds(start, 3), :]
+        return carry
+
+    lax.fori_loop(0, NZ, rows, 0, unroll=8)
+    out[pl.ds(RATES * NZ, 8), :] = jnp.zeros((8, NX), jnp.float32)
+
+
+def pack_rates(feed, decay):
+    return pallas(pack_rates_kernel, "pack_rates", 4, out_shape=vmem(RATE_ROWS, NX))(feed, decay)
+
+
 def pack_y_kernel(u, v, feed, decay, x_b, x_a, out_b, out_a):
     even_x, even_y = is_even("gx"), is_even("gy")
     _, inner, _ = lanes()
     top = lax.broadcasted_iota(jnp.int32, (8, NX), 0) < 4
     starts = (jnp.where(even_y, OWN, OWN + 28), jnp.where(even_y, OWN + 28, OWN))
-    rate_starts = (jnp.where(even_y, OWN, OWN + 29), jnp.where(even_y, OWN + 29, OWN))
+    rate_start = jnp.where(even_y, OWN + 29, OWN)
 
     def rows(z, carry):
-        for out, start, rate_start in zip((out_b, out_a), starts, rate_starts):
-            at = z * MSG
-            out[pl.ds(at, 4), :] = u[z, pl.ds(start, 4), :]
-            out[pl.ds(at + 4, 4), :] = v[z, pl.ds(start, 4), :]
-            out[pl.ds(at + 8, 3), :] = feed[z, pl.ds(rate_start, 3), :]
-            out[pl.ds(at + 11, 3), :] = decay[z, pl.ds(rate_start, 3), :]
+        for out, start in zip((out_b, out_a), starts):
+            out[pl.ds(FIELDS * z, 4), :] = u[z, pl.ds(start, 4), :]
+            out[pl.ds(FIELDS * z + 4, 4), :] = v[z, pl.ds(start, 4), :]
+        out_a[pl.ds(TAIL + RATES * z, 3), :] = feed[z, pl.ds(rate_start, 3), :]
+        out_a[pl.ds(TAIL + RATES * z + 3, 3), :] = decay[z, pl.ds(rate_start, 3), :]
         return carry
 
     lax.fori_loop(0, NZ, rows, 0, unroll=4)
+    out_a[pl.ds(TAIL + RATES * NZ, 8), :] = jnp.zeros((8, NX), jnp.float32)
     for j in range(GZ):
         made = []
         for first, base in ((0, 0), (4, 12)):
@@ -166,7 +216,9 @@
 
 
 def pack_y(u, v, feed, decay, x_b, x_a):
-    return pallas(pack_y_kernel, "pack_y", 8, out_shape=(vmem(*MESSAGE),) * 2)(u, v, feed, decay, x_b, x_a)
+    return pallas(pack_y_kernel, "pack_y", 8, out_shape=(vmem(TAIL, NX), vmem(TAIL + RATE_ROWS, NX)))(
+        u, v, feed, decay, x_b, x_a
+    )
 
 
 def x_sums(src_u, src_v, z, rows):
@@ -281,13 +333,13 @@
         rows = INNER_ROWS if step < STEPS - 1 else LAST_INNER_ROWS
         strip_ends(levels[step], INNER_ROWS, group)
         emit = to_planes(levels[step + 1], rows)
-        sweep(levels[step], (s_feed, s_decay), rows, 2 * GZ, strip_place, emit, 7)
+        sweep(levels[step], (s_feed, s_decay), rows, 2 * GZ, strip_place, emit, 14)
     merge_strips((su4, sv4), (mu, mv), LAST_INNER_ROWS, inner)
 
     levels = [(u0, v0), (u1, v1), (u2, v2), (u3, v3)]
     for step in range(STEPS - 1):
         emit = to_planes(levels[step + 1], INNER_ROWS)
-        sweep(levels[step], (feed, decay), INNER_ROWS, NZ, main_place, emit, 8)
+        sweep(levels[step], (feed, decay), INNER_ROWS, NZ, main_place, emit, 14)
     edge = (lane < 4) | (lane >= 124)
 
     def finish(z, values):
@@ -295,7 +347,7 @@
             for out, merged, value in zip((o_u, o_v), (mu, mv), new):
                 out[z, pl.ds(row - OWN, 8), :] = with_edges(merged, z, row, value, edge)
 
-    sweep(levels[-1], (feed, decay), LAST_INNER_ROWS, NZ, main_place, finish, 8)
+    sweep(levels[-1], (feed, decay), LAST_INNER_ROWS, NZ, main_place, finish, 14)
 
 
 def interior(u0, v0, feed, decay, x_b, x_a, su0, sv0, s_feed, s_decay):
@@ -315,9 +367,9 @@
 
 
 def border_kernel(*refs):
-    y_b, y_a = refs[:2]
-    state = refs[2 + N_STATE : 2 + 2 * N_STATE]
-    out_u, out_v, su4, sv4, mu, mv, sems = refs[2 + 2 * N_STATE :]
+    y_b, r_b, y_a = refs[:3]
+    state = refs[3 + N_STATE : 3 + 2 * N_STATE]
+    out_u, out_v, su4, sv4, mu, mv, sems = refs[3 + 2 * N_STATE :]
     (u0, v0, feed, decay, su0, sv0, s_feed, s_decay) = state[:8]
     (u1, v1, u2, v2, u3, v3, su1, sv1, su2, sv2, su3, sv3, o_u, o_v) = state[8:]
     even_y = is_even("gy")
@@ -325,13 +377,14 @@
     start = (jnp.where(even_y, LOW, HIGH), jnp.where(even_y, HIGH, LOW))
     rate_start = (jnp.where(even_y, LOW + 1, HIGH), jnp.where(even_y, HIGH, LOW + 1))
 
+    sides = ((y_b, r_b, 0), (y_a, y_a, TAIL))
+
     def rows(z, carry):
-        for src, to, rate_to in zip((y_b, y_a), start, rate_start):
-            at = z * MSG
-            u0[z, pl.ds(to, 4), :] = src[pl.ds(at, 4), :]
-            v0[z, pl.ds(to, 4), :] = src[pl.ds(at + 4, 4), :]
-            feed[z, pl.ds(rate_to, 3), :] = src[pl.ds(at + 8, 3), :]
-            decay[z, pl.ds(rate_to, 3), :] = src[pl.ds(at + 11, 3), :]
+        for (src, rate_src, tail), to, rate_to in zip(sides, start, rate_start):
+            u0[z, pl.ds(to, 4), :] = src[pl.ds(FIELDS * z, 4), :]
+            v0[z, pl.ds(to, 4), :] = src[pl.ds(FIELDS * z + 4, 4), :]
+            feed[z, pl.ds(rate_to, 3), :] = rate_src[pl.ds(tail + RATES * z, 3), :]
+            decay[z, pl.ds(rate_to, 3), :] = rate_src[pl.ds(tail + RATES * z + 3, 3), :]
         return carry
 
     lax.fori_loop(0, NZ, rows, 0, unroll=4)
@@ -340,12 +393,12 @@
     left_halo = (inner >= 4) & (inner < 8)
 
     def strip(j, carry):
-        for y, to, rate_to in zip((y_b, y_a), start, rate_start):
+        for (y, rate_src, tail), to, rate_to in zip(sides, start, rate_start):
             fields = rates = None
             for g in range(GROUPS):
-                at = (GZ * g + j) * MSG
-                one = turn(y[pl.ds(at, 8), :], 16 * g + 8)
-                two = turn(y[pl.ds(at + 6, 8), :], 16 * g + 8)
+                z = GZ * g + j
+                one = turn(y[pl.ds(FIELDS * z, 8), :], 16 * g + 8)
+                two = turn(rate_src[pl.ds(tail + RATES * z, 8), :], 16 * g + 8)
                 fields = one if g == 0 else jnp.where(group == g, one, fields)
                 rates = two if g == 0 else jnp.where(group == g, two, rates)
             corner = y[pl.ds(CORNER + 8 * j, 8), :]
@@ -356,8 +409,8 @@
             ):
                 su0[plane, pl.ds(to, 4), :] = jnp.where(mask, turn(top, lane_at), fields)[:4]
                 sv0[plane, pl.ds(to, 4), :] = jnp.where(mask, turn(bottom, lane_at - 4), fields)[4:]
-                s_feed[plane, pl.ds(rate_to, 3), :] = rates[2:5]
-                s_decay[plane, pl.ds(rate_to, 3), :] = rates[5:]
+                s_feed[plane, pl.ds(rate_to, 3), :] = rates[:3]
+                s_decay[plane, pl.ds(rate_to, 3), :] = rates[3:6]
                 for n, ref in ((2, s_feed), (3, s_decay)):
                     halo = turn(top, lane_at - 4 * n)[:4]
                     at = pl.ds(to, 4)
@@ -377,7 +430,7 @@
     levels = [(u0, v0), (u1, v1), (u2, v2), (u3, v3)]
     for step in range(STEPS - 1):
         emit = to_planes(levels[step + 1], BORDER_ROWS)
-        sweep(levels[step], (feed, decay), BORDER_ROWS, NZ, main_place, emit, 14)
+        sweep(levels[step], (feed, decay), BORDER_ROWS, NZ, main_place, emit, 28)
     edge = (lane < 4) | (lane >= 124)
 
     def finish(z, values):
@@ -401,7 +454,7 @@
         copy.wait()
 
 
-def border(y_b, y_a, *state):
+def border(y_b, r_b, y_a, *state):
     out = tuple(vmem(*a.shape) for a in state) + (jax.ShapeDtypeStruct((NZ, NY, NX), jnp.float32),) * 2
     specs = [pl.BlockSpec(memory_space=pltpu.VMEM)] * N_STATE + [pl.BlockSpec(memory_space=pltpu.HBM)] * 2
     return pallas(
@@ -411,9 +464,9 @@
         20_000_000,
         out_shape=out,
         out_specs=tuple(specs),
-        input_output_aliases={2 + n: n for n in range(N_STATE)},
+        input_output_aliases={3 + n: n for n in range(N_STATE)},
         scratch_shapes=[vmem(*STRIP)] * 2 + [vmem(GZ, PY, NX)] * 2 + [pltpu.SemaphoreType.DMA((8,))],
-    )(y_b, y_a, *state)[N_STATE:]
+    )(y_b, r_b, y_a, *state)[N_STATE:]
 
 
 def shards(activator, inhibitor, feed_rate, kill_rate):
@@ -422,11 +475,16 @@
     )
     x_b = swap(x_send_b, "gx", 1)
     x_a = swap(x_send_a, "gx", 0)
+    rates = pack_rates(feed, decay)
+    half_way = relay(rates, "gy")
+    x_b, x_a, _ = lax.optimization_barrier((x_b, x_a, rates))
     send_b, send_a = pack_y(u0, v0, feed, decay, x_b, x_a)
     y_b = swap(send_b, "gy", 1)
+    send_a, half_way, x_b = lax.optimization_barrier((send_a, half_way, x_b))
     y_a = swap(send_a, "gy", 0)
+    r_b = after_relay(half_way, "gy")
     made = interior(u0, v0, feed, decay, x_b, x_a, su0, sv0, s_feed, s_decay)
-    return border(y_b, y_a, u0, v0, feed, decay, *made)
+    return border(y_b, r_b, y_a, u0, v0, feed, decay, *made)
 
 
 def solution(mesh):

time: 55 us -> 52.3 us (0.951); the launches traced: 54.8 us -> 51.3 us
  starting transfers between devices: 21.8 us -> 28.1 us
  Pallas kernels: 22.4 us -> 17.1 us
  waiting for transfers between devices: 9.93 us -> 5.29 us
    ppermute x0 -> x2, starting transfers between devices: none -> 12.9 us  [the longest x1 10.9 us: relay(): lax.ppermute(block, axis, relay_pairs(count))]
    ppermute x4, starting transfers between devices: 21.8 us -> 15.3 us  [swap(): return lax.ppermute(block, axis, swap_pairs(lax.axis_size(axis), parity))]
    ppermute x4, waiting for transfers between devices: 9.93 us -> 5.29 us  [swap(): return lax.ppermute(block, axis, swap_pairs(lax.axis_size(axis), parity))]
    pallas_call x1, Pallas kernels: 7.55 us -> 4.22 us  [load(): pallas(load_kernel, 'load', 8, out_shape=(vmem(*FIELD),) * 4 + (vmem(*STR...]
    pallas_call x1, Pallas kernels: 8.76 us -> 7.15 us  [interior(): pallas(interior_kernel, 'interior', 4, 40000000, out_shape=out, input_out...]
  transfers between devices with their start and end apart: 4 -> 6, of which waited for: 2 -> 2; matrix products, arithmetic and copies ran while one was open for 0% -> 0% of each run, Pallas kernels for 16% -> 15%
where the time goes in v4:
time: 52.3 us; the launch traced here: 51.3 us
  starting transfers between devices  28.1 us (54%)
  Pallas kernels  17.1 us (33%)
  waiting for transfers between devices  5.29 us (10%)
  between operations  0.72 us (1%)
    ppermute x4, starting transfers between devices, swap(): return lax.ppermute(block, axis, swap_pairs(lax.axis_size(axis), parity))  15.3 us
    ppermute x1, starting transfers between devices, relay(): lax.ppermute(block, axis, relay_pairs(count))  10.9 us
    pallas_call x1, Pallas kernels, interior(): pallas(interior_kernel, 'interior', 4, 40000000, out_shape=out, input_out...  7.15 us
    pallas_call x1, Pallas kernels, border(): pallas(border_kernel, 'border', 4, 20000000, out_shape=out, out_specs=tup...  5.34 us
    ppermute x4, waiting for transfers between devices, swap(): return lax.ppermute(block, axis, swap_pairs(lax.axis_size(axis), parity))  5.29 us
    pallas_call x1, Pallas kernels, load(): pallas(load_kernel, 'load', 8, out_shape=(vmem(*FIELD),) * 4 + (vmem(*STR...  4.22 us
    ppermute x1, starting transfers between devices, after_relay(): lax.ppermute(block, axis, second_pairs(count) if count % SPAN == 0 else s...  1.92 us
  transfers between devices with their start and end apart: 6, of which 2 were waited for; matrix products, arithmetic and copies ran while one was open for 0% of the time, Pallas kernels for 15%

profile of v4, /device:TPU:6, one launch (start us, length us, event | category | flops | bytes accessed | tf_op | source)
XLA Modules:
  0.0 51.3 jit_solution(16442611338089953419)
XLA Ops:
  0.6 4.2 %load.1 = (f32[56,48,128]{2,1,0:T(8,128)S(1)}, f32[56,48,128]{2,1,0:T(8,128)S(1)}, f32[56,48,128]{2,1,0:T(8,128)S(1)}, f32[56,48,128]{2,1,0:T(8,128)S(1)}, f32[1...) custom-call(f32[56,32,128]{2,1,0:T(8,128)} %u.1, ...), custom_call_target="tpu_custom_call" | custom-call | tf_op jit(solution)/shard_map/load/pallas_call | solution.py:156
  4.9 0.1 pack_rates.1
  5.0 10.9 %collective-permute-start.3 = (f32[344,128]{1,0:T(8,128)S(1)}, f32[344,128]{1,0:T(8,128)S(1)}, u32[]{:S(2)}, u32[]{:S(2)}) collective-permute-start(f32[344,128]{1,0:T(8,128)S(1)} %pack_rates.1), channel_id=1, source_target_pairs={{0,24},{1,1},{2,2},{3,3},{4,4},{5,5},{6,6},{7,15},{8,0},{9,9},{10,... | collective-permute-start | bytes 528392 | tf_op jit(solution)/shard_map/ppermute | solution.py:58
  15.9 2.8 %collective-permute-start = (f32[4,7,8,128]{3,2,1,0:T(8,128)S(1)}, f32[4,7,8,128]{3,2,1,0:T(8,128)S(1)}, u32[]{:S(2)}, u32[]{:S(2)}) collective-permute-start(f32[4,7,8,128]{3,2,1,0:T(8,128)S(1)} %get-tuple-element.43), channel_id=1, source_target_pairs={{32,64},{64,32},{96,128},{128,96},{160,192},{192,160},{224,256},{2... | collective-permute-start | bytes 344072 | tf_op jit(solution)/shard_map/ppermute | solution.py:31
  18.7 2.6 %collective-permute-start.1 = (f32[4,7,8,128]{3,2,1,0:T(8,128)S(1)}, f32[4,7,8,128]{3,2,1,0:T(8,128)S(1)}, u32[]{:S(2)}, u32[]{:S(2)}) collective-permute-start(f32[4,7,8,128]{3,2,1,0:T(8,128)S(1)} %get-tuple-element.44), channel_id=1, source_target_pairs={{0,32},{32,0},{64,96},{96,64},{128,160},{160,128},{192,224},{224,1... | collective-permute-start | bytes 344072 | tf_op jit(solution)/shard_map/ppermute | solution.py:31
  21.3 3.1 %collective-permute-done.x_b = f32[4,7,8,128]{3,2,1,0:T(8,128)S(1)} collective-permute-done((f32[4,7,8,128]{3,2,1,0:T(8,128)S(1)}, f32[4,7,8,128]{3,2,1,0:T(8,128)S(1)}, u32[]{:S(2)}, u32[]{:S(2)}) %collective-permute-start) | collective-permute-done | bytes 114720 | tf_op jit(solution)/shard_map/ppermute | solution.py:31
  24.4 0.0 collective-permute-done.1.x_a
  24.4 0.3 pack_y.1
  24.8 0.0 collective-permute-done.3
  24.8 1.9 %collective-permute-start.5 = (f32[848,128]{1,0:T(8,128)S(1)}, f32[848,128]{1,0:T(8,128)S(1)}, u32[]{:S(2)}, u32[]{:S(2)}) collective-permute-start(f32[848,128]{1,0:T(8,128)S(1)} %get-tuple-element.50), channel_id=1, source_target_pairs={{0,1},{1,0},{2,3},{3,2},{4,5},{5,4},{6,7},{7,6},{8,9},{9,8},{10,11... | collective-permute-start | bytes 1302536 | tf_op jit(solution)/shard_map/ppermute | solution.py:31
  26.7 7.9 %collective-permute-start.2 = (f32[504,128]{1,0:T(8,128)S(1)}, f32[504,128]{1,0:T(8,128)S(1)}, u32[]{:S(2)}, u32[]{:S(2)}) collective-permute-start(f32[504,128]{1,0:T(8,128)S(1)} %get-tuple-element.47), channel_id=1, source_target_pairs={{1,2},{2,1},{3,4},{4,3},{5,6},{6,5},{7,8},{8,7},{9,10},{10,9},{11,... | collective-permute-start | bytes 774152 | tf_op jit(solution)/shard_map/ppermute | solution.py:31
  34.6 1.9 %collective-permute-start.4 = (f32[344,128]{1,0:T(8,128)S(1)}, f32[344,128]{1,0:T(8,128)S(1)}, u32[]{:S(2)}, u32[]{:S(2)}) collective-permute-start(f32[344,128]{1,0:T(8,128)S(1)} %collective-permute-done.3), channel_id=1, source_target_pairs={{0,7},{1,2},{2,1},{3,4},{4,3},{5,6},{6,5},{7,0},{8,15},{9,10},{10,... | collective-permute-start | bytes 528392 | tf_op jit(solution)/shard_map/ppermute | solution.py:63
  36.6 7.2 %interior.1 = (f32[18,48,128]{2,1,0:T(8,128)S(1)}, f32[18,48,128]{2,1,0:T(8,128)S(1)}, f32[18,48,128]{2,1,0:T(8,128)S(1)}, f32[18,48,128]{2,1,0:T(8,128)S(1)}, f...) custom-call(f32[56,48,128]{2,1,0:T(8,128)S(1)} %get-tuple-element.39, ...), custom_call_target="tpu_custom_call", output_to_operand_aliasing={{0}: (6, {}), {1}: (7, {}), {2}: (8, {}), {3}: (9, {})} | custom-call | flops 40000000 | bytes 10000000 | tf_op jit(solution)/shard_map/interior/pallas_call | solution.py:355
  43.7 0.0 collective-permute-done.4.refs_1_
  43.7 2.2 %collective-permute-done.2.refs_0_ = f32[504,128]{1,0:T(8,128)S(1)} collective-permute-done((f32[504,128]{1,0:T(8,128)S(1)}, f32[504,128]{1,0:T(8,128)S(1)}, u32[]{:S(2)}, u32[]{:S(2)}) %collective-permute-start.2) | collective-permute-done | bytes 258080 | tf_op jit(solution)/shard_map/ppermute | solution.py:31
  45.9 0.0 collective-permute-done.5.refs_2_
  45.9 5.3 %border.1 = (f32[56,48,128]{2,1,0:T(8,128)S(1)}, f32[56,48,128]{2,1,0:T(8,128)S(1)}, f32[56,48,128]{2,1,0:T(8,128)S(1)}, f32[56,48,128]{2,1,0:T(8,128)S(1)}, f32...) custom-call(f32[504,128]{1,0:T(8,128)S(1)} %collective-permute-done., ...), custom_call_target="tpu_custom_call", output_to_operand_aliasing={{0}: (3, {}), {1}: (4, {}), {2}: (5, {}), {3}: (6, {}), {4}... | custom-call | flops 20000000 | bytes 5000000 | tf_op jit(solution)/shard_map/border/pallas_call | solution.py:460
Async XLA Ops:
  5.0 19.8 %collective-permute-start.3 = (f32[344,128]{1,0:T(8,128)S(1)}, f32[344,128]{1,0:T(8,128)S(1)}, u32[]{:S(2)}, u32[]{:S(2)}) collective-permute-start(f32[344,128]{1,0:T(8,128)S(1)} %pack_rates.1), channel_id=1, source_target_pairs={{0,24},{1,1},{2,2},{3,3},{4,4},{5,5},{6,6},{7,15},{8,0},{9,9},{10,... | collective-permute-start | bytes 528392 | tf_op jit(solution)/shard_map/ppermute | solution.py:58
  15.9 8.5 %collective-permute-start = (f32[4,7,8,128]{3,2,1,0:T(8,128)S(1)}, f32[4,7,8,128]{3,2,1,0:T(8,128)S(1)}, u32[]{:S(2)}, u32[]{:S(2)}) collective-permute-start(f32[4,7,8,128]{3,2,1,0:T(8,128)S(1)} %get-tuple-element.43), channel_id=1, source_target_pairs={{32,64},{64,32},{96,128},{128,96},{160,192},{192,160},{224,256},{2... | collective-permute-start | bytes 344072 | tf_op jit(solution)/shard_map/ppermute | solution.py:31
  18.7 5.7 %collective-permute-start.1 = (f32[4,7,8,128]{3,2,1,0:T(8,128)S(1)}, f32[4,7,8,128]{3,2,1,0:T(8,128)S(1)}, u32[]{:S(2)}, u32[]{:S(2)}) collective-permute-start(f32[4,7,8,128]{3,2,1,0:T(8,128)S(1)} %get-tuple-element.44), channel_id=1, source_target_pairs={{0,32},{32,0},{64,96},{96,64},{128,160},{160,128},{192,224},{224,1... | collective-permute-start | bytes 344072 | tf_op jit(solution)/shard_map/ppermute | solution.py:31
  24.8 21.1 %collective-permute-start.5 = (f32[848,128]{1,0:T(8,128)S(1)}, f32[848,128]{1,0:T(8,128)S(1)}, u32[]{:S(2)}, u32[]{:S(2)}) collective-permute-start(f32[848,128]{1,0:T(8,128)S(1)} %get-tuple-element.50), channel_id=1, source_target_pairs={{0,1},{1,0},{2,3},{3,2},{4,5},{5,4},{6,7},{7,6},{8,9},{9,8},{10,11... | collective-permute-start | bytes 1302536 | tf_op jit(solution)/shard_map/ppermute | solution.py:31
  26.7 19.2 %collective-permute-start.2 = (f32[504,128]{1,0:T(8,128)S(1)}, f32[504,128]{1,0:T(8,128)S(1)}, u32[]{:S(2)}, u32[]{:S(2)}) collective-permute-start(f32[504,128]{1,0:T(8,128)S(1)} %get-tuple-element.47), channel_id=1, source_target_pairs={{1,2},{2,1},{3,4},{4,3},{5,6},{6,5},{7,8},{8,7},{9,10},{10,9},{11,... | collective-permute-start | bytes 774152 | tf_op jit(solution)/shard_map/ppermute | solution.py:31
  34.6 9.1 %collective-permute-start.4 = (f32[344,128]{1,0:T(8,128)S(1)}, f32[344,128]{1,0:T(8,128)S(1)}, u32[]{:S(2)}, u32[]{:S(2)}) collective-permute-start(f32[344,128]{1,0:T(8,128)S(1)} %collective-permute-done.3), channel_id=1, source_target_pairs={{0,7},{1,2},{2,1},{3,4},{4,3},{5,6},{6,5},{7,0},{8,15},{9,10},{10,... | collective-permute-start | bytes 528392 | tf_op jit(solution)/shard_map/ppermute | solution.py:63

commit v5 on v4

--- a/solution.py
+++ b/solution.py
@@ -1,3 +1,5 @@
+import functools
+
 import jax
 import jax.numpy as jnp
 from jax import lax
@@ -179,24 +181,26 @@
     return pallas(pack_rates_kernel, "pack_rates", 4, out_shape=vmem(RATE_ROWS, NX))(feed, decay)
 
 
-def pack_y_kernel(u, v, feed, decay, x_b, x_a, out_b, out_a):
-    even_x, even_y = is_even("gx"), is_even("gy")
-    _, inner, _ = lanes()
+def pack_y_kernel(which, u, v, feed, decay, x_b, x_a, _, out):
+    even_x = is_even("gx")
+    to_low = is_even("gy") if which else jnp.logical_not(is_even("gy"))
+    inner = lanes()[1]
     top = lax.broadcasted_iota(jnp.int32, (8, NX), 0) < 4
-    starts = (jnp.where(even_y, OWN, OWN + 28), jnp.where(even_y, OWN + 28, OWN))
-    rate_start = jnp.where(even_y, OWN + 29, OWN)
+    start, rate_start = jnp.where(to_low, OWN, OWN + 28), jnp.where(to_low, OWN, OWN + 29)
 
     def rows(z, carry):
-        for out, start in zip((out_b, out_a), starts):
-            out[pl.ds(FIELDS * z, 4), :] = u[z, pl.ds(start, 4), :]
-            out[pl.ds(FIELDS * z + 4, 4), :] = v[z, pl.ds(start, 4), :]
-        out_a[pl.ds(TAIL + RATES * z, 3), :] = feed[z, pl.ds(rate_start, 3), :]
-        out_a[pl.ds(TAIL + RATES * z + 3, 3), :] = decay[z, pl.ds(rate_start, 3), :]
-        return carry
-
-    lax.fori_loop(0, NZ, rows, 0, unroll=4)
-    out_a[pl.ds(TAIL + RATES * NZ, 8), :] = jnp.zeros((8, NX), jnp.float32)
-    for j in range(GZ):
+        out[pl.ds(FIELDS * z, 4), :] = u[z, pl.ds(start, 4), :]
+        out[pl.ds(FIELDS * z + 4, 4), :] = v[z, pl.ds(start, 4), :]
+        if not which:
+            out[pl.ds(TAIL + RATES * z, 3), :] = feed[z, pl.ds(rate_start, 3), :]
+            out[pl.ds(TAIL + RATES * z + 3, 3), :] = decay[z, pl.ds(rate_start, 3), :]
+        return carry
+
+    lax.fori_loop(0, NZ, rows, 0, unroll=8)
+    if not which:
+        out[pl.ds(TAIL + RATES * NZ, 8), :] = jnp.zeros((8, NX), jnp.float32)
+
+    def corner(j, carry):
         made = []
         for first, base in ((0, 0), (4, 12)):
             sides = []
@@ -210,15 +214,20 @@
                     value = halo if n == 0 else jnp.where(here, halo, value)
                 sides.append(turn(value, (0 if is_right else 4) - first, 0))
             made.append(jnp.where(top, sides[0], sides[1]))
-        at = pl.ds(CORNER + 8 * j, 8)
-        out_b[at, :] = jnp.where(even_y, made[0], made[1])
-        out_a[at, :] = jnp.where(even_y, made[1], made[0])
-
-
-def pack_y(u, v, feed, decay, x_b, x_a):
-    return pallas(pack_y_kernel, "pack_y", 8, out_shape=(vmem(TAIL, NX), vmem(TAIL + RATE_ROWS, NX)))(
-        u, v, feed, decay, x_b, x_a
-    )
+        out[pl.ds(CORNER + 8 * j, 8), :] = jnp.where(to_low, made[0], made[1])
+        return carry
+
+    lax.fori_loop(0, GZ, corner, 0, unroll=True)
+
+
+def pack_y(which, u, v, feed, decay, x_b, x_a, after):
+    return pallas(
+        functools.partial(pack_y_kernel, which),
+        "pack_odd" if which else "pack_even",
+        8,
+        out_shape=vmem(TAIL + (0 if which else RATE_ROWS), NX),
+        in_specs=[pl.BlockSpec(memory_space=pltpu.VMEM)] * 6 + [pl.BlockSpec(memory_space=pl.ANY)],
+    )(u, v, feed, decay, x_b, x_a, after)
 
 
 def x_sums(src_u, src_v, z, rows):
@@ -356,7 +365,7 @@
         interior_kernel,
         "interior",
         4,
-        40_000_000,
+        40_000_000_000,
         out_shape=out,
         input_output_aliases={6: 0, 7: 1, 8: 2, 9: 3},
         scratch_shapes=[vmem(*STRIP)] * 2 + [vmem(GZ, PY, NX)] * 2,
@@ -475,13 +484,13 @@
     )
     x_b = swap(x_send_b, "gx", 1)
     x_a = swap(x_send_a, "gx", 0)
-    rates = pack_rates(feed, decay)
+    rates, x_b, x_a = lax.optimization_barrier((pack_rates(feed, decay), x_b, x_a))
     half_way = relay(rates, "gy")
-    x_b, x_a, _ = lax.optimization_barrier((x_b, x_a, rates))
-    send_b, send_a = pack_y(u0, v0, feed, decay, x_b, x_a)
+    send_b = pack_y(1, u0, v0, feed, decay, x_b, x_a, rates)
     y_b = swap(send_b, "gy", 1)
-    send_a, half_way, x_b = lax.optimization_barrier((send_a, half_way, x_b))
+    send_a = pack_y(0, u0, v0, feed, decay, x_b, x_a, send_b)
     y_a = swap(send_a, "gy", 0)
+    half_way, x_b, _ = lax.optimization_barrier((half_way, x_b, send_a))
     r_b = after_relay(half_way, "gy")
     made = interior(u0, v0, feed, decay, x_b, x_a, su0, sv0, s_feed, s_decay)
     return border(y_b, r_b, y_a, u0, v0, feed, decay, *made)

time: 52.3 us -> 50.3 us (0.962)
  the two profiles are of different devices: /device:TPU:6 before, /device:TPU:1 now
where the time goes in v5:
time: 50.3 us; the launch traced here: 50 us
  starting transfers between devices  31 us (62%)
  Pallas kernels  17.4 us (35%)
  waiting for transfers between devices  0.85 us (2%)
  between operations  0.75 us (1%)
    ppermute x4, starting transfers between devices, swap(): return lax.ppermute(block, axis, swap_pairs(lax.axis_size(axis), parity))  17.5 us
    ppermute x1, starting transfers between devices, relay(): lax.ppermute(block, axis, relay_pairs(count))  8.37 us
    pallas_call x1, Pallas kernels, interior(): pallas(interior_kernel, 'interior', 4, 40000000000, out_shape=out, input_...  7.15 us
    pallas_call x1, Pallas kernels, border(): pallas(border_kernel, 'border', 4, 20000000, out_shape=out, out_specs=tup...  5.4 us
    ppermute x1, starting transfers between devices, after_relay(): lax.ppermute(block, axis, second_pairs(count) if count % SPAN == 0 else s...  5.22 us
    pallas_call x1, Pallas kernels, load(): pallas(load_kernel, 'load', 8, out_shape=(vmem(*FIELD),) * 4 + (vmem(*STR...  4.22 us
  transfers between devices with their start and end apart: 6, of which 1 were waited for; matrix products, arithmetic and copies ran while one was open for 0% of the time, Pallas kernels for 16%

profile of v5, /device:TPU:1, one launch (start us, length us, event | category | flops | bytes accessed | tf_op | source)
XLA Modules:
  0.0 50.0 jit_solution(9910327587473947373)
XLA Ops:
  0.6 4.2 %load.1 = (f32[56,48,128]{2,1,0:T(8,128)S(1)}, f32[56,48,128]{2,1,0:T(8,128)S(1)}, f32[56,48,128]{2,1,0:T(8,128)S(1)}, f32[56,48,128]{2,1,0:T(8,128)S(1)}, f32[1...) custom-call(f32[56,32,128]{2,1,0:T(8,128)} %u.1, ...), custom_call_target="tpu_custom_call" | custom-call | tf_op jit(solution)/shard_map/load/pallas_call | solution.py:158
  4.9 5.4 %collective-permute-start = (f32[4,7,8,128]{3,2,1,0:T(8,128)S(1)}, f32[4,7,8,128]{3,2,1,0:T(8,128)S(1)}, u32[]{:S(2)}, u32[]{:S(2)}) collective-permute-start(f32[4,7,8,128]{3,2,1,0:T(8,128)S(1)} %get-tuple-element.41), channel_id=1, source_target_pairs={{32,64},{64,32},{96,128},{128,96},{160,192},{192,160},{224,256},{2... | collective-permute-start | bytes 344072 | tf_op jit(solution)/shard_map/ppermute | solution.py:33
  10.3 5.3 %collective-permute-start.1 = (f32[4,7,8,128]{3,2,1,0:T(8,128)S(1)}, f32[4,7,8,128]{3,2,1,0:T(8,128)S(1)}, u32[]{:S(2)}, u32[]{:S(2)}) collective-permute-start(f32[4,7,8,128]{3,2,1,0:T(8,128)S(1)} %get-tuple-element.42), channel_id=1, source_target_pairs={{0,32},{32,0},{64,96},{96,64},{128,160},{160,128},{192,224},{224,1... | collective-permute-start | bytes 344072 | tf_op jit(solution)/shard_map/ppermute | solution.py:33
  15.6 0.1 pack_rates.1._
  15.7 0.0 collective-permute-done.x_b
  15.7 0.8 %collective-permute-done.1.x_a = f32[4,7,8,128]{3,2,1,0:T(8,128)S(1)} collective-permute-done((f32[4,7,8,128]{3,2,1,0:T(8,128)S(1)}, f32[4,7,8,128]{3,2,1,0:T(8,128)S(1)}, u32[]{:S(2)}, u32[]{:S(2)}) %collective-permute-start.1) | collective-permute-done | bytes 114720 | tf_op jit(solution)/shard_map/ppermute | solution.py:33
  16.5 8.4 %collective-permute-start.3 = (f32[344,128]{1,0:T(8,128)S(1)}, f32[344,128]{1,0:T(8,128)S(1)}, u32[]{:S(2)}, u32[]{:S(2)}) collective-permute-start(f32[344,128]{1,0:T(8,128)S(1)} %pack_rates.1._), channel_id=1, source_target_pairs={{0,24},{1,1},{2,2},{3,3},{4,4},{5,5},{6,6},{7,15},{8,0},{9,9},{10,... | collective-permute-start | bytes 528392 | tf_op jit(solution)/shard_map/ppermute | solution.py:60
  24.9 0.3 pack_odd.1._
  25.2 4.8 %collective-permute-start.2 = (f32[504,128]{1,0:T(8,128)S(1)}, f32[504,128]{1,0:T(8,128)S(1)}, u32[]{:S(2)}, u32[]{:S(2)}) collective-permute-start(f32[504,128]{1,0:T(8,128)S(1)} %pack_odd.1._), channel_id=1, source_target_pairs={{1,2},{2,1},{3,4},{4,3},{5,6},{6,5},{7,8},{8,7},{9,10},{10,9},{11,... | collective-permute-start | bytes 774152 | tf_op jit(solution)/shard_map/ppermute | solution.py:33
  30.0 0.3 pack_even.1
  30.3 1.9 %collective-permute-start.5 = (f32[848,128]{1,0:T(8,128)S(1)}, f32[848,128]{1,0:T(8,128)S(1)}, u32[]{:S(2)}, u32[]{:S(2)}) collective-permute-start(f32[848,128]{1,0:T(8,128)S(1)} %pack_even.1), channel_id=1, source_target_pairs={{0,1},{1,0},{2,3},{3,2},{4,5},{5,4},{6,7},{7,6},{8,9},{9,8},{10,11... | collective-permute-start | bytes 1302536 | tf_op jit(solution)/shard_map/ppermute | solution.py:33
  32.2 0.0 collective-permute-done.3
  32.2 5.2 %collective-permute-start.4 = (f32[344,128]{1,0:T(8,128)S(1)}, f32[344,128]{1,0:T(8,128)S(1)}, u32[]{:S(2)}, u32[]{:S(2)}) collective-permute-start(f32[344,128]{1,0:T(8,128)S(1)} %collective-permute-done.3), channel_id=1, source_target_pairs={{0,7},{1,2},{2,1},{3,4},{4,3},{5,6},{6,5},{7,0},{8,15},{9,10},{10,... | collective-permute-start | bytes 528392 | tf_op jit(solution)/shard_map/ppermute | solution.py:65
  37.5 7.2 %interior.1 = (f32[18,48,128]{2,1,0:T(8,128)S(1)}, f32[18,48,128]{2,1,0:T(8,128)S(1)}, f32[18,48,128]{2,1,0:T(8,128)S(1)}, f32[18,48,128]{2,1,0:T(8,128)S(1)}, f...) custom-call(f32[56,48,128]{2,1,0:T(8,128)S(1)} %get-tuple-element.37, ...), custom_call_target="tpu_custom_call", output_to_operand_aliasing={{0}: (6, {}), {1}: (7, {}), {2}: (8, {}), {3}: (9, {})} | custom-call | flops 40000000000 | bytes 10000000000 | tf_op jit(solution)/shard_map/interior/pallas_call | solution.py:364
  44.6 0.0 collective-permute-done.2.refs_0_
  44.6 0.0 collective-permute-done.4.refs_1_
  44.6 0.0 collective-permute-done.5.refs_2_
  44.6 5.4 %border.1 = (f32[56,48,128]{2,1,0:T(8,128)S(1)}, f32[56,48,128]{2,1,0:T(8,128)S(1)}, f32[56,48,128]{2,1,0:T(8,128)S(1)}, f32[56,48,128]{2,1,0:T(8,128)S(1)}, f32...) custom-call(f32[504,128]{1,0:T(8,128)S(1)} %collective-permute-done., ...), custom_call_target="tpu_custom_call", output_to_operand_aliasing={{0}: (3, {}), {1}: (4, {}), {2}: (5, {}), {3}: (6, {}), {4}... | custom-call | flops 20000000 | bytes 5000000 | tf_op jit(solution)/shard_map/border/pallas_call | solution.py:469
Async XLA Ops:
  4.9 10.8 %collective-permute-start = (f32[4,7,8,128]{3,2,1,0:T(8,128)S(1)}, f32[4,7,8,128]{3,2,1,0:T(8,128)S(1)}, u32[]{:S(2)}, u32[]{:S(2)}) collective-permute-start(f32[4,7,8,128]{3,2,1,0:T(8,128)S(1)} %get-tuple-element.41), channel_id=1, source_target_pairs={{32,64},{64,32},{96,128},{128,96},{160,192},{192,160},{224,256},{2... | collective-permute-start | bytes 344072 | tf_op jit(solution)/shard_map/ppermute | solution.py:33
  10.3 6.3 %collective-permute-start.1 = (f32[4,7,8,128]{3,2,1,0:T(8,128)S(1)}, f32[4,7,8,128]{3,2,1,0:T(8,128)S(1)}, u32[]{:S(2)}, u32[]{:S(2)}) collective-permute-start(f32[4,7,8,128]{3,2,1,0:T(8,128)S(1)} %get-tuple-element.42), channel_id=1, source_target_pairs={{0,32},{32,0},{64,96},{96,64},{128,160},{160,128},{192,224},{224,1... | collective-permute-start | bytes 344072 | tf_op jit(solution)/shard_map/ppermute | solution.py:33
  16.5 15.7 %collective-permute-start.3 = (f32[344,128]{1,0:T(8,128)S(1)}, f32[344,128]{1,0:T(8,128)S(1)}, u32[]{:S(2)}, u32[]{:S(2)}) collective-permute-start(f32[344,128]{1,0:T(8,128)S(1)} %pack_rates.1._), channel_id=1, source_target_pairs={{0,24},{1,1},{2,2},{3,3},{4,4},{5,5},{6,6},{7,15},{8,0},{9,9},{10,... | collective-permute-start | bytes 528392 | tf_op jit(solution)/shard_map/ppermute | solution.py:60
  25.2 19.5 %collective-permute-start.2 = (f32[504,128]{1,0:T(8,128)S(1)}, f32[504,128]{1,0:T(8,128)S(1)}, u32[]{:S(2)}, u32[]{:S(2)}) collective-permute-start(f32[504,128]{1,0:T(8,128)S(1)} %pack_odd.1._), channel_id=1, source_target_pairs={{1,2},{2,1},{3,4},{4,3},{5,6},{6,5},{7,8},{8,7},{9,10},{10,9},{11,... | collective-permute-start | bytes 774152 | tf_op jit(solution)/shard_map/ppermute | solution.py:33
  30.3 14.3 %collective-permute-start.5 = (f32[848,128]{1,0:T(8,128)S(1)}, f32[848,128]{1,0:T(8,128)S(1)}, u32[]{:S(2)}, u32[]{:S(2)}) collective-permute-start(f32[848,128]{1,0:T(8,128)S(1)} %pack_even.1), channel_id=1, source_target_pairs={{0,1},{1,0},{2,3},{3,2},{4,5},{5,4},{6,7},{7,6},{8,9},{9,8},{10,11... | collective-permute-start | bytes 1302536 | tf_op jit(solution)/shard_map/ppermute | solution.py:33
  32.2 12.4 %collective-permute-start.4 = (f32[344,128]{1,0:T(8,128)S(1)}, f32[344,128]{1,0:T(8,128)S(1)}, u32[]{:S(2)}, u32[]{:S(2)}) collective-permute-start(f32[344,128]{1,0:T(8,128)S(1)} %collective-permute-done.3), channel_id=1, source_target_pairs={{0,7},{1,2},{2,1},{3,4},{4,3},{5,6},{6,5},{7,0},{8,15},{9,10},{10,... | collective-permute-start | bytes 528392 | tf_op jit(solution)/shard_map/ppermute | solution.py:65

commit v6 on v5

--- a/solution.py
+++ b/solution.py
@@ -314,11 +314,14 @@
 LAST_BORDER_ROWS = (8, 36)
 
 
-def interior_kernel(
+EARLY_STEPS = 2
+
+
+def early_kernel(
     u0, v0, feed, decay, x_b, x_a, su0_in, sv0_in, s_feed_in, s_decay_in,
-    su0, sv0, s_feed, s_decay, u1, v1, u2, v2, u3, v3, su1, sv1, su2, sv2, su3, sv3, o_u, o_v,
-    su4, sv4, mu, mv,
+    su0, sv0, s_feed, s_decay, su1, sv1, su2, sv2, su3, sv3, mu, mv, *fields_and_scratch,
 ):
+    *fields, su4, sv4 = fields_and_scratch
     even_x = is_even("gx")
     lane, inner, group = lanes()
     right_halo = (inner >= 8) & (inner < 12)
@@ -345,8 +348,30 @@
         sweep(levels[step], (s_feed, s_decay), rows, 2 * GZ, strip_place, emit, 14)
     merge_strips((su4, sv4), (mu, mv), LAST_INNER_ROWS, inner)
 
-    levels = [(u0, v0), (u1, v1), (u2, v2), (u3, v3)]
-    for step in range(STEPS - 1):
+    levels = [(u0, v0)] + list(zip(fields[::2], fields[1::2]))
+    for step in range(EARLY_STEPS):
+        emit = to_planes(levels[step + 1], INNER_ROWS)
+        sweep(levels[step], (feed, decay), INNER_ROWS, NZ, main_place, emit, 14)
+
+
+def early(u0, v0, feed, decay, x_b, x_a, su0, sv0, s_feed, s_decay):
+    out = (vmem(*STRIP),) * 10 + (vmem(GZ, PY, NX),) * 2 + (vmem(*FIELD),) * (2 * EARLY_STEPS)
+    return pallas(
+        early_kernel,
+        "early",
+        4,
+        20_000_000_000,
+        out_shape=out,
+        input_output_aliases={6: 0, 7: 1, 8: 2, 9: 3},
+        scratch_shapes=[vmem(*STRIP)] * 2,
+    )(u0, v0, feed, decay, x_b, x_a, su0, sv0, s_feed, s_decay)
+
+
+def late_kernel(feed, decay, mu, mv, first_u, first_v, *outs):
+    lane = lanes()[0]
+    *fields, o_u, o_v = outs
+    levels = [(first_u, first_v)] + list(zip(fields[::2], fields[1::2]))
+    for step in range(STEPS - 1 - EARLY_STEPS):
         emit = to_planes(levels[step + 1], INNER_ROWS)
         sweep(levels[step], (feed, decay), INNER_ROWS, NZ, main_place, emit, 14)
     edge = (lane < 4) | (lane >= 124)
@@ -359,17 +384,9 @@
     sweep(levels[-1], (feed, decay), LAST_INNER_ROWS, NZ, main_place, finish, 14)
 
 
-def interior(u0, v0, feed, decay, x_b, x_a, su0, sv0, s_feed, s_decay):
-    out = (vmem(*STRIP),) * 4 + (vmem(*FIELD),) * 6 + (vmem(*STRIP),) * 6 + (vmem(NZ, NY, NX),) * 2
-    return pallas(
-        interior_kernel,
-        "interior",
-        4,
-        40_000_000_000,
-        out_shape=out,
-        input_output_aliases={6: 0, 7: 1, 8: 2, 9: 3},
-        scratch_shapes=[vmem(*STRIP)] * 2 + [vmem(GZ, PY, NX)] * 2,
-    )(u0, v0, feed, decay, x_b, x_a, su0, sv0, s_feed, s_decay)
+def late(feed, decay, mu, mv, first_u, first_v):
+    out = (vmem(*FIELD),) * (2 * (STEPS - 1 - EARLY_STEPS)) + (vmem(NZ, NY, NX),) * 2
+    return pallas(late_kernel, "late", 4, 20_000_000_000, out_shape=out)(feed, decay, mu, mv, first_u, first_v)
 
 
 N_STATE = 22
@@ -380,7 +397,7 @@
     state = refs[3 + N_STATE : 3 + 2 * N_STATE]
     out_u, out_v, su4, sv4, mu, mv, sems = refs[3 + 2 * N_STATE :]
     (u0, v0, feed, decay, su0, sv0, s_feed, s_decay) = state[:8]
-    (u1, v1, u2, v2, u3, v3, su1, sv1, su2, sv2, su3, sv3, o_u, o_v) = state[8:]
+    (su1, sv1, su2, sv2, su3, sv3, u1, v1, u2, v2, u3, v3, o_u, o_v) = state[8:]
     even_y = is_even("gy")
     lane, inner, group = lanes()
     start = (jnp.where(even_y, LOW, HIGH), jnp.where(even_y, HIGH, LOW))
@@ -490,10 +507,13 @@
     y_b = swap(send_b, "gy", 1)
     send_a = pack_y(0, u0, v0, feed, decay, x_b, x_a, send_b)
     y_a = swap(send_a, "gy", 0)
-    half_way, x_b, _ = lax.optimization_barrier((half_way, x_b, send_a))
+    x_b, _ = lax.optimization_barrier((x_b, send_a))
+    made = early(u0, v0, feed, decay, x_b, x_a, su0, sv0, s_feed, s_decay)
+    strips, (mu, mv), fields = made[:10], made[10:12], made[12:]
+    half_way, mu = lax.optimization_barrier((half_way, mu))
     r_b = after_relay(half_way, "gy")
-    made = interior(u0, v0, feed, decay, x_b, x_a, su0, sv0, s_feed, s_decay)
-    return border(y_b, r_b, y_a, u0, v0, feed, decay, *made)
+    rest = late(feed, decay, mu, mv, *fields[-2:])
+    return border(y_b, r_b, y_a, u0, v0, feed, decay, *strips, *fields, *rest)
 
 
 def solution(mesh):

time: 50.3 us -> 50.3 us (level)
  the two profiles are of different devices: /device:TPU:1 before, /device:TPU:6 now
where the time goes in v6:
time: 50.3 us; the launch traced here: 49.5 us
  starting transfers between devices  25.6 us (51%)
  Pallas kernels  17.5 us (35%)
  waiting for transfers between devices  5.64 us (11%)
  between operations  0.73 us (1%)
    ppermute x4, starting transfers between devices, swap(): return lax.ppermute(block, axis, swap_pairs(lax.axis_size(axis), parity))  13.1 us
    ppermute x1, starting transfers between devices, relay(): lax.ppermute(block, axis, relay_pairs(count))  10.6 us
    pallas_call x1, Pallas kernels, border(): pallas(border_kernel, 'border', 4, 20000000, out_shape=out, out_specs=tup...  5.42 us
    ppermute x4, waiting for transfers between devices, swap(): return lax.ppermute(block, axis, swap_pairs(lax.axis_size(axis), parity))  4.75 us
    pallas_call x1, Pallas kernels, early(): pallas(early_kernel, 'early', 4, 20000000000, out_shape=out, input_output...  4.39 us
    pallas_call x1, Pallas kernels, load(): pallas(load_kernel, 'load', 8, out_shape=(vmem(*FIELD),) * 4 + (vmem(*STR...  4.22 us
    pallas_call x1, Pallas kernels, late(): pallas(late_kernel, 'late', 4, 20000000000, out_shape=out)  2.88 us
    ppermute x1, starting transfers between devices, after_relay(): lax.ppermute(block, axis, second_pairs(count) if count % SPAN == 0 else s...  1.92 us
  transfers between devices with their start and end apart: 6, of which 3 were waited for; matrix products, arithmetic and copies ran while one was open for 0% of the time, Pallas kernels for 16%

profile of v6, /device:TPU:6, one launch (start us, length us, event | category | flops | bytes accessed | tf_op | source)
XLA Modules:
  0.0 49.5 jit_solution(16008031956108806880)
XLA Ops:
  0.6 4.2 %load.1 = (f32[56,48,128]{2,1,0:T(8,128)S(1)}, f32[56,48,128]{2,1,0:T(8,128)S(1)}, f32[56,48,128]{2,1,0:T(8,128)S(1)}, f32[56,48,128]{2,1,0:T(8,128)S(1)}, f32[1...) custom-call(f32[56,32,128]{2,1,0:T(8,128)} %u.1, ...), custom_call_target="tpu_custom_call" | custom-call | tf_op jit(solution)/shard_map/load/pallas_call | solution.py:158
  4.9 4.0 %collective-permute-start = (f32[4,7,8,128]{3,2,1,0:T(8,128)S(1)}, f32[4,7,8,128]{3,2,1,0:T(8,128)S(1)}, u32[]{:S(2)}, u32[]{:S(2)}) collective-permute-start(f32[4,7,8,128]{3,2,1,0:T(8,128)S(1)} %get-tuple-element.44), channel_id=1, source_target_pairs={{32,64},{64,32},{96,128},{128,96},{160,192},{192,160},{224,256},{2... | collective-permute-start | bytes 344072 | tf_op jit(solution)/shard_map/ppermute | solution.py:33
  8.8 2.3 %collective-permute-start.1 = (f32[4,7,8,128]{3,2,1,0:T(8,128)S(1)}, f32[4,7,8,128]{3,2,1,0:T(8,128)S(1)}, u32[]{:S(2)}, u32[]{:S(2)}) collective-permute-start(f32[4,7,8,128]{3,2,1,0:T(8,128)S(1)} %get-tuple-element.45), channel_id=1, source_target_pairs={{0,32},{32,0},{64,96},{96,64},{128,160},{160,128},{192,224},{224,1... | collective-permute-start | bytes 344072 | tf_op jit(solution)/shard_map/ppermute | solution.py:33
  11.2 0.1 pack_rates.1._
  11.3 1.5 %collective-permute-done.x_b = f32[4,7,8,128]{3,2,1,0:T(8,128)S(1)} collective-permute-done((f32[4,7,8,128]{3,2,1,0:T(8,128)S(1)}, f32[4,7,8,128]{3,2,1,0:T(8,128)S(1)}, u32[]{:S(2)}, u32[]{:S(2)}) %collective-permute-start) | collective-permute-done | bytes 114720 | tf_op jit(solution)/shard_map/ppermute | solution.py:33
  12.8 0.0 collective-permute-done.1.x_a
  12.8 10.6 %collective-permute-start.3 = (f32[344,128]{1,0:T(8,128)S(1)}, f32[344,128]{1,0:T(8,128)S(1)}, u32[]{:S(2)}, u32[]{:S(2)}) collective-permute-start(f32[344,128]{1,0:T(8,128)S(1)} %pack_rates.1._), channel_id=1, source_target_pairs={{0,24},{1,1},{2,2},{3,3},{4,4},{5,5},{6,6},{7,15},{8,0},{9,9},{10,... | collective-permute-start | bytes 528392 | tf_op jit(solution)/shard_map/ppermute | solution.py:60
  23.4 0.3 pack_odd.1._
  23.7 4.8 %collective-permute-start.2 = (f32[504,128]{1,0:T(8,128)S(1)}, f32[504,128]{1,0:T(8,128)S(1)}, u32[]{:S(2)}, u32[]{:S(2)}) collective-permute-start(f32[504,128]{1,0:T(8,128)S(1)} %pack_odd.1._), channel_id=1, source_target_pairs={{1,2},{2,1},{3,4},{4,3},{5,6},{6,5},{7,8},{8,7},{9,10},{10,9},{11,... | collective-permute-start | bytes 774152 | tf_op jit(solution)/shard_map/ppermute | solution.py:33
  28.5 0.3 pack_even.1
  28.8 1.9 %collective-permute-start.5 = (f32[848,128]{1,0:T(8,128)S(1)}, f32[848,128]{1,0:T(8,128)S(1)}, u32[]{:S(2)}, u32[]{:S(2)}) collective-permute-start(f32[848,128]{1,0:T(8,128)S(1)} %pack_even.1), channel_id=1, source_target_pairs={{0,1},{1,0},{2,3},{3,2},{4,5},{5,4},{6,7},{7,6},{8,9},{9,8},{10,11... | collective-permute-start | bytes 1302536 | tf_op jit(solution)/shard_map/ppermute | solution.py:33
  30.8 4.4 %early.1 = (f32[18,48,128]{2,1,0:T(8,128)S(1)}, f32[18,48,128]{2,1,0:T(8,128)S(1)}, f32[18,48,128]{2,1,0:T(8,128)S(1)}, f32[18,48,128]{2,1,0:T(8,128)S(1)}, f32[...) custom-call(f32[56,48,128]{2,1,0:T(8,128)S(1)} %get-tuple-element.40, ...), custom_call_target="tpu_custom_call", output_to_operand_aliasing={{0}: (6, {}), {1}: (7, {}), {2}: (8, {}), {3}: (9, {})} | custom-call | flops 20000000000 | bytes 5000000000 | tf_op jit(solution)/shard_map/early/pallas_call | solution.py:359
  35.1 0.0 collective-permute-done.3
  35.2 1.9 %collective-permute-start.4 = (f32[344,128]{1,0:T(8,128)S(1)}, f32[344,128]{1,0:T(8,128)S(1)}, u32[]{:S(2)}, u32[]{:S(2)}) collective-permute-start(f32[344,128]{1,0:T(8,128)S(1)} %collective-permute-done.3), channel_id=1, source_target_pairs={{0,7},{1,2},{2,1},{3,4},{4,3},{5,6},{6,5},{7,0},{8,15},{9,10},{10,... | collective-permute-start | bytes 528392 | tf_op jit(solution)/shard_map/ppermute | solution.py:65
  37.1 2.9 %late.1 = (f32[56,48,128]{2,1,0:T(8,128)S(1)}, f32[56,48,128]{2,1,0:T(8,128)S(1)}, f32[56,32,128]{2,1,0:T(8,128)S(1)}, f32[56,32,128]{2,1,0:T(8,128)S(1)}) custom-call(f32[56,48,128]{2,1,0:T(8,128)S(1)} %get-tuple-element.42.feed.refs_5_, f32[56,48,128]{2,1,0:T(8,128)S(1)} %get-tuple-element.43.decay.refs_6_, f32[7,48,128]{2,1,0:T(8,128)S(1)} %get-tuple-element.70.mu, ...), custom_call_target="tpu_custom_call" | custom-call | flops 20000000000 | bytes 5000000000 | tf_op jit(solution)/shard_map/late/pallas_call | solution.py:389
  40.0 3.2 %collective-permute-done.2.refs_0_ = f32[504,128]{1,0:T(8,128)S(1)} collective-permute-done((f32[504,128]{1,0:T(8,128)S(1)}, f32[504,128]{1,0:T(8,128)S(1)}, u32[]{:S(2)}, u32[]{:S(2)}) %collective-permute-start.2) | collective-permute-done | bytes 258080 | tf_op jit(solution)/shard_map/ppermute | solution.py:33
  43.2 0.9 %collective-permute-done.4.refs_1_ = f32[344,128]{1,0:T(8,128)S(1)} collective-permute-done((f32[344,128]{1,0:T(8,128)S(1)}, f32[344,128]{1,0:T(8,128)S(1)}, u32[]{:S(2)}, u32[]{:S(2)}) %collective-permute-start.4) | collective-permute-done | bytes 176160 | tf_op jit(solution)/shard_map/ppermute | solution.py:65
  44.1 0.0 collective-permute-done.5.refs_2_
  44.1 5.4 %border.1 = (f32[56,48,128]{2,1,0:T(8,128)S(1)}, f32[56,48,128]{2,1,0:T(8,128)S(1)}, f32[56,48,128]{2,1,0:T(8,128)S(1)}, f32[56,48,128]{2,1,0:T(8,128)S(1)}, f32...) custom-call(f32[504,128]{1,0:T(8,128)S(1)} %collective-permute-done., ...), custom_call_target="tpu_custom_call", output_to_operand_aliasing={{0}: (3, {}), {1}: (4, {}), {2}: (5, {}), {3}: (6, {}), {4}... | custom-call | flops 20000000 | bytes 5000000 | tf_op jit(solution)/shard_map/border/pallas_call | solution.py:486
Async XLA Ops:
  4.9 7.9 %collective-permute-start = (f32[4,7,8,128]{3,2,1,0:T(8,128)S(1)}, f32[4,7,8,128]{3,2,1,0:T(8,128)S(1)}, u32[]{:S(2)}, u32[]{:S(2)}) collective-permute-start(f32[4,7,8,128]{3,2,1,0:T(8,128)S(1)} %get-tuple-element.44), channel_id=1, source_target_pairs={{32,64},{64,32},{96,128},{128,96},{160,192},{192,160},{224,256},{2... | collective-permute-start | bytes 344072 | tf_op jit(solution)/shard_map/ppermute | solution.py:33
  8.8 3.9 %collective-permute-start.1 = (f32[4,7,8,128]{3,2,1,0:T(8,128)S(1)}, f32[4,7,8,128]{3,2,1,0:T(8,128)S(1)}, u32[]{:S(2)}, u32[]{:S(2)}) collective-permute-start(f32[4,7,8,128]{3,2,1,0:T(8,128)S(1)} %get-tuple-element.45), channel_id=1, source_target_pairs={{0,32},{32,0},{64,96},{96,64},{128,160},{160,128},{192,224},{224,1... | collective-permute-start | bytes 344072 | tf_op jit(solution)/shard_map/ppermute | solution.py:33
  12.8 22.4 %collective-permute-start.3 = (f32[344,128]{1,0:T(8,128)S(1)}, f32[344,128]{1,0:T(8,128)S(1)}, u32[]{:S(2)}, u32[]{:S(2)}) collective-permute-start(f32[344,128]{1,0:T(8,128)S(1)} %pack_rates.1._), channel_id=1, source_target_pairs={{0,24},{1,1},{2,2},{3,3},{4,4},{5,5},{6,6},{7,15},{8,0},{9,9},{10,... | collective-permute-start | bytes 528392 | tf_op jit(solution)/shard_map/ppermute | solution.py:60
  23.7 19.5 %collective-permute-start.2 = (f32[504,128]{1,0:T(8,128)S(1)}, f32[504,128]{1,0:T(8,128)S(1)}, u32[]{:S(2)}, u32[]{:S(2)}) collective-permute-start(f32[504,128]{1,0:T(8,128)S(1)} %pack_odd.1._), channel_id=1, source_target_pairs={{1,2},{2,1},{3,4},{4,3},{5,6},{6,5},{7,8},{8,7},{9,10},{10,9},{11,... | collective-permute-start | bytes 774152 | tf_op jit(solution)/shard_map/ppermute | solution.py:33
  28.8 15.3 %collective-permute-start.5 = (f32[848,128]{1,0:T(8,128)S(1)}, f32[848,128]{1,0:T(8,128)S(1)}, u32[]{:S(2)}, u32[]{:S(2)}) collective-permute-start(f32[848,128]{1,0:T(8,128)S(1)} %pack_even.1), channel_id=1, source_target_pairs={{0,1},{1,0},{2,3},{3,2},{4,5},{5,4},{6,7},{7,6},{8,9},{9,8},{10,11... | collective-permute-start | bytes 1302536 | tf_op jit(solution)/shard_map/ppermute | solution.py:33
  35.2 8.9 %collective-permute-start.4 = (f32[344,128]{1,0:T(8,128)S(1)}, f32[344,128]{1,0:T(8,128)S(1)}, u32[]{:S(2)}, u32[]{:S(2)}) collective-permute-start(f32[344,128]{1,0:T(8,128)S(1)} %collective-permute-done.3), channel_id=1, source_target_pairs={{0,7},{1,2},{2,1},{3,4},{4,3},{5,6},{6,5},{7,0},{8,15},{9,10},{10,... | collective-permute-start | bytes 528392 | tf_op jit(solution)/shard_map/ppermute | solution.py:65

commit v7 on v6

--- a/solution.py
+++ b/solution.py
@@ -310,8 +310,6 @@
 
 INNER_ROWS = (8, 16, 24, 32)
 LAST_INNER_ROWS = (12, 20, 28)
-BORDER_ROWS = (4, 36)
-LAST_BORDER_ROWS = (8, 36)
 
 
 EARLY_STEPS = 2
@@ -392,86 +390,90 @@
 N_STATE = 22
 
 
-def border_kernel(*refs):
-    y_b, r_b, y_a = refs[:3]
-    state = refs[3 + N_STATE : 3 + 2 * N_STATE]
-    out_u, out_v, su4, sv4, mu, mv, sems = refs[3 + 2 * N_STATE :]
+def border_kernel(is_last, *refs):
+    n_messages = 2 if is_last else 1
+    messages = refs[:n_messages]
+    state = refs[n_messages + N_STATE : n_messages + 2 * N_STATE]
+    rest = refs[n_messages + 2 * N_STATE :]
     (u0, v0, feed, decay, su0, sv0, s_feed, s_decay) = state[:8]
     (su1, sv1, su2, sv2, su3, sv3, u1, v1, u2, v2, u3, v3, o_u, o_v) = state[8:]
-    even_y = is_even("gy")
+    if is_last:
+        (y, rate_src), tail = messages, 0
+        out_u, out_v, su4, sv4, mu, mv, sems = rest
+    else:
+        y, rate_src, tail = messages[0], messages[0], TAIL
+        su4, sv4, mu, mv = rest
+    is_low = is_even("gy") if is_last else jnp.logical_not(is_even("gy"))
     lane, inner, group = lanes()
-    start = (jnp.where(even_y, LOW, HIGH), jnp.where(even_y, HIGH, LOW))
-    rate_start = (jnp.where(even_y, LOW + 1, HIGH), jnp.where(even_y, HIGH, LOW + 1))
-
-    sides = ((y_b, r_b, 0), (y_a, y_a, TAIL))
+    to, rate_to = jnp.where(is_low, LOW, HIGH), jnp.where(is_low, LOW + 1, HIGH)
+    tile, last_tile, out_row = jnp.where(is_low, 4, 36), jnp.where(is_low, 8, 36), jnp.where(is_low, 0, NY - 4)
 
     def rows(z, carry):
-        for (src, rate_src, tail), to, rate_to in zip(sides, start, rate_start):
-            u0[z, pl.ds(to, 4), :] = src[pl.ds(FIELDS * z, 4), :]
-            v0[z, pl.ds(to, 4), :] = src[pl.ds(FIELDS * z + 4, 4), :]
-            feed[z, pl.ds(rate_to, 3), :] = rate_src[pl.ds(tail + RATES * z, 3), :]
-            decay[z, pl.ds(rate_to, 3), :] = rate_src[pl.ds(tail + RATES * z + 3, 3), :]
-        return carry
-
-    lax.fori_loop(0, NZ, rows, 0, unroll=4)
+        u0[z, pl.ds(to, 4), :] = y[pl.ds(FIELDS * z, 4), :]
+        v0[z, pl.ds(to, 4), :] = y[pl.ds(FIELDS * z + 4, 4), :]
+        feed[z, pl.ds(rate_to, 3), :] = rate_src[pl.ds(tail + RATES * z, 3), :]
+        decay[z, pl.ds(rate_to, 3), :] = rate_src[pl.ds(tail + RATES * z + 3, 3), :]
+        return carry
+
+    lax.fori_loop(0, NZ, rows, 0, unroll=8)
 
     right_halo = (inner >= 8) & (inner < 12)
     left_halo = (inner >= 4) & (inner < 8)
 
     def strip(j, carry):
-        for (y, rate_src, tail), to, rate_to in zip(sides, start, rate_start):
-            fields = rates = None
-            for g in range(GROUPS):
-                z = GZ * g + j
-                one = turn(y[pl.ds(FIELDS * z, 8), :], 16 * g + 8)
-                two = turn(rate_src[pl.ds(tail + RATES * z, 8), :], 16 * g + 8)
-                fields = one if g == 0 else jnp.where(group == g, one, fields)
-                rates = two if g == 0 else jnp.where(group == g, two, rates)
-            corner = y[pl.ds(CORNER + 8 * j, 8), :]
-            other = turn(corner, 4, 0)
-            for plane, mask, lane_at, top, bottom in (
-                (j + RIGHT, right_halo, 8, corner, other),
-                (j + LEFT, left_halo, 4, other, corner),
-            ):
-                su0[plane, pl.ds(to, 4), :] = jnp.where(mask, turn(top, lane_at), fields)[:4]
-                sv0[plane, pl.ds(to, 4), :] = jnp.where(mask, turn(bottom, lane_at - 4), fields)[4:]
-                s_feed[plane, pl.ds(rate_to, 3), :] = rates[:3]
-                s_decay[plane, pl.ds(rate_to, 3), :] = rates[3:6]
-                for n, ref in ((2, s_feed), (3, s_decay)):
-                    halo = turn(top, lane_at - 4 * n)[:4]
-                    at = pl.ds(to, 4)
-                    ref[plane, at, :] = jnp.where(mask[:4], halo, ref[plane, at, :])
+        fields = rates = None
+        for g in range(GROUPS):
+            z = GZ * g + j
+            one = turn(y[pl.ds(FIELDS * z, 8), :], 16 * g + 8)
+            two = turn(rate_src[pl.ds(tail + RATES * z, 8), :], 16 * g + 8)
+            fields = one if g == 0 else jnp.where(group == g, one, fields)
+            rates = two if g == 0 else jnp.where(group == g, two, rates)
+        corner = y[pl.ds(CORNER + 8 * j, 8), :]
+        other = turn(corner, 4, 0)
+        for plane, mask, lane_at, top, bottom in (
+            (j + RIGHT, right_halo, 8, corner, other),
+            (j + LEFT, left_halo, 4, other, corner),
+        ):
+            su0[plane, pl.ds(to, 4), :] = jnp.where(mask, turn(top, lane_at), fields)[:4]
+            sv0[plane, pl.ds(to, 4), :] = jnp.where(mask, turn(bottom, lane_at - 4), fields)[4:]
+            s_feed[plane, pl.ds(rate_to, 3), :] = rates[:3]
+            s_decay[plane, pl.ds(rate_to, 3), :] = rates[3:6]
+            for n, ref in ((2, s_feed), (3, s_decay)):
+                halo = turn(top, lane_at - 4 * n)[:4]
+                at = pl.ds(to, 4)
+                ref[plane, at, :] = jnp.where(mask[:4], halo, ref[plane, at, :])
         return carry
 
     lax.fori_loop(0, GZ, strip, 0, unroll=True)
 
     levels = [(su0, sv0), (su1, sv1), (su2, sv2), (su3, sv3), (su4, sv4)]
     for step in range(STEPS):
-        rows_now = BORDER_ROWS if step < STEPS - 1 else LAST_BORDER_ROWS
-        strip_ends(levels[step], BORDER_ROWS, group)
-        emit = to_planes(levels[step + 1], rows_now)
-        sweep(levels[step], (s_feed, s_decay), rows_now, 2 * GZ, strip_place, emit, 14)
-    merge_strips((su4, sv4), (mu, mv), LAST_BORDER_ROWS, inner)
+        now = (tile,) if step < STEPS - 1 else (last_tile,)
+        strip_ends(levels[step], (tile,), group)
+        sweep(levels[step], (s_feed, s_decay), now, 2 * GZ, strip_place, to_planes(levels[step + 1], now), 14)
+    merge_strips((su4, sv4), (mu, mv), (last_tile,), inner)
 
     levels = [(u0, v0), (u1, v1), (u2, v2), (u3, v3)]
     for step in range(STEPS - 1):
-        emit = to_planes(levels[step + 1], BORDER_ROWS)
-        sweep(levels[step], (feed, decay), BORDER_ROWS, NZ, main_place, emit, 28)
+        sweep(levels[step], (feed, decay), (tile,), NZ, main_place, to_planes(levels[step + 1], (tile,)), 28)
     edge = (lane < 4) | (lane >= 124)
 
     def finish(z, values):
-        for row, to, new in zip(LAST_BORDER_ROWS, (0, NY - 4), values):
-            for out, merged, value in zip((o_u, o_v), (mu, mv), new):
-                out[z, pl.ds(to, 4), :] = with_edges(merged, z, row, value, edge)[:4]
-
+        for out, merged, value in zip((o_u, o_v), (mu, mv), values[0]):
+            out[z, pl.ds(out_row, 4), :] = with_edges(merged, z, last_tile, value, edge)[:4]
+
+    if not is_last:
+        sweep(levels[-1], (feed, decay), (last_tile,), NZ, main_place, finish, 28)
+        return
     copies = []
-    part = NZ // 4
-    for c in range(4):
+    parts = 2
+    part = NZ // parts
+    for c in range(parts):
 
         def place(i, c=c):
             return main_place(i + c * part)
 
-        sweep(levels[-1], (feed, decay), LAST_BORDER_ROWS, part, place, finish, part)
+        sweep(levels[-1], (feed, decay), (last_tile,), part, place, finish, part)
         for n, (src, dst) in enumerate(((o_u, out_u), (o_v, out_v))):
             at = pl.ds(c * part, part)
             copies.append(pltpu.make_async_copy(src.at[at], dst.at[at], sems.at[2 * c + n]))
@@ -480,19 +482,25 @@
         copy.wait()
 
 
-def border(y_b, r_b, y_a, *state):
-    out = tuple(vmem(*a.shape) for a in state) + (jax.ShapeDtypeStruct((NZ, NY, NX), jnp.float32),) * 2
-    specs = [pl.BlockSpec(memory_space=pltpu.VMEM)] * N_STATE + [pl.BlockSpec(memory_space=pltpu.HBM)] * 2
+def border(messages, state):
+    is_last = len(messages) == 2
+    out = tuple(vmem(*a.shape) for a in state)
+    specs = [pl.BlockSpec(memory_space=pltpu.VMEM)] * N_STATE
+    scratch = [vmem(*STRIP)] * 2 + [vmem(GZ, PY, NX)] * 2
+    if is_last:
+        out += (jax.ShapeDtypeStruct((NZ, NY, NX), jnp.float32),) * 2
+        specs += [pl.BlockSpec(memory_space=pltpu.HBM)] * 2
+        scratch += [pltpu.SemaphoreType.DMA((4,))]
     return pallas(
-        border_kernel,
-        "border",
+        functools.partial(border_kernel, is_last),
+        "border_odd" if is_last else "border_even",
         4,
-        20_000_000,
+        20_000_000_000,
         out_shape=out,
         out_specs=tuple(specs),
-        input_output_aliases={3 + n: n for n in range(N_STATE)},
-        scratch_shapes=[vmem(*STRIP)] * 2 + [vmem(GZ, PY, NX)] * 2 + [pltpu.SemaphoreType.DMA((8,))],
-    )(y_b, r_b, y_a, *state)[N_STATE:]
+        input_output_aliases={len(messages) + n: n for n in range(N_STATE)},
+        scratch_shapes=scratch,
+    )(*messages, *state)
 
 
 def shards(activator, inhibitor, feed_rate, kill_rate):
@@ -513,7 +521,8 @@
     half_way, mu = lax.optimization_barrier((half_way, mu))
     r_b = after_relay(half_way, "gy")
     rest = late(feed, decay, mu, mv, *fields[-2:])
-    return border(y_b, r_b, y_a, u0, v0, feed, decay, *strips, *fields, *rest)
+    state = border((y_a,), (u0, v0, feed, decay, *strips, *fields, *rest))
+    return border((y_b, r_b), state)[N_STATE:]
 
 
 def solution(mesh):

time: 50.3 us -> 49.8 us (0.990)
  waiting for transfers between devices: 5.64 us -> 3.54 us
  Pallas kernels: 17.5 us -> 19 us
    pallas_call x1 -> x2, Pallas kernels: 5.42 us -> 6.83 us  [border(): pallas(functools.partial(border_kernel, is_last), 'border_odd' if is_last...]
    ppermute x4, waiting for transfers between devices: 4.75 us -> 3.54 us  [swap(): return lax.ppermute(block, axis, swap_pairs(lax.axis_size(axis), parity))]
    ppermute x1, waiting for transfers between devices: 0.89 us -> 0.01 us  [after_relay(): lax.ppermute(block, axis, second_pairs(count) if count % SPAN == 0 else s...]
  transfers between devices with their start and end apart: 6 -> 6, of which waited for: 3 -> 2; matrix products, arithmetic and copies ran while one was open for 0% -> 0% of each run, Pallas kernels for 16% -> 22%
where the time goes in v7:
time: 49.8 us; the launch traced here: 48.9 us
  starting transfers between devices  25.6 us (51%)
  Pallas kernels  19 us (38%)
  waiting for transfers between devices  3.54 us (7%)
  between operations  0.75 us (2%)
    ppermute x4, starting transfers between devices, swap(): return lax.ppermute(block, axis, swap_pairs(lax.axis_size(axis), parity))  13 us
    ppermute x1, starting transfers between devices, relay(): lax.ppermute(block, axis, relay_pairs(count))  10.6 us
    pallas_call x2, Pallas kernels, border(): pallas(functools.partial(border_kernel, is_last), 'border_odd' if is_last...  6.83 us
    pallas_call x1, Pallas kernels, early(): pallas(early_kernel, 'early', 4, 20000000000, out_shape=out, input_output...  4.4 us
    pallas_call x1, Pallas kernels, load(): pallas(load_kernel, 'load', 8, out_shape=(vmem(*FIELD),) * 4 + (vmem(*STR...  4.22 us
    ppermute x4, waiting for transfers between devices, swap(): return lax.ppermute(block, axis, swap_pairs(lax.axis_size(axis), parity))  3.54 us
    pallas_call x1, Pallas kernels, late(): pallas(late_kernel, 'late', 4, 20000000000, out_shape=out)  2.96 us
    ppermute x1, starting transfers between devices, after_relay(): lax.ppermute(block, axis, second_pairs(count) if count % SPAN == 0 else s...  1.92 us
  transfers between devices with their start and end apart: 6, of which 2 were waited for; matrix products, arithmetic and copies ran while one was open for 0% of the time, Pallas kernels for 22%

profile of v7, /device:TPU:6, one launch (start us, length us, event | category | flops | bytes accessed | tf_op | source)
XLA Modules:
  0.0 48.9 jit_solution(7166862232722635156)
XLA Ops:
  0.6 4.2 %load.1 = (f32[56,48,128]{2,1,0:T(8,128)S(1)}, f32[56,48,128]{2,1,0:T(8,128)S(1)}, f32[56,48,128]{2,1,0:T(8,128)S(1)}, f32[56,48,128]{2,1,0:T(8,128)S(1)}, f32[1...) custom-call(f32[56,32,128]{2,1,0:T(8,128)} %u.1, ...), custom_call_target="tpu_custom_call" | custom-call | tf_op jit(solution)/shard_map/load/pallas_call | solution.py:158
  4.9 4.0 %collective-permute-start = (f32[4,7,8,128]{3,2,1,0:T(8,128)S(1)}, f32[4,7,8,128]{3,2,1,0:T(8,128)S(1)}, u32[]{:S(2)}, u32[]{:S(2)}) collective-permute-start(f32[4,7,8,128]{3,2,1,0:T(8,128)S(1)} %get-tuple-element.66), channel_id=1, source_target_pairs={{32,64},{64,32},{96,128},{128,96},{160,192},{192,160},{224,256},{2... | collective-permute-start | bytes 344072 | tf_op jit(solution)/shard_map/ppermute | solution.py:33
  8.8 2.3 %collective-permute-start.1 = (f32[4,7,8,128]{3,2,1,0:T(8,128)S(1)}, f32[4,7,8,128]{3,2,1,0:T(8,128)S(1)}, u32[]{:S(2)}, u32[]{:S(2)}) collective-permute-start(f32[4,7,8,128]{3,2,1,0:T(8,128)S(1)} %get-tuple-element.67), channel_id=1, source_target_pairs={{0,32},{32,0},{64,96},{96,64},{128,160},{160,128},{192,224},{224,1... | collective-permute-start | bytes 344072 | tf_op jit(solution)/shard_map/ppermute | solution.py:33
  11.2 0.1 pack_rates.1._
  11.3 1.5 %collective-permute-done.x_b = f32[4,7,8,128]{3,2,1,0:T(8,128)S(1)} collective-permute-done((f32[4,7,8,128]{3,2,1,0:T(8,128)S(1)}, f32[4,7,8,128]{3,2,1,0:T(8,128)S(1)}, u32[]{:S(2)}, u32[]{:S(2)}) %collective-permute-start) | collective-permute-done | bytes 114720 | tf_op jit(solution)/shard_map/ppermute | solution.py:33
  12.8 0.0 collective-permute-done.1.x_a
  12.8 10.6 %collective-permute-start.3 = (f32[344,128]{1,0:T(8,128)S(1)}, f32[344,128]{1,0:T(8,128)S(1)}, u32[]{:S(2)}, u32[]{:S(2)}) collective-permute-start(f32[344,128]{1,0:T(8,128)S(1)} %pack_rates.1._), channel_id=1, source_target_pairs={{0,24},{1,1},{2,2},{3,3},{4,4},{5,5},{6,6},{7,15},{8,0},{9,9},{10,... | collective-permute-start | bytes 528392 | tf_op jit(solution)/shard_map/ppermute | solution.py:60
  23.4 0.3 pack_odd.1._
  23.7 4.8 %collective-permute-start.2 = (f32[504,128]{1,0:T(8,128)S(1)}, f32[504,128]{1,0:T(8,128)S(1)}, u32[]{:S(2)}, u32[]{:S(2)}) collective-permute-start(f32[504,128]{1,0:T(8,128)S(1)} %pack_odd.1._), channel_id=1, source_target_pairs={{1,2},{2,1},{3,4},{4,3},{5,6},{6,5},{7,8},{8,7},{9,10},{10,9},{11,... | collective-permute-start | bytes 774152 | tf_op jit(solution)/shard_map/ppermute | solution.py:33
  28.5 0.3 pack_even.1
  28.8 1.9 %collective-permute-start.5 = (f32[848,128]{1,0:T(8,128)S(1)}, f32[848,128]{1,0:T(8,128)S(1)}, u32[]{:S(2)}, u32[]{:S(2)}) collective-permute-start(f32[848,128]{1,0:T(8,128)S(1)} %pack_even.1), channel_id=1, source_target_pairs={{0,1},{1,0},{2,3},{3,2},{4,5},{5,4},{6,7},{7,6},{8,9},{9,8},{10,11... | collective-permute-start | bytes 1302536 | tf_op jit(solution)/shard_map/ppermute | solution.py:33
  30.7 4.4 %early.1 = (f32[18,48,128]{2,1,0:T(8,128)S(1)}, f32[18,48,128]{2,1,0:T(8,128)S(1)}, f32[18,48,128]{2,1,0:T(8,128)S(1)}, f32[18,48,128]{2,1,0:T(8,128)S(1)}, f32[...) custom-call(f32[56,48,128]{2,1,0:T(8,128)S(1)} %get-tuple-element.62, ...), custom_call_target="tpu_custom_call", output_to_operand_aliasing={{0}: (6, {}), {1}: (7, {}), {2}: (8, {}), {3}: (9, {})} | custom-call | flops 20000000000 | bytes 5000000000 | tf_op jit(solution)/shard_map/early/pallas_call | solution.py:357
  35.1 0.0 collective-permute-done.3
  35.2 1.9 %collective-permute-start.4 = (f32[344,128]{1,0:T(8,128)S(1)}, f32[344,128]{1,0:T(8,128)S(1)}, u32[]{:S(2)}, u32[]{:S(2)}) collective-permute-start(f32[344,128]{1,0:T(8,128)S(1)} %collective-permute-done.3), channel_id=1, source_target_pairs={{0,7},{1,2},{2,1},{3,4},{4,3},{5,6},{6,5},{7,0},{8,15},{9,10},{10,... | collective-permute-start | bytes 528392 | tf_op jit(solution)/shard_map/ppermute | solution.py:65
  37.1 3.0 %late.1 = (f32[56,48,128]{2,1,0:T(8,128)S(1)}, f32[56,48,128]{2,1,0:T(8,128)S(1)}, f32[56,32,128]{2,1,0:T(8,128)S(1)}, f32[56,32,128]{2,1,0:T(8,128)S(1)}) custom-call(f32[56,48,128]{2,1,0:T(8,128)S(1)} %get-tuple-element.64.feed.refs_3_, f32[56,48,128]{2,1,0:T(8,128)S(1)} %get-tuple-element.65.decay.refs_4_, f32[7,48,128]{2,1,0:T(8,128)S(1)} %get-tuple-element.92.mu, ...), custom_call_target="tpu_custom_call" | custom-call | flops 20000000000 | bytes 5000000000 | tf_op jit(solution)/shard_map/late/pallas_call | solution.py:387
  40.0 2.0 %collective-permute-done.5.refs_0_ = f32[848,128]{1,0:T(8,128)S(1)} collective-permute-done((f32[848,128]{1,0:T(8,128)S(1)}, f32[848,128]{1,0:T(8,128)S(1)}, u32[]{:S(2)}, u32[]{:S(2)}) %collective-permute-start.5) | collective-permute-done | bytes 434208 | tf_op jit(solution)/shard_map/ppermute | solution.py:33
  42.1 3.0 %border_even.1 = (f32[56,48,128]{2,1,0:T(8,128)S(1)}, f32[56,48,128]{2,1,0:T(8,128)S(1)}, f32[56,48,128]{2,1,0:T(8,128)S(1)}, f32[56,48,128]{2,1,0:T(8,128)S(1)}...) custom-call(f32[848,128]{1,0:T(8,128)S(1)} %collective-permute-done., ...), custom_call_target="tpu_custom_call", output_to_operand_aliasing={{0}: (1, {}), {1}: (2, {}), {2}: (3, {}), {3}: (4, {}), {4}... | custom-call | flops 20000000000 | bytes 5000000000 | tf_op jit(solution)/shard_map/border_even/pallas_call | solution.py:494
  45.0 0.0 collective-permute-done.2.refs_0_
  45.0 0.0 collective-permute-done.4.refs_1_
  45.1 3.9 %border_odd.1 = (f32[56,48,128]{2,1,0:T(8,128)S(1)}, f32[56,48,128]{2,1,0:T(8,128)S(1)}, f32[56,48,128]{2,1,0:T(8,128)S(1)}, f32[56,48,128]{2,1,0:T(8,128)S(1)},...) custom-call(f32[504,128]{1,0:T(8,128)S(1)} %collective-permute-done., ...), custom_call_target="tpu_custom_call", output_to_operand_aliasing={{0}: (2, {}), {1}: (3, {}), {2}: (4, {}), {3}: (5, {}), {4}... | custom-call | flops 20000000000 | bytes 5000000000 | tf_op jit(solution)/shard_map/border_odd/pallas_call | solution.py:494
Async XLA Ops:
  4.9 7.9 %collective-permute-start = (f32[4,7,8,128]{3,2,1,0:T(8,128)S(1)}, f32[4,7,8,128]{3,2,1,0:T(8,128)S(1)}, u32[]{:S(2)}, u32[]{:S(2)}) collective-permute-start(f32[4,7,8,128]{3,2,1,0:T(8,128)S(1)} %get-tuple-element.66), channel_id=1, source_target_pairs={{32,64},{64,32},{96,128},{128,96},{160,192},{192,160},{224,256},{2... | collective-permute-start | bytes 344072 | tf_op jit(solution)/shard_map/ppermute | solution.py:33
  8.8 3.9 %collective-permute-start.1 = (f32[4,7,8,128]{3,2,1,0:T(8,128)S(1)}, f32[4,7,8,128]{3,2,1,0:T(8,128)S(1)}, u32[]{:S(2)}, u32[]{:S(2)}) collective-permute-start(f32[4,7,8,128]{3,2,1,0:T(8,128)S(1)} %get-tuple-element.67), channel_id=1, source_target_pairs={{0,32},{32,0},{64,96},{96,64},{128,160},{160,128},{192,224},{224,1... | collective-permute-start | bytes 344072 | tf_op jit(solution)/shard_map/ppermute | solution.py:33
  12.8 22.4 %collective-permute-start.3 = (f32[344,128]{1,0:T(8,128)S(1)}, f32[344,128]{1,0:T(8,128)S(1)}, u32[]{:S(2)}, u32[]{:S(2)}) collective-permute-start(f32[344,128]{1,0:T(8,128)S(1)} %pack_rates.1._), channel_id=1, source_target_pairs={{0,24},{1,1},{2,2},{3,3},{4,4},{5,5},{6,6},{7,15},{8,0},{9,9},{10,... | collective-permute-start | bytes 528392 | tf_op jit(solution)/shard_map/ppermute | solution.py:60
  23.7 21.3 %collective-permute-start.2 = (f32[504,128]{1,0:T(8,128)S(1)}, f32[504,128]{1,0:T(8,128)S(1)}, u32[]{:S(2)}, u32[]{:S(2)}) collective-permute-start(f32[504,128]{1,0:T(8,128)S(1)} %pack_odd.1._), channel_id=1, source_target_pairs={{1,2},{2,1},{3,4},{4,3},{5,6},{6,5},{7,8},{8,7},{9,10},{10,9},{11,... | collective-permute-start | bytes 774152 | tf_op jit(solution)/shard_map/ppermute | solution.py:33
  28.8 13.2 %collective-permute-start.5 = (f32[848,128]{1,0:T(8,128)S(1)}, f32[848,128]{1,0:T(8,128)S(1)}, u32[]{:S(2)}, u32[]{:S(2)}) collective-permute-start(f32[848,128]{1,0:T(8,128)S(1)} %pack_even.1), channel_id=1, source_target_pairs={{0,1},{1,0},{2,3},{3,2},{4,5},{5,4},{6,7},{7,6},{8,9},{9,8},{10,11... | collective-permute-start | bytes 1302536 | tf_op jit(solution)/shard_map/ppermute | solution.py:33
  35.2 9.9 %collective-permute-start.4 = (f32[344,128]{1,0:T(8,128)S(1)}, f32[344,128]{1,0:T(8,128)S(1)}, u32[]{:S(2)}, u32[]{:S(2)}) collective-permute-start(f32[344,128]{1,0:T(8,128)S(1)} %collective-permute-done.3), channel_id=1, source_target_pairs={{0,7},{1,2},{2,1},{3,4},{4,3},{5,6},{6,5},{7,0},{8,15},{9,10},{10,... | collective-permute-start | bytes 528392 | tf_op jit(solution)/shard_map/ppermute | solution.py:65

commit v8 on v7

--- a/solution.py
+++ b/solution.py
@@ -16,7 +16,7 @@
 FIELDS, RATES = 2 * W, 2 * (W - 1)
 CORNER = NZ * FIELDS
 TAIL = CORNER + 8 * GZ
-RATE_ROWS = NZ * RATES + 8
+MESSAGE = (TAIL + NZ * RATES + 8, NX)
 RIGHT, LEFT = 1, GZ + 3
 SPLANES = 2 * GZ + 4
 
@@ -31,38 +31,6 @@
 
 def swap(block, axis, parity):
     return lax.ppermute(block, axis, swap_pairs(lax.axis_size(axis), parity))
-
-
-SPAN = 8
-
-
-def relay_pairs(count):
-    pairs = []
-    for i in range(count):
-        run, place = divmod(i, SPAN)
-        runs = count // SPAN
-        step = {0: -1, SPAN - 1: 1}.get(place, 0)
-        pairs.append((i, (run + step) % runs * SPAN + place))
-    return pairs
-
-
-def second_pairs(count):
-    pairs = []
-    for i in range(count):
-        run, place = divmod(i, SPAN)
-        other = (place + 1 if place % 2 else place - 1) % SPAN
-        pairs.append((i, run * SPAN + other))
-    return pairs
-
-
-def relay(block, axis):
-    count = lax.axis_size(axis)
-    return lax.ppermute(block, axis, relay_pairs(count)) if count % SPAN == 0 else block
-
-
-def after_relay(block, axis):
-    count = lax.axis_size(axis)
-    return lax.ppermute(block, axis, second_pairs(count) if count % SPAN == 0 else swap_pairs(count, 1))
 
 
 def is_even(axis):
@@ -121,7 +89,7 @@
 
     copies[0].wait()
     copies[1].wait()
-    lax.fori_loop(0, NZ, rates, 0, unroll=4)
+    lax.fori_loop(0, NZ, rates, 0, unroll=14)
 
     def pack(arrays):
         def body(j, carry):
@@ -165,22 +133,6 @@
     )(u, v, f, k)
 
 
-def pack_rates_kernel(feed, decay, out):
-    start = jnp.where(is_even("gy"), OWN, OWN + 29)
-
-    def rows(z, carry):
-        out[pl.ds(RATES * z, 3), :] = feed[z, pl.ds(start, 3), :]
-        out[pl.ds(RATES * z + 3, 3), :] = decay[z, pl.ds(start, 3), :]
-        return carry
-
-    lax.fori_loop(0, NZ, rows, 0, unroll=8)
-    out[pl.ds(RATES * NZ, 8), :] = jnp.zeros((8, NX), jnp.float32)
-
-
-def pack_rates(feed, decay):
-    return pallas(pack_rates_kernel, "pack_rates", 4, out_shape=vmem(RATE_ROWS, NX))(feed, decay)
-
-
 def pack_y_kernel(which, u, v, feed, decay, x_b, x_a, _, out):
     even_x = is_even("gx")
     to_low = is_even("gy") if which else jnp.logical_not(is_even("gy"))
@@ -191,14 +143,12 @@
     def rows(z, carry):
         out[pl.ds(FIELDS * z, 4), :] = u[z, pl.ds(start, 4), :]
         out[pl.ds(FIELDS * z + 4, 4), :] = v[z, pl.ds(start, 4), :]
-        if not which:
-            out[pl.ds(TAIL + RATES * z, 3), :] = feed[z, pl.ds(rate_start, 3), :]
-            out[pl.ds(TAIL + RATES * z + 3, 3), :] = decay[z, pl.ds(rate_start, 3), :]
+        out[pl.ds(TAIL + RATES * z, 3), :] = feed[z, pl.ds(rate_start, 3), :]
+        out[pl.ds(TAIL + RATES * z + 3, 3), :] = decay[z, pl.ds(rate_start, 3), :]
         return carry
 
     lax.fori_loop(0, NZ, rows, 0, unroll=8)
-    if not which:
-        out[pl.ds(TAIL + RATES * NZ, 8), :] = jnp.zeros((8, NX), jnp.float32)
+    out[pl.ds(TAIL + RATES * NZ, 8), :] = jnp.zeros((8, NX), jnp.float32)
 
     def corner(j, carry):
         made = []
@@ -225,7 +175,7 @@
         functools.partial(pack_y_kernel, which),
         "pack_odd" if which else "pack_even",
         8,
-        out_shape=vmem(TAIL + (0 if which else RATE_ROWS), NX),
+        out_shape=vmem(*MESSAGE),
         in_specs=[pl.BlockSpec(memory_space=pltpu.VMEM)] * 6 + [pl.BlockSpec(memory_space=pl.ANY)],
     )(u, v, feed, decay, x_b, x_a, after)
 
@@ -349,7 +299,7 @@
     levels = [(u0, v0)] + list(zip(fields[::2], fields[1::2]))
     for step in range(EARLY_STEPS):
         emit = to_planes(levels[step + 1], INNER_ROWS)
-        sweep(levels[step], (feed, decay), INNER_ROWS, NZ, main_place, emit, 14)
+        sweep(levels[step], (feed, decay), INNER_ROWS, NZ, main_place, emit, 28)
 
 
 def early(u0, v0, feed, decay, x_b, x_a, su0, sv0, s_feed, s_decay):
@@ -371,7 +321,7 @@
     levels = [(first_u, first_v)] + list(zip(fields[::2], fields[1::2]))
     for step in range(STEPS - 1 - EARLY_STEPS):
         emit = to_planes(levels[step + 1], INNER_ROWS)
-        sweep(levels[step], (feed, decay), INNER_ROWS, NZ, main_place, emit, 14)
+        sweep(levels[step], (feed, decay), INNER_ROWS, NZ, main_place, emit, 28)
     edge = (lane < 4) | (lane >= 124)
 
     def finish(z, values):
@@ -379,7 +329,7 @@
             for out, merged, value in zip((o_u, o_v), (mu, mv), new):
                 out[z, pl.ds(row - OWN, 8), :] = with_edges(merged, z, row, value, edge)
 
-    sweep(levels[-1], (feed, decay), LAST_INNER_ROWS, NZ, main_place, finish, 14)
+    sweep(levels[-1], (feed, decay), LAST_INNER_ROWS, NZ, main_place, finish, 28)
 
 
 def late(feed, decay, mu, mv, first_u, first_v):
@@ -391,17 +341,12 @@
 
 
 def border_kernel(is_last, *refs):
-    n_messages = 2 if is_last else 1
-    messages = refs[:n_messages]
-    state = refs[n_messages + N_STATE : n_messages + 2 * N_STATE]
-    rest = refs[n_messages + 2 * N_STATE :]
+    y, state, rest = refs[0], refs[1 + N_STATE : 1 + 2 * N_STATE], refs[1 + 2 * N_STATE :]
     (u0, v0, feed, decay, su0, sv0, s_feed, s_decay) = state[:8]
     (su1, sv1, su2, sv2, su3, sv3, u1, v1, u2, v2, u3, v3, o_u, o_v) = state[8:]
     if is_last:
-        (y, rate_src), tail = messages, 0
         out_u, out_v, su4, sv4, mu, mv, sems = rest
     else:
-        y, rate_src, tail = messages[0], messages[0], TAIL
         su4, sv4, mu, mv = rest
     is_low = is_even("gy") if is_last else jnp.logical_not(is_even("gy"))
     lane, inner, group = lanes()
@@ -411,8 +356,8 @@
     def rows(z, carry):
         u0[z, pl.ds(to, 4), :] = y[pl.ds(FIELDS * z, 4), :]
         v0[z, pl.ds(to, 4), :] = y[pl.ds(FIELDS * z + 4, 4), :]
-        feed[z, pl.ds(rate_to, 3), :] = rate_src[pl.ds(tail + RATES * z, 3), :]
-        decay[z, pl.ds(rate_to, 3), :] = rate_src[pl.ds(tail + RATES * z + 3, 3), :]
+        feed[z, pl.ds(rate_to, 3), :] = y[pl.ds(TAIL + RATES * z, 3), :]
+        decay[z, pl.ds(rate_to, 3), :] = y[pl.ds(TAIL + RATES * z + 3, 3), :]
         return carry
 
     lax.fori_loop(0, NZ, rows, 0, unroll=8)
@@ -425,7 +370,7 @@
         for g in range(GROUPS):
             z = GZ * g + j
             one = turn(y[pl.ds(FIELDS * z, 8), :], 16 * g + 8)
-            two = turn(rate_src[pl.ds(tail + RATES * z, 8), :], 16 * g + 8)
+            two = turn(y[pl.ds(TAIL + RATES * z, 8), :], 16 * g + 8)
             fields = one if g == 0 else jnp.where(group == g, one, fields)
             rates = two if g == 0 else jnp.where(group == g, two, rates)
         corner = y[pl.ds(CORNER + 8 * j, 8), :]
@@ -455,7 +400,7 @@
 
     levels = [(u0, v0), (u1, v1), (u2, v2), (u3, v3)]
     for step in range(STEPS - 1):
-        sweep(levels[step], (feed, decay), (tile,), NZ, main_place, to_planes(levels[step + 1], (tile,)), 28)
+        sweep(levels[step], (feed, decay), (tile,), NZ, main_place, to_planes(levels[step + 1], (tile,)), 56)
     edge = (lane < 4) | (lane >= 124)
 
     def finish(z, values):
@@ -463,7 +408,7 @@
             out[z, pl.ds(out_row, 4), :] = with_edges(merged, z, last_tile, value, edge)[:4]
 
     if not is_last:
-        sweep(levels[-1], (feed, decay), (last_tile,), NZ, main_place, finish, 28)
+        sweep(levels[-1], (feed, decay), (last_tile,), NZ, main_place, finish, 56)
         return
     copies = []
     parts = 2
@@ -482,8 +427,7 @@
         copy.wait()
 
 
-def border(messages, state):
-    is_last = len(messages) == 2
+def border(is_last, message, state):
     out = tuple(vmem(*a.shape) for a in state)
     specs = [pl.BlockSpec(memory_space=pltpu.VMEM)] * N_STATE
     scratch = [vmem(*STRIP)] * 2 + [vmem(GZ, PY, NX)] * 2
@@ -498,9 +442,9 @@
         20_000_000_000,
         out_shape=out,
         out_specs=tuple(specs),
-        input_output_aliases={len(messages) + n: n for n in range(N_STATE)},
+        input_output_aliases={1 + n: n for n in range(N_STATE)},
         scratch_shapes=scratch,
-    )(*messages, *state)
+    )(message, *state)
 
 
 def shards(activator, inhibitor, feed_rate, kill_rate):
@@ -509,20 +453,16 @@
     )
     x_b = swap(x_send_b, "gx", 1)
     x_a = swap(x_send_a, "gx", 0)
-    rates, x_b, x_a = lax.optimization_barrier((pack_rates(feed, decay), x_b, x_a))
-    half_way = relay(rates, "gy")
-    send_b = pack_y(1, u0, v0, feed, decay, x_b, x_a, rates)
+    send_b = pack_y(1, u0, v0, feed, decay, x_b, x_a, feed)
     y_b = swap(send_b, "gy", 1)
     send_a = pack_y(0, u0, v0, feed, decay, x_b, x_a, send_b)
     y_a = swap(send_a, "gy", 0)
     x_b, _ = lax.optimization_barrier((x_b, send_a))
     made = early(u0, v0, feed, decay, x_b, x_a, su0, sv0, s_feed, s_decay)
     strips, (mu, mv), fields = made[:10], made[10:12], made[12:]
-    half_way, mu = lax.optimization_barrier((half_way, mu))
-    r_b = after_relay(half_way, "gy")
     rest = late(feed, decay, mu, mv, *fields[-2:])
-    state = border((y_a,), (u0, v0, feed, decay, *strips, *fields, *rest))
-    return border((y_b, r_b), state)[N_STATE:]
+    state = border(False, y_a, (u0, v0, feed, decay, *strips, *fields, *rest))
+    return border(True, y_b, state)[N_STATE:]
 
 
 def solution(mesh):

time: 49.8 us -> 49.3 us (0.990); the launches traced: 48.9 us -> 49 us
  waiting for transfers between devices: 3.54 us -> 9.63 us
  starting transfers between devices: 25.6 us -> 21.8 us
  Pallas kernels: 19 us -> 16.9 us
    ppermute x2 -> x0, starting transfers between devices: 12.5 us -> none  [the longest x1 10.6 us: relay(): lax.ppermute(block, axis, relay_pairs(count))]
    ppermute x4, starting transfers between devices: 13 us -> 21.8 us  [swap(): return lax.ppermute(block, axis, swap_pairs(lax.axis_size(axis), parity))]
    ppermute x4, waiting for transfers between devices: 3.54 us -> 9.63 us  [swap(): return lax.ppermute(block, axis, swap_pairs(lax.axis_size(axis), parity))]
    pallas_call x2, Pallas kernels: 6.83 us -> 5.49 us  [border(): pallas(functools.partial(border_kernel, is_last), 'border_odd' if is_last...]
  transfers between devices with their start and end apart: 6 -> 4, of which waited for: 2 -> 3; matrix products, arithmetic and copies ran while one was open for 0% -> 0% of each run, Pallas kernels for 22% -> 19%
where the time goes in v8:
time: 49.3 us; the launch traced here: 49 us
  starting transfers between devices  21.8 us (44%)
  Pallas kernels  16.9 us (34%)
  waiting for transfers between devices  9.63 us (20%)
  between operations  0.7 us (1%)
    ppermute x4, starting transfers between devices, swap(): return lax.ppermute(block, axis, swap_pairs(lax.axis_size(axis), parity))  21.8 us
    ppermute x4, waiting for transfers between devices, swap(): return lax.ppermute(block, axis, swap_pairs(lax.axis_size(axis), parity))  9.63 us
    pallas_call x2, Pallas kernels, border(): pallas(functools.partial(border_kernel, is_last), 'border_odd' if is_last...  5.49 us
    pallas_call x1, Pallas kernels, load(): pallas(load_kernel, 'load', 8, out_shape=(vmem(*FIELD),) * 4 + (vmem(*STR...  4.18 us
    pallas_call x1, Pallas kernels, early(): pallas(early_kernel, 'early', 4, 20000000000, out_shape=out, input_output...  4.04 us
    pallas_call x1, Pallas kernels, late(): pallas(late_kernel, 'late', 4, 20000000000, out_shape=out)  2.68 us
  transfers between devices with their start and end apart: 4, of which 3 were waited for; matrix products, arithmetic and copies ran while one was open for 0% of the time, Pallas kernels for 19%

profile of v8, /device:TPU:6, one launch (start us, length us, event | category | flops | bytes accessed | tf_op | source)
XLA Modules:
  0.0 49.0 jit_solution(11562321699242376243)
XLA Ops:
  0.6 4.2 %load.1 = (f32[56,48,128]{2,1,0:T(8,128)S(1)}, f32[56,48,128]{2,1,0:T(8,128)S(1)}, f32[56,48,128]{2,1,0:T(8,128)S(1)}, f32[56,48,128]{2,1,0:T(8,128)S(1)}, f32[1...) custom-call(f32[56,32,128]{2,1,0:T(8,128)} %u.1, ...), custom_call_target="tpu_custom_call" | custom-call | tf_op jit(solution)/shard_map/load/pallas_call | solution.py:126
  4.8 4.0 %collective-permute-start = (f32[4,7,8,128]{3,2,1,0:T(8,128)S(1)}, f32[4,7,8,128]{3,2,1,0:T(8,128)S(1)}, u32[]{:S(2)}, u32[]{:S(2)}) collective-permute-start(f32[4,7,8,128]{3,2,1,0:T(8,128)S(1)} %get-tuple-element.61), channel_id=1, source_target_pairs={{32,64},{64,32},{96,128},{128,96},{160,192},{192,160},{224,256},{2... | collective-permute-start | bytes 344072 | tf_op jit(solution)/shard_map/ppermute | solution.py:33
  8.8 2.3 %collective-permute-start.1 = (f32[4,7,8,128]{3,2,1,0:T(8,128)S(1)}, f32[4,7,8,128]{3,2,1,0:T(8,128)S(1)}, u32[]{:S(2)}, u32[]{:S(2)}) collective-permute-start(f32[4,7,8,128]{3,2,1,0:T(8,128)S(1)} %get-tuple-element.62), channel_id=1, source_target_pairs={{0,32},{32,0},{64,96},{96,64},{128,160},{160,128},{192,224},{224,1... | collective-permute-start | bytes 344072 | tf_op jit(solution)/shard_map/ppermute | solution.py:33
  11.1 1.6 %collective-permute-done.x_b = f32[4,7,8,128]{3,2,1,0:T(8,128)S(1)} collective-permute-done((f32[4,7,8,128]{3,2,1,0:T(8,128)S(1)}, f32[4,7,8,128]{3,2,1,0:T(8,128)S(1)}, u32[]{:S(2)}, u32[]{:S(2)}) %collective-permute-start) | collective-permute-done | bytes 114720 | tf_op jit(solution)/shard_map/ppermute | solution.py:33
  12.8 0.0 collective-permute-done.1.x_a
  12.8 0.3 pack_odd.1._
  13.0 13.5 %collective-permute-start.2 = (f32[848,128]{1,0:T(8,128)S(1)}, f32[848,128]{1,0:T(8,128)S(1)}, u32[]{:S(2)}, u32[]{:S(2)}) collective-permute-start(f32[848,128]{1,0:T(8,128)S(1)} %pack_odd.1._), channel_id=1, source_target_pairs={{1,2},{2,1},{3,4},{4,3},{5,6},{6,5},{7,8},{8,7},{9,10},{10,9},{11,... | collective-permute-start | bytes 1302536 | tf_op jit(solution)/shard_map/ppermute | solution.py:33
  26.6 0.3 pack_even.1
  26.9 1.9 %collective-permute-start.3 = (f32[848,128]{1,0:T(8,128)S(1)}, f32[848,128]{1,0:T(8,128)S(1)}, u32[]{:S(2)}, u32[]{:S(2)}) collective-permute-start(f32[848,128]{1,0:T(8,128)S(1)} %pack_even.1), channel_id=1, source_target_pairs={{0,1},{1,0},{2,3},{3,2},{4,5},{5,4},{6,7},{7,6},{8,9},{9,8},{10,11... | collective-permute-start | bytes 1302536 | tf_op jit(solution)/shard_map/ppermute | solution.py:33
  28.8 4.0 %early.1 = (f32[18,48,128]{2,1,0:T(8,128)S(1)}, f32[18,48,128]{2,1,0:T(8,128)S(1)}, f32[18,48,128]{2,1,0:T(8,128)S(1)}, f32[18,48,128]{2,1,0:T(8,128)S(1)}, f32[...) custom-call(f32[56,48,128]{2,1,0:T(8,128)S(1)} %get-tuple-element.57, ...), custom_call_target="tpu_custom_call", output_to_operand_aliasing={{0}: (6, {}), {1}: (7, {}), {2}: (8, {}), {3}: (9, {})} | custom-call | flops 20000000000 | bytes 5000000000 | tf_op jit(solution)/shard_map/early/pallas_call | solution.py:307
  32.8 2.7 %late.1 = (f32[56,48,128]{2,1,0:T(8,128)S(1)}, f32[56,48,128]{2,1,0:T(8,128)S(1)}, f32[56,32,128]{2,1,0:T(8,128)S(1)}, f32[56,32,128]{2,1,0:T(8,128)S(1)}) custom-call(f32[56,48,128]{2,1,0:T(8,128)S(1)} %get-tuple-element.59.feed._.refs_3_, f32[56,48,128]{2,1,0:T(8,128)S(1)} %get-tuple-element.60.decay.refs_4_, f32[7,48,128]{2,1,0:T(8,128)S(1)} %get-tuple-element.82.mu, ...), custom_call_target="tpu_custom_call" | custom-call | flops 20000000000 | bytes 5000000000 | tf_op jit(solution)/shard_map/late/pallas_call | solution.py:337
  35.5 4.6 %collective-permute-done.3.refs_0_ = f32[848,128]{1,0:T(8,128)S(1)} collective-permute-done((f32[848,128]{1,0:T(8,128)S(1)}, f32[848,128]{1,0:T(8,128)S(1)}, u32[]{:S(2)}, u32[]{:S(2)}) %collective-permute-start.3) | collective-permute-done | bytes 434208 | tf_op jit(solution)/shard_map/ppermute | solution.py:33
  40.1 2.2 %border_even.1 = (f32[56,48,128]{2,1,0:T(8,128)S(1)}, f32[56,48,128]{2,1,0:T(8,128)S(1)}, f32[56,48,128]{2,1,0:T(8,128)S(1)}, f32[56,48,128]{2,1,0:T(8,128)S(1)}...) custom-call(f32[848,128]{1,0:T(8,128)S(1)} %collective-permute-done., ...), custom_call_target="tpu_custom_call", output_to_operand_aliasing={{0}: (1, {}), {1}: (2, {}), {2}: (3, {}), {3}: (4, {}), {4}... | custom-call | flops 20000000000 | bytes 5000000000 | tf_op jit(solution)/shard_map/border_even/pallas_call | solution.py:438
  42.3 3.4 %collective-permute-done.2.refs_0_ = f32[848,128]{1,0:T(8,128)S(1)} collective-permute-done((f32[848,128]{1,0:T(8,128)S(1)}, f32[848,128]{1,0:T(8,128)S(1)}, u32[]{:S(2)}, u32[]{:S(2)}) %collective-permute-start.2) | collective-permute-done | bytes 434208 | tf_op jit(solution)/shard_map/ppermute | solution.py:33
  45.8 3.3 %border_odd.1 = (f32[56,48,128]{2,1,0:T(8,128)S(1)}, f32[56,48,128]{2,1,0:T(8,128)S(1)}, f32[56,48,128]{2,1,0:T(8,128)S(1)}, f32[56,48,128]{2,1,0:T(8,128)S(1)},...) custom-call(f32[848,128]{1,0:T(8,128)S(1)} %collective-permute-done., ...), custom_call_target="tpu_custom_call", output_to_operand_aliasing={{0}: (1, {}), {1}: (2, {}), {2}: (3, {}), {3}: (4, {}), {4}... | custom-call | flops 20000000000 | bytes 5000000000 | tf_op jit(solution)/shard_map/border_odd/pallas_call | solution.py:438
Async XLA Ops:
  4.8 7.9 %collective-permute-start = (f32[4,7,8,128]{3,2,1,0:T(8,128)S(1)}, f32[4,7,8,128]{3,2,1,0:T(8,128)S(1)}, u32[]{:S(2)}, u32[]{:S(2)}) collective-permute-start(f32[4,7,8,128]{3,2,1,0:T(8,128)S(1)} %get-tuple-element.61), channel_id=1, source_target_pairs={{32,64},{64,32},{96,128},{128,96},{160,192},{192,160},{224,256},{2... | collective-permute-start | bytes 344072 | tf_op jit(solution)/shard_map/ppermute | solution.py:33
  8.8 3.9 %collective-permute-start.1 = (f32[4,7,8,128]{3,2,1,0:T(8,128)S(1)}, f32[4,7,8,128]{3,2,1,0:T(8,128)S(1)}, u32[]{:S(2)}, u32[]{:S(2)}) collective-permute-start(f32[4,7,8,128]{3,2,1,0:T(8,128)S(1)} %get-tuple-element.62), channel_id=1, source_target_pairs={{0,32},{32,0},{64,96},{96,64},{128,160},{160,128},{192,224},{224,1... | collective-permute-start | bytes 344072 | tf_op jit(solution)/shard_map/ppermute | solution.py:33
  13.0 32.7 %collective-permute-start.2 = (f32[848,128]{1,0:T(8,128)S(1)}, f32[848,128]{1,0:T(8,128)S(1)}, u32[]{:S(2)}, u32[]{:S(2)}) collective-permute-start(f32[848,128]{1,0:T(8,128)S(1)} %pack_odd.1._), channel_id=1, source_target_pairs={{1,2},{2,1},{3,4},{4,3},{5,6},{6,5},{7,8},{8,7},{9,10},{10,9},{11,... | collective-permute-start | bytes 1302536 | tf_op jit(solution)/shard_map/ppermute | solution.py:33
  26.9 13.2 %collective-permute-start.3 = (f32[848,128]{1,0:T(8,128)S(1)}, f32[848,128]{1,0:T(8,128)S(1)}, u32[]{:S(2)}, u32[]{:S(2)}) collective-permute-start(f32[848,128]{1,0:T(8,128)S(1)} %pack_even.1), channel_id=1, source_target_pairs={{0,1},{1,0},{2,3},{3,2},{4,5},{5,4},{6,7},{7,6},{8,9},{9,8},{10,11... | collective-permute-start | bytes 1302536 | tf_op jit(solution)/shard_map/ppermute | solution.py:33

commit v9 on v8

--- a/solution.py
+++ b/solution.py
@@ -14,9 +14,9 @@
 OWN, LOW, HIGH = 8, 4, 40
 GROUPS, GZ = 8, NZ // 8
 FIELDS, RATES = 2 * W, 2 * (W - 1)
-CORNER = NZ * FIELDS
-TAIL = CORNER + 8 * GZ
-MESSAGE = (TAIL + NZ * RATES + 8, NX)
+TAIL = NZ * FIELDS
+CORNER = TAIL + NZ * RATES
+MESSAGE = (CORNER + 8 * GZ, NX)
 RIGHT, LEFT = 1, GZ + 3
 SPLANES = 2 * GZ + 4
 
@@ -91,27 +91,40 @@
     copies[1].wait()
     lax.fori_loop(0, NZ, rates, 0, unroll=14)
 
+    def strips_of(arrays, j):
+        made = []
+        for _, src, dst in arrays:
+            for t in range(4):
+                at = pl.ds(OWN + 8 * t, 8)
+                both = None
+                for g in range(GROUPS):
+                    value = turn(src[GZ * g + j, at, :], 16 * g + 8)
+                    both = value if g == 0 else jnp.where(group == g, value, both)
+                dst[j + RIGHT, at, :] = both
+                dst[j + LEFT, at, :] = both
+                made.append(both)
+        return tuple(made)
+
+    def edges_of(arrays, j, strips):
+        for a, (n, _, _) in enumerate(arrays):
+            left_edge = right_edge = None
+            for t in range(4):
+                both = strips[4 * a + t]
+                low, high = turn(both, 4 * t - 8), turn(both, 4 * t - 4)
+                here = (inner >= 4 * t) & (inner < 4 * t + 4)
+                left_edge = low if t == 0 else jnp.where(here, low, left_edge)
+                right_edge = high if t == 0 else jnp.where(here, high, right_edge)
+            out_b[n, j] = jnp.where(even, left_edge, right_edge)
+            out_a[n, j] = jnp.where(even, right_edge, left_edge)
+
     def pack(arrays):
-        def body(j, carry):
-            for n, src, dst in arrays:
-                left_edge = right_edge = None
-                for t in range(4):
-                    at = pl.ds(OWN + 8 * t, 8)
-                    both = None
-                    for g in range(GROUPS):
-                        value = turn(src[GZ * g + j, at, :], 16 * g + 8)
-                        both = value if g == 0 else jnp.where(group == g, value, both)
-                    dst[j + RIGHT, at, :] = both
-                    dst[j + LEFT, at, :] = both
-                    low, high = turn(both, 4 * t - 8), turn(both, 4 * t - 4)
-                    here = (inner >= 4 * t) & (inner < 4 * t + 4)
-                    left_edge = low if t == 0 else jnp.where(here, low, left_edge)
-                    right_edge = high if t == 0 else jnp.where(here, high, right_edge)
-                out_b[n, j] = jnp.where(even, left_edge, right_edge)
-                out_a[n, j] = jnp.where(even, right_edge, left_edge)
-            return carry
-
-        lax.fori_loop(0, GZ, body, 0, unroll=2)
+        def body(j, strips):
+            made = strips_of(arrays, j)
+            edges_of(arrays, j - 1, strips)
+            return made
+
+        last = lax.fori_loop(1, GZ, body, strips_of(arrays, 0), unroll=3)
+        edges_of(arrays, GZ - 1, last)
 
     pack(((2, feed, s_feed), (3, decay, s_decay)))
     copies[2].wait()
@@ -148,7 +161,6 @@
         return carry
 
     lax.fori_loop(0, NZ, rows, 0, unroll=8)
-    out[pl.ds(TAIL + RATES * NZ, 8), :] = jnp.zeros((8, NX), jnp.float32)
 
     def corner(j, carry):
         made = []

time: 49.3 us -> 48 us (0.974)
  Pallas kernels: 16.9 us -> 16 us
    pallas_call x1, Pallas kernels: 4.18 us -> 3.06 us  [load(): pallas(load_kernel, 'load', 8, out_shape=(vmem(*FIELD),) * 4 + (vmem(*STR...]
  transfers between devices with their start and end apart: 4 -> 4, of which waited for: 3 -> 3; matrix products, arithmetic and copies ran while one was open for 0% -> 0% of each run, Pallas kernels for 19% -> 20%
where the time goes in v9:
time: 48 us; the launch traced here: 47.8 us
  starting transfers between devices  21.8 us (45%)
  Pallas kernels  16 us (33%)
  waiting for transfers between devices  9.31 us (19%)
  between operations  0.7 us (1%)
    ppermute x4, starting transfers between devices, swap(): return lax.ppermute(block, axis, swap_pairs(lax.axis_size(axis), parity))  21.8 us
    ppermute x4, waiting for transfers between devices, swap(): return lax.ppermute(block, axis, swap_pairs(lax.axis_size(axis), parity))  9.31 us
    pallas_call x2, Pallas kernels, border(): pallas(functools.partial(border_kernel, is_last), 'border_odd' if is_last...  5.5 us
    pallas_call x1, Pallas kernels, early(): pallas(early_kernel, 'early', 4, 20000000000, out_shape=out, input_output...  4.18 us
    pallas_call x1, Pallas kernels, load(): pallas(load_kernel, 'load', 8, out_shape=(vmem(*FIELD),) * 4 + (vmem(*STR...  3.06 us
    pallas_call x1, Pallas kernels, late(): pallas(late_kernel, 'late', 4, 20000000000, out_shape=out)  2.68 us
  transfers between devices with their start and end apart: 4, of which 3 were waited for; matrix products, arithmetic and copies ran while one was open for 0% of the time, Pallas kernels for 20%

profile of v9, /device:TPU:6, one launch (start us, length us, event | category | flops | bytes accessed | tf_op | source)
XLA Modules:
  0.0 47.8 jit_solution(3037018577151228163)
XLA Ops:
  0.6 3.1 %load.1 = (f32[56,48,128]{2,1,0:T(8,128)S(1)}, f32[56,48,128]{2,1,0:T(8,128)S(1)}, f32[56,48,128]{2,1,0:T(8,128)S(1)}, f32[56,48,128]{2,1,0:T(8,128)S(1)}, f32[1...) custom-call(f32[56,32,128]{2,1,0:T(8,128)} %u.1, ...), custom_call_target="tpu_custom_call" | custom-call | tf_op jit(solution)/shard_map/load/pallas_call | solution.py:139
  3.7 4.0 %collective-permute-start = (f32[4,7,8,128]{3,2,1,0:T(8,128)S(1)}, f32[4,7,8,128]{3,2,1,0:T(8,128)S(1)}, u32[]{:S(2)}, u32[]{:S(2)}) collective-permute-start(f32[4,7,8,128]{3,2,1,0:T(8,128)S(1)} %get-tuple-element.61), channel_id=1, source_target_pairs={{32,64},{64,32},{96,128},{128,96},{160,192},{192,160},{224,256},{2... | collective-permute-start | bytes 344072 | tf_op jit(solution)/shard_map/ppermute | solution.py:33
  7.7 2.3 %collective-permute-start.1 = (f32[4,7,8,128]{3,2,1,0:T(8,128)S(1)}, f32[4,7,8,128]{3,2,1,0:T(8,128)S(1)}, u32[]{:S(2)}, u32[]{:S(2)}) collective-permute-start(f32[4,7,8,128]{3,2,1,0:T(8,128)S(1)} %get-tuple-element.62), channel_id=1, source_target_pairs={{0,32},{32,0},{64,96},{96,64},{128,160},{160,128},{192,224},{224,1... | collective-permute-start | bytes 344072 | tf_op jit(solution)/shard_map/ppermute | solution.py:33
  10.0 1.6 %collective-permute-done.x_b = f32[4,7,8,128]{3,2,1,0:T(8,128)S(1)} collective-permute-done((f32[4,7,8,128]{3,2,1,0:T(8,128)S(1)}, f32[4,7,8,128]{3,2,1,0:T(8,128)S(1)}, u32[]{:S(2)}, u32[]{:S(2)}) %collective-permute-start) | collective-permute-done | bytes 114720 | tf_op jit(solution)/shard_map/ppermute | solution.py:33
  11.6 0.0 collective-permute-done.1.x_a
  11.6 0.3 pack_odd.1._
  11.9 13.5 %collective-permute-start.2 = (f32[840,128]{1,0:T(8,128)S(1)}, f32[840,128]{1,0:T(8,128)S(1)}, u32[]{:S(2)}, u32[]{:S(2)}) collective-permute-start(f32[840,128]{1,0:T(8,128)S(1)} %pack_odd.1._), channel_id=1, source_target_pairs={{1,2},{2,1},{3,4},{4,3},{5,6},{6,5},{7,8},{8,7},{9,10},{10,9},{11,... | collective-permute-start | bytes 1290248 | tf_op jit(solution)/shard_map/ppermute | solution.py:33
  25.5 0.3 pack_even.1
  25.8 1.9 %collective-permute-start.3 = (f32[840,128]{1,0:T(8,128)S(1)}, f32[840,128]{1,0:T(8,128)S(1)}, u32[]{:S(2)}, u32[]{:S(2)}) collective-permute-start(f32[840,128]{1,0:T(8,128)S(1)} %pack_even.1), channel_id=1, source_target_pairs={{0,1},{1,0},{2,3},{3,2},{4,5},{5,4},{6,7},{7,6},{8,9},{9,8},{10,11... | collective-permute-start | bytes 1290248 | tf_op jit(solution)/shard_map/ppermute | solution.py:33
  27.7 4.2 %early.1 = (f32[18,48,128]{2,1,0:T(8,128)S(1)}, f32[18,48,128]{2,1,0:T(8,128)S(1)}, f32[18,48,128]{2,1,0:T(8,128)S(1)}, f32[18,48,128]{2,1,0:T(8,128)S(1)}, f32[...) custom-call(f32[56,48,128]{2,1,0:T(8,128)S(1)} %get-tuple-element.57, ...), custom_call_target="tpu_custom_call", output_to_operand_aliasing={{0}: (6, {}), {1}: (7, {}), {2}: (8, {}), {3}: (9, {})} | custom-call | flops 20000000000 | bytes 5000000000 | tf_op jit(solution)/shard_map/early/pallas_call | solution.py:319
  31.9 2.7 %late.1 = (f32[56,48,128]{2,1,0:T(8,128)S(1)}, f32[56,48,128]{2,1,0:T(8,128)S(1)}, f32[56,32,128]{2,1,0:T(8,128)S(1)}, f32[56,32,128]{2,1,0:T(8,128)S(1)}) custom-call(f32[56,48,128]{2,1,0:T(8,128)S(1)} %get-tuple-element.59.feed._.refs_3_, f32[56,48,128]{2,1,0:T(8,128)S(1)} %get-tuple-element.60.decay.refs_4_, f32[7,48,128]{2,1,0:T(8,128)S(1)} %get-tuple-element.82.mu, ...), custom_call_target="tpu_custom_call" | custom-call | flops 20000000000 | bytes 5000000000 | tf_op jit(solution)/shard_map/late/pallas_call | solution.py:349
  34.6 4.4 %collective-permute-done.3.refs_0_ = f32[840,128]{1,0:T(8,128)S(1)} collective-permute-done((f32[840,128]{1,0:T(8,128)S(1)}, f32[840,128]{1,0:T(8,128)S(1)}, u32[]{:S(2)}, u32[]{:S(2)}) %collective-permute-start.3) | collective-permute-done | bytes 430112 | tf_op jit(solution)/shard_map/ppermute | solution.py:33
  38.9 2.2 %border_even.1 = (f32[56,48,128]{2,1,0:T(8,128)S(1)}, f32[56,48,128]{2,1,0:T(8,128)S(1)}, f32[56,48,128]{2,1,0:T(8,128)S(1)}, f32[56,48,128]{2,1,0:T(8,128)S(1)}...) custom-call(f32[840,128]{1,0:T(8,128)S(1)} %collective-permute-done., ...), custom_call_target="tpu_custom_call", output_to_operand_aliasing={{0}: (1, {}), {1}: (2, {}), {2}: (3, {}), {3}: (4, {}), {4}... | custom-call | flops 20000000000 | bytes 5000000000 | tf_op jit(solution)/shard_map/border_even/pallas_call | solution.py:450
  41.1 3.3 %collective-permute-done.2.refs_0_ = f32[840,128]{1,0:T(8,128)S(1)} collective-permute-done((f32[840,128]{1,0:T(8,128)S(1)}, f32[840,128]{1,0:T(8,128)S(1)}, u32[]{:S(2)}, u32[]{:S(2)}) %collective-permute-start.2) | collective-permute-done | bytes 430112 | tf_op jit(solution)/shard_map/ppermute | solution.py:33
  44.5 3.3 %border_odd.1 = (f32[56,48,128]{2,1,0:T(8,128)S(1)}, f32[56,48,128]{2,1,0:T(8,128)S(1)}, f32[56,48,128]{2,1,0:T(8,128)S(1)}, f32[56,48,128]{2,1,0:T(8,128)S(1)},...) custom-call(f32[840,128]{1,0:T(8,128)S(1)} %collective-permute-done., ...), custom_call_target="tpu_custom_call", output_to_operand_aliasing={{0}: (1, {}), {1}: (2, {}), {2}: (3, {}), {3}: (4, {}), {4}... | custom-call | flops 20000000000 | bytes 5000000000 | tf_op jit(solution)/shard_map/border_odd/pallas_call | solution.py:450
Async XLA Ops:
  3.7 7.9 %collective-permute-start = (f32[4,7,8,128]{3,2,1,0:T(8,128)S(1)}, f32[4,7,8,128]{3,2,1,0:T(8,128)S(1)}, u32[]{:S(2)}, u32[]{:S(2)}) collective-permute-start(f32[4,7,8,128]{3,2,1,0:T(8,128)S(1)} %get-tuple-element.61), channel_id=1, source_target_pairs={{32,64},{64,32},{96,128},{128,96},{160,192},{192,160},{224,256},{2... | collective-permute-start | bytes 344072 | tf_op jit(solution)/shard_map/ppermute | solution.py:33
  7.7 3.9 %collective-permute-start.1 = (f32[4,7,8,128]{3,2,1,0:T(8,128)S(1)}, f32[4,7,8,128]{3,2,1,0:T(8,128)S(1)}, u32[]{:S(2)}, u32[]{:S(2)}) collective-permute-start(f32[4,7,8,128]{3,2,1,0:T(8,128)S(1)} %get-tuple-element.62), channel_id=1, source_target_pairs={{0,32},{32,0},{64,96},{96,64},{128,160},{160,128},{192,224},{224,1... | collective-permute-start | bytes 344072 | tf_op jit(solution)/shard_map/ppermute | solution.py:33
  11.9 32.6 %collective-permute-start.2 = (f32[840,128]{1,0:T(8,128)S(1)}, f32[840,128]{1,0:T(8,128)S(1)}, u32[]{:S(2)}, u32[]{:S(2)}) collective-permute-start(f32[840,128]{1,0:T(8,128)S(1)} %pack_odd.1._), channel_id=1, source_target_pairs={{1,2},{2,1},{3,4},{4,3},{5,6},{6,5},{7,8},{8,7},{9,10},{10,9},{11,... | collective-permute-start | bytes 1290248 | tf_op jit(solution)/shard_map/ppermute | solution.py:33
  25.8 13.2 %collective-permute-start.3 = (f32[840,128]{1,0:T(8,128)S(1)}, f32[840,128]{1,0:T(8,128)S(1)}, u32[]{:S(2)}, u32[]{:S(2)}) collective-permute-start(f32[840,128]{1,0:T(8,128)S(1)} %pack_even.1), channel_id=1, source_target_pairs={{0,1},{1,0},{2,3},{3,2},{4,5},{5,4},{6,7},{7,6},{8,9},{9,8},{10,11... | collective-permute-start | bytes 1290248 | tf_op jit(solution)/shard_map/ppermute | solution.py:33
